TPU v7x, 128 devices: a whole 4x4x4 slice. The times are simulated.
128 devices in a mesh: dp: 2 (over core), expert: 16 (over z, x), tensor: 4 (over y).
Axes of the slice: x: 4, y: 4, z: 4, core: 2. Of those that a mesh axis runs over, the one named last changes fastest.
Arguments:
- expert_out: bfloat16 [512, 16, 20, 7168], P(('dp', 'expert'), None, None, 'tensor'), parts along dimension 0, may hold values from -6 to 6
- expert_ids: int32 [16384, 8], P(('dp', 'expert')), parts along dimension 0, may hold values from 0 to 255, all different within a row; in each aligned block of 512 rows (0 to 511, 512 to 1023, ...) at most 20 rows name the same one
- gate_levels: int32 [16384, 8], P(('dp', 'expert')), parts along dimension 0, may hold values from 1 to 255
- residual: bfloat16 [16384, 7168], P(('dp', 'expert'), 'tensor'), parts along dimension 0, may hold values from -24 to 24
- attn_gain: float32 [7168], P('tensor'), may hold values from 0.1 to 1.9
- wq_a: bfloat16 [7168, 1536], P('tensor', 'expert'), may hold values from -0.0625 to 0.0625
- latent_gain: float32 [1536], replicated, may hold values from 0.1 to 1.9
- wq_b: bfloat16 [1536, 12288], P('expert', 'tensor'), may hold values from -0.15625 to 0.15625
Outputs:
- stream: bfloat16 [16384, 7168], P(('dp', 'expert'), 'tensor'), parts along dimension 0
- normed: bfloat16 [16384, 7168], P(('dp', 'expert'), 'tensor'), parts along dimension 0
- queries: bfloat16 [16384, 12288], P(('dp', 'expert'), 'tensor'), parts along dimension 0
There are 2 independent parts, one for each index of `dp`. A program takes and returns all parts, laid end to end along the dimension named above; an argument that names none is the same for every part. Nothing has to cross between parts.
Inputs may be any that keep to these rules, and one draw needn't show every extreme that they name: `expert_ids`: each row names 8 different experts. Among the 512 rows of one owner (aligned blocks of rows) no expert is named more than 20 times, a bound that some block reaches.
All inputs are finite; a program needn't handle non-finite values.
Results may differ from a plain program's by a relative error of at most 0.024.
Values may be sent and summed in bfloat16 or wider, within the bound.
No kernel may reach another device: no remote copies, remote signals or barrier semaphores. Data moves between devices by JAX's collectives and lax.ppermute only.
A program may use at most 192 MiB of HBM per device.

v0:
```python
import jax
import jax.numpy as jnp
from jax import lax
from jax.sharding import PartitionSpec as P

D = 7168
QL = 1536


route_scale = 2.5
epsilon = 1e-06


def block_ranks(owner_ids, expert_total):
    length = owner_ids.shape[0]
    one_hot = jnp.sum(
        (owner_ids[:, :, None] == jnp.arange(expert_total, dtype=jnp.int32)[None, None, :]).astype(
            jnp.float32
        ),
        axis=1,
    )
    position = jnp.arange(length, dtype=jnp.int32)
    earlier = (position[:, None] > position[None, :]).astype(jnp.float32)
    before = jnp.dot(
        earlier, one_hot, precision=lax.Precision.HIGHEST, preferred_element_type=jnp.float32
    )
    return jnp.take_along_axis(before, owner_ids, axis=1).astype(jnp.int32)


def gate_weights(levels):
    wide = levels.astype(jnp.float32)
    return route_scale * wide / jnp.sum(wide, axis=1, keepdims=True)


def latent_norm(latent, latent_gain):
    latent_scale = lax.rsqrt(jnp.sum(latent * latent, axis=1) / QL + epsilon)
    return (latent * latent_scale[:, None] * latent_gain).astype(jnp.bfloat16)


def weighted_slots(slot_local, weight, slot_total, slot_rows):
    slot_range = jnp.arange(slot_total, dtype=jnp.int32)
    matrix = jnp.sum(
        jnp.where(slot_local[:, :, None] == slot_range[None, None, :], weight[:, :, None], 0.0),
        axis=1,
    )
    part_sum = jnp.dot(
        matrix,
        slot_rows.astype(jnp.float32),
        precision=lax.Precision.HIGHEST,
        preferred_element_type=jnp.float32,
    )
    return lax.optimization_barrier(part_sum.astype(jnp.bfloat16)).astype(jnp.float32)


def shards(expert_out, expert_ids, gate_levels, residual, attn_gain, wq_a, latent_gain, wq_b):
    owner_count = lax.axis_size("expert")
    my_index = lax.axis_index("expert")
    tok_rows = expert_ids.shape[0]
    top_count = expert_ids.shape[1]
    local_count = expert_out.shape[0]
    capacity = expert_out.shape[2]
    columns = expert_out.shape[3]
    experts = local_count * owner_count
    slot_total = local_count * capacity
    all_ids, all_levels = (
        lax.all_gather(expert_ids, "expert", axis=0, tiled=True),
        lax.all_gather(gate_levels, "expert", axis=0, tiled=True),
    )
    slot_rank = lax.map(
        lambda block: block_ranks(block, experts), all_ids.reshape(owner_count, tok_rows, top_count)
    ).reshape(owner_count * tok_rows, top_count)
    local_ids = all_ids - my_index * local_count
    is_local = (local_ids >= 0) & (local_ids < local_count)
    slot_local_all = jnp.where(
        is_local, jnp.clip(local_ids, 0, local_count - 1) * capacity + slot_rank, -1
    )
    weight_all = gate_weights(all_levels)

    def one_owner(offset):
        row_start = offset * tok_rows
        slot_local = lax.dynamic_slice_in_dim(slot_local_all, row_start, tok_rows, 0)
        row_weight = lax.dynamic_slice_in_dim(weight_all, row_start, tok_rows, 0)
        slot_rows = lax.dynamic_index_in_dim(expert_out, offset, 1, keepdims=False).reshape(
            slot_total, columns
        )
        return weighted_slots(slot_local, row_weight, slot_total, slot_rows)

    blocks = lax.map(
        one_owner, jnp.arange(lax.axis_size("expert") * tok_rows // tok_rows, dtype=jnp.int32)
    )
    combined = lax.psum_scatter(
        blocks.reshape(lax.axis_size("expert") * tok_rows, columns).astype(jnp.bfloat16),
        "expert",
        scatter_dimension=0,
        tiled=True,
    ).astype(jnp.float32)
    stream = (residual.astype(jnp.float32) + combined).astype(jnp.bfloat16)
    stream_wide = stream.astype(jnp.float32)
    total_squares = lax.psum(jnp.sum(stream_wide * stream_wide, axis=1), "tensor")
    inv_scale = lax.rsqrt(total_squares / D + epsilon)
    normed = (stream_wide * inv_scale[:, None] * attn_gain).astype(jnp.bfloat16)
    partial_value = jnp.dot(
        normed,
        lax.all_gather(wq_a, "expert", axis=1, tiled=True),
        preferred_element_type=jnp.float32,
    )
    latent = lax.psum(partial_value.astype(jnp.bfloat16), "tensor").astype(jnp.float32)
    compressed = latent_norm(latent, latent_gain)
    queries = jnp.dot(
        compressed,
        lax.all_gather(wq_b, "expert", axis=0, tiled=True),
        preferred_element_type=jnp.float32,
    )
    return (stream, normed, queries.astype(jnp.bfloat16))


def solution(mesh):
    return jax.shard_map(
        shards,
        mesh=mesh,
        in_specs=(
            P(("dp", "expert"), None, None, "tensor"),
            P(("dp", "expert"), None),
            P(("dp", "expert"), None),
            P(("dp", "expert"), "tensor"),
            P("tensor"),
            P("tensor", "expert"),
            P(),
            P("expert", "tensor"),
        ),
        out_specs=(
            P(("dp", "expert"), "tensor"),
            P(("dp", "expert"), "tensor"),
            P(("dp", "expert"), "tensor"),
        ),
        check_vma=False,
    )
```

profile of v0, /device:TPU:1, one launch (start us, length us, event | category | flops | bytes accessed | tf_op | source)
XLA Modules:
  0.0 1256.0 jit_solution(1408675557640040325)
XLA Ops:
  7.2 20.7 %all_gather.12 = s32[8192,8]{0,1:T(8,128)S(1)} all-gather(s32[512,8]{0,1:T(8,128)} %param.13), channel_id=1, replica_groups=mesh['dp'=2,'expert'=16,'tensor'=4] {'expert'}, dimensions={0}, use_global_device_ids=true | all-gather | bytes 278528 | tf_op jit(solution)/shard_map/all_gather | solution.py:66
  27.9 633.8 %while.20 = (s32[]{:T(128)}, s32[16,512,8]{1,2,0:T(8,128)S(1)}, s32[16,512,8]{1,2,0:T(8,128)S(1)}, s32[]{:T(128)}) while((s32[]{:T(128)}, s32[16,512,8]{1,2,0:T(8,128)S(1)}, s32[16,512,8]{1,2,0:T(8,128)S(1)}, s32[]{:T(128)}) %tuple.53), condition=%wide.region_2.0_spmd, body=%wide.region_0.2_spmd.sunk | while | flops 808648704 | bytes 1933377 | solution.py:69
  34.5 32.8 %gather_fusion = f32[4096]{0:T(1024)S(1)} fusion(f32[512,256]{1,0:T(8,128)S(1)} %fusion.25, s32[4096]{0:T(1024)S(1)} %reshape.84), kind=kCustom, calls=%fused_computation.clone.1 | custom fusion | bytes 65536 | tf_op jit(solution)/shard_map/while/body/eval_jaxpr/jit(take_along_axis)/gather | solution.py:27
  74.1 32.8 %gather_fusion = f32[4096]{0:T(1024)S(1)} fusion(f32[512,256]{1,0:T(8,128)S(1)} %fusion.25, s32[4096]{0:T(1024)S(1)} %reshape.84), kind=kCustom, calls=%fused_computation.clone.1 | custom fusion | bytes 65536 | tf_op jit(solution)/shard_map/while/body/eval_jaxpr/jit(take_along_axis)/gather | solution.py:27
  113.7 32.8 %gather_fusion = f32[4096]{0:T(1024)S(1)} fusion(f32[512,256]{1,0:T(8,128)S(1)} %fusion.25, s32[4096]{0:T(1024)S(1)} %reshape.84), kind=kCustom, calls=%fused_computation.clone.1 | custom fusion | bytes 65536 | tf_op jit(solution)/shard_map/while/body/eval_jaxpr/jit(take_along_axis)/gather | solution.py:27
  153.3 32.8 %gather_fusion = f32[4096]{0:T(1024)S(1)} fusion(f32[512,256]{1,0:T(8,128)S(1)} %fusion.25, s32[4096]{0:T(1024)S(1)} %reshape.84), kind=kCustom, calls=%fused_computation.clone.1 | custom fusion | bytes 65536 | tf_op jit(solution)/shard_map/while/body/eval_jaxpr/jit(take_along_axis)/gather | solution.py:27
  193.0 32.8 %gather_fusion = f32[4096]{0:T(1024)S(1)} fusion(f32[512,256]{1,0:T(8,128)S(1)} %fusion.25, s32[4096]{0:T(1024)S(1)} %reshape.84), kind=kCustom, calls=%fused_computation.clone.1 | custom fusion | bytes 65536 | tf_op jit(solution)/shard_map/while/body/eval_jaxpr/jit(take_along_axis)/gather | solution.py:27
  232.6 32.8 %gather_fusion = f32[4096]{0:T(1024)S(1)} fusion(f32[512,256]{1,0:T(8,128)S(1)} %fusion.25, s32[4096]{0:T(1024)S(1)} %reshape.84), kind=kCustom, calls=%fused_computation.clone.1 | custom fusion | bytes 65536 | tf_op jit(solution)/shard_map/while/body/eval_jaxpr/jit(take_along_axis)/gather | solution.py:27
  272.2 32.8 %gather_fusion = f32[4096]{0:T(1024)S(1)} fusion(f32[512,256]{1,0:T(8,128)S(1)} %fusion.25, s32[4096]{0:T(1024)S(1)} %reshape.84), kind=kCustom, calls=%fused_computation.clone.1 | custom fusion | bytes 65536 | tf_op jit(solution)/shard_map/while/body/eval_jaxpr/jit(take_along_axis)/gather | solution.py:27
  311.8 32.8 %gather_fusion = f32[4096]{0:T(1024)S(1)} fusion(f32[512,256]{1,0:T(8,128)S(1)} %fusion.25, s32[4096]{0:T(1024)S(1)} %reshape.84), kind=kCustom, calls=%fused_computation.clone.1 | custom fusion | bytes 65536 | tf_op jit(solution)/shard_map/while/body/eval_jaxpr/jit(take_along_axis)/gather | solution.py:27
  351.4 32.8 %gather_fusion = f32[4096]{0:T(1024)S(1)} fusion(f32[512,256]{1,0:T(8,128)S(1)} %fusion.25, s32[4096]{0:T(1024)S(1)} %reshape.84), kind=kCustom, calls=%fused_computation.clone.1 | custom fusion | bytes 65536 | tf_op jit(solution)/shard_map/while/body/eval_jaxpr/jit(take_along_axis)/gather | solution.py:27
  391.0 32.8 %gather_fusion = f32[4096]{0:T(1024)S(1)} fusion(f32[512,256]{1,0:T(8,128)S(1)} %fusion.25, s32[4096]{0:T(1024)S(1)} %reshape.84), kind=kCustom, calls=%fused_computation.clone.1 | custom fusion | bytes 65536 | tf_op jit(solution)/shard_map/while/body/eval_jaxpr/jit(take_along_axis)/gather | solution.py:27
  430.6 32.8 %gather_fusion = f32[4096]{0:T(1024)S(1)} fusion(f32[512,256]{1,0:T(8,128)S(1)} %fusion.25, s32[4096]{0:T(1024)S(1)} %reshape.84), kind=kCustom, calls=%fused_computation.clone.1 | custom fusion | bytes 65536 | tf_op jit(solution)/shard_map/while/body/eval_jaxpr/jit(take_along_axis)/gather | solution.py:27
  470.2 32.8 %gather_fusion = f32[4096]{0:T(1024)S(1)} fusion(f32[512,256]{1,0:T(8,128)S(1)} %fusion.25, s32[4096]{0:T(1024)S(1)} %reshape.84), kind=kCustom, calls=%fused_computation.clone.1 | custom fusion | bytes 65536 | tf_op jit(solution)/shard_map/while/body/eval_jaxpr/jit(take_along_axis)/gather | solution.py:27
  509.9 32.8 %gather_fusion = f32[4096]{0:T(1024)S(1)} fusion(f32[512,256]{1,0:T(8,128)S(1)} %fusion.25, s32[4096]{0:T(1024)S(1)} %reshape.84), kind=kCustom, calls=%fused_computation.clone.1 | custom fusion | bytes 65536 | tf_op jit(solution)/shard_map/while/body/eval_jaxpr/jit(take_along_axis)/gather | solution.py:27
  549.5 32.8 %gather_fusion = f32[4096]{0:T(1024)S(1)} fusion(f32[512,256]{1,0:T(8,128)S(1)} %fusion.25, s32[4096]{0:T(1024)S(1)} %reshape.84), kind=kCustom, calls=%fused_computation.clone.1 | custom fusion | bytes 65536 | tf_op jit(solution)/shard_map/while/body/eval_jaxpr/jit(take_along_axis)/gather | solution.py:27
  589.1 32.8 %gather_fusion = f32[4096]{0:T(1024)S(1)} fusion(f32[512,256]{1,0:T(8,128)S(1)} %fusion.25, s32[4096]{0:T(1024)S(1)} %reshape.84), kind=kCustom, calls=%fused_computation.clone.1 | custom fusion | bytes 65536 | tf_op jit(solution)/shard_map/while/body/eval_jaxpr/jit(take_along_axis)/gather | solution.py:27
  628.7 32.8 %gather_fusion = f32[4096]{0:T(1024)S(1)} fusion(f32[512,256]{1,0:T(8,128)S(1)} %fusion.25, s32[4096]{0:T(1024)S(1)} %reshape.84), kind=kCustom, calls=%fused_computation.clone.1 | custom fusion | bytes 65536 | tf_op jit(solution)/shard_map/while/body/eval_jaxpr/jit(take_along_axis)/gather | solution.py:27
  679.2 19.3 %copy.27 = bf16[16,16,20,1792]{3,2,0,1:T(8,128)(2,1)} copy(bf16[16,16,20,1792]{3,1,2,0:T(8,128)(2,1)} %param.12) | data formatting | bytes 36700160 | tf_op jit(solution)/shard_map/while | solution.py:88
  698.7 161.8 %while.21 = (s32[]{:T(128)}, bf16[16,512,1792]{2,1,0:T(8,128)(2,1)}, s32[16]{0:T(128)S(1)}, s32[8192,8]{0,1:T(8,128)S(1)}, f32[8192,8]{0,1:T(8,128)S(1)}, /*inde...) while((s32[]{:T(128)}, ...), condition=%wide.region_6.7_spmd, body=%wide.region_4.6_spmd.sunk | while | flops 3528818688 | bytes 16581389 | solution.py:88
  861.4 183.8 %reduce-scatter.2.cloned.1.call-done = bf16[512,1792]{1,0:T(8,128)(2,1)} async-done(((bf16[8192,1792]{1,0:T(8,128)(2,1)}), bf16[512,1792]{1,0:T(8,128)(2,1)}) %reduce-scatter.2.cloned.1.call-update) | async-done | bytes 1835024 | tf_op jit(solution)/shard_map/reduce_scatter | solution.py:91
  1058.3 46.5 %all-gather.3.cloned.1.call-done = bf16[1792,1536]{0,1:T(8,128)(2,1)} async-done(((bf16[1792,96]{0,1:T(8,128)(2,1)}), bf16[1792,1536]{0,1:T(8,128)(2,1)}) %all-gather.3.cloned.1.call-update) | async-done | bytes 5505040 | tf_op jit(solution)/shard_map/all_gather | solution.py:104
  1112.7 49.5 %all-reduce.2.cloned.1.call-done = bf16[512,1536]{1,0:T(8,128)(2,1)} async-done(((bf16[512,1536]{1,0:T(8,128)(2,1)}), bf16[512,1536]{1,0:T(8,128)(2,1)}) %all-reduce.2.cloned.1.call-update) | async-done | bytes 1572880 | tf_op jit(solution)/shard_map/psum | solution.py:107
  1164.0 76.3 %all-gather.5.cloned.1.call-done = bf16[1536,3072]{1,0:T(8,128)(2,1)} async-done(((bf16[96,3072]{1,0:T(8,128)(2,1)}), bf16[1536,3072]{1,0:T(8,128)(2,1)}) %all-gather.5.cloned.1.call-update) | async-done | bytes 9437200 | tf_op jit(solution)/shard_map/all_gather | solution.py:111
  (383 shorter events, 278.0 us)
Async XLA Ops:
  7.2 1038.0 %reduce-scatter.2.cloned.1.call-start = ((), (), s32[]{:S(2)}) async-start(), calls=%async_computation.1 | async-start | bytes 31195136 | tf_op jit(solution)/shard_map/reduce_scatter | solution.py:91
  27.9 633.8 %copy-start.3 = (s32[512,8]{0,1:T(8,128)S(1)}, s32[512,8]{0,1:T(8,128)}, u32[]{:S(2)}) copy-start(s32[512,8]{0,1:T(8,128)} %param.14) | copy-start | bytes 49156
  707.4 1.4 copy-start.2
  717.5 1.4 copy-start.2
  727.6 1.4 copy-start.2
  737.7 1.4 copy-start.2
  747.8 1.5 copy-start.2
  758.0 1.4 copy-start.2
  768.1 1.4 copy-start.2
  778.2 1.4 copy-start.2
  788.3 1.4 copy-start.2
  798.4 1.4 copy-start.2
  808.5 1.4 copy-start.2
  818.6 1.4 copy-start.2
  828.7 1.4 copy-start.2
  838.9 1.5 copy-start.2
  849.0 1.4 copy-start.2
  859.2 1.4 copy-start.2
  860.5 196.0 %copy-start.4 = (f32[1792]{0:T(1024)S(1)}, f32[1792]{0:T(1024)}, u32[]{:S(2)}) copy-start(f32[1792]{0:T(1024)} %param.16) | copy-start | bytes 21508
  860.6 244.2 %all-gather.3.cloned.1.call-start = ((), (), s32[]{:S(2)}) async-start(), calls=%async_computation.2 | async-start | bytes 5849088 | tf_op jit(solution)/shard_map/all_gather | solution.py:104
  861.3 300.8 %all-reduce.2.cloned.1.call-start = ((), (), s32[]{:S(2)}) async-start(), calls=%async_computation.3 | async-start | bytes 3145728 | tf_op jit(solution)/shard_map/psum | solution.py:107
  1047.9 64.1 %copy-start = (bf16[512,1792]{1,0:T(8,128)(2,1)}, bf16[512,1792]{1,0:T(8,128)(2,1)S(1)}, u32[]{:S(2)}) copy-start(bf16[512,1792]{1,0:T(8,128)(2,1)S(1)} %get-tuple-element.91) | copy-start | bytes 5505028
  1112.1 128.2 %copy-start.5 = (f32[1536]{0:T(1024)S(1)}, f32[1536]{0:T(1024)}, u32[]{:S(2)}) copy-start(f32[1536]{0:T(1024)} %param.18) | copy-start | bytes 18436
  1112.1 128.1 %all-gather.5.cloned.1.call-start = ((), (), s32[]{:S(2)}) async-start(), calls=%async_computation.4 | async-start | bytes 10027008 | tf_op jit(solution)/shard_map/all_gather | solution.py:111
  (16 other events, 20.4 us)
Sparse Core Ops, SparseCore 0:
  860.7 184.4 reduce-scatter.1
  1047.3 57.4 all-gather.2
  1112.2 49.8 all-reduce.1
  1164.1 76.0 all-gather.4
where the time goes:
time: 1260 us
  local copies, waits for them, and re-layouts  591 us (47%)
  waiting for transfers between devices  357 us (28%)
  other arithmetic  127 us (10%)
  matrix products  76.1 us (6%)
  blocking collectives  46.6 us (4%)
  loops' own time  43.8 us (3%)
  between operations  13.8 us (1%)
    gather x80, local copies, waits for them, and re-layouts, block_ranks(): return jnp.take_along_axis(before, owner_ids, axis=1).astype(jnp.int32)  533 us
    reduce_scatter x1, waiting for transfers between devices, shards(): lax.psum_scatter(blocks.reshape(lax.axis_size('expert') * tok_rows, colum...  184 us
    reduce_sum x16, other arithmetic, block_ranks(): jnp.sum((owner_ids[:, :, None] == jnp.arange(expert_total, dtype=jnp.int3...  86.9 us
    all_gather x1, waiting for transfers between devices, shards(): lax.all_gather(wq_b, 'expert', axis=0, tiled=True)  76.3 us
    psum x1, waiting for transfers between devices, shards(): lax.psum(partial_value.astype(jnp.bfloat16), 'tensor').astype(jnp.float32)  49.5 us
    dot_general x16, matrix products, weighted_slots(): jnp.dot(matrix, slot_rows.astype(jnp.float32), precision=lax.Precision.HI...  49.1 us
    all_gather x1, waiting for transfers between devices, shards(): lax.all_gather(wq_a, 'expert', axis=1, tiled=True)  46.5 us
    another operation x1, loops' own time, shards(): lax.map(one_owner, jnp.arange(lax.axis_size('expert') * tok_rows // tok_r...  42.5 us
  transfers between devices with their start and end apart: 4, of which 4 were waited for; matrix products, arithmetic and copies ran while one was open for 1% of the time, Pallas kernels for 0%

commit v1 on v0

v1 whole, which is shorter than its diff:
```python
import jax
import jax.numpy as jnp
import numpy as np
from jax import lax
from jax.experimental import pallas as pl
from jax.experimental.pallas import tpu as pltpu
from jax.sharding import PartitionSpec as P

D = 7168
QL = 1536
CAP = 20
HOLD = 16
SLOTS = HOLD * CAP
SIDE = 4
RING = 16
ROUTE_SCALE = 2.5
EPSILON = 1e-06

GROUPS = ((0, 512), (512, 512), (1024, 384), (1408, 384))
ORDERS = ("PQpq", "QpqP", "pqPQ", "qPQp")
EVEN = (1, 0, 3, 2)
ODD = (3, 2, 1, 0)


def partner(kind, place):
    slow, fast = divmod(place, SIDE)
    if kind == "P":
        slow = EVEN[slow]
    elif kind == "Q":
        slow = ODD[slow]
    elif kind == "p":
        fast = EVEN[fast]
    else:
        fast = ODD[fast]
    return slow * SIDE + fast


def order_of(group, half):
    return ORDERS[(group + 2 * half) % 4]


def keep(order, step, place):
    if step == 4:
        return [place]
    return keep(order, step + 1, partner(order[step], place)) + keep(order, step + 1, place)


def owner_table():
    return np.array(
        [[[keep(order_of(g, h), 0, e) for g in range(4)] for e in range(RING)] for h in range(2)],
        np.int32,
    )


def holder_table():
    return np.array(
        [[[e] + [partner(order_of(g, h)[0], e) for g in range(4)] for e in range(RING)] for h in range(2)],
        np.int32,
    )


def swap(value, group, step):
    pairs = [
        (half * RING + e, half * RING + partner(order_of(group, half)[step], e))
        for half in range(2)
        for e in range(RING)
    ]
    return lax.ppermute(value, ("dp", "expert"), pairs)


def relay_kernel(owner_ref, x_ref, first_ref, second_ref, keep_ref, turned):
    turned[...] = jnp.swapaxes(x_ref[...], 0, 1)
    for i in range(4):
        first_ref[i] = turned[owner_ref[i]]
        second_ref[i] = turned[owner_ref[4 + i]]
    for i in range(8):
        keep_ref[i] = turned[owner_ref[8 + i]]


def relay(slots, owners, start, width):
    lanes = 128
    base = start // lanes
    out = lambda n: pl.BlockSpec((n, SLOTS, lanes), lambda j, o: (0, 0, j))
    return pl.pallas_call(
        relay_kernel,
        grid_spec=pltpu.PrefetchScalarGridSpec(
            num_scalar_prefetch=1,
            grid=(width // lanes,),
            in_specs=[pl.BlockSpec((SLOTS, RING, lanes), lambda j, o: (0, 0, base + j))],
            out_specs=[out(4), out(4), out(8)],
            scratch_shapes=[pltpu.VMEM((RING, SLOTS, lanes), jnp.bfloat16)],
        ),
        out_shape=[
            jax.ShapeDtypeStruct((n, SLOTS, width), jnp.bfloat16) for n in (4, 4, 8)
        ],
        compiler_params=pltpu.CompilerParams(vmem_limit_bytes=40 << 20),
        cost_estimate=pl.CostEstimate(
            flops=0, bytes_accessed=2 * RING * SLOTS * width * 2, transcendentals=0
        ),
        name="relay",
    )(owners, slots)


def route_kernel(packed_ref, expert_ref, earlier_ref, out_ref):
    table = packed_ref[0].astype(jnp.float32).T
    levels = table[:, 8:16]
    weight = ROUTE_SCALE * levels / jnp.sum(levels, axis=1, keepdims=True)
    experts = expert_ref[0:1, :]
    named = jnp.zeros((table.shape[0], 128), jnp.float32)
    weighed = jnp.zeros((table.shape[0], 128), jnp.float32)
    for k in range(8):
        hit = table[:, k : k + 1] == experts
        named = jnp.where(hit, 1.0, named)
        weighed = jnp.where(hit, weight[:, k : k + 1], weighed)
    rank = jnp.dot(earlier_ref[...], named.astype(jnp.bfloat16), preferred_element_type=jnp.float32)
    out_ref[0, :, 0:128] = weighed.astype(jnp.bfloat16)
    out_ref[0, :, 128:256] = rank.astype(jnp.bfloat16)


def route(packed, experts, earlier, tokens):
    return pl.pallas_call(
        route_kernel,
        grid=(RING,),
        in_specs=[
            pl.BlockSpec((1, 16, tokens), lambda i: (i, 0, 0)),
            pl.BlockSpec((8, 128), lambda i: (0, 0)),
            pl.BlockSpec((tokens, tokens), lambda i: (0, 0)),
        ],
        out_specs=pl.BlockSpec((1, tokens, 256), lambda i: (i, 0, 0)),
        out_shape=jax.ShapeDtypeStruct((RING, tokens, 256), jnp.bfloat16),
        compiler_params=pltpu.CompilerParams(vmem_limit_bytes=40 << 20),
        cost_estimate=pl.CostEstimate(
            flops=RING * 2 * tokens * tokens * 128 * 4, bytes_accessed=RING * tokens * 512, transcendentals=0
        ),
        name="route",
    )(packed, experts, earlier)


def combine_kernel(owner_ref, route_ref, spread_ref, turn_ref, mine_ref, theirs_ref, out_ref, rows):
    rows[0:SLOTS] = mine_ref[0]
    rows[SLOTS : 2 * SLOTS] = theirs_ref[0]
    weight = jnp.dot(route_ref[0, :, 0:128], spread_ref[...], preferred_element_type=jnp.float32)
    rank = jnp.dot(route_ref[0, :, 128:256], spread_ref[...], preferred_element_type=jnp.float32)
    matrix = jnp.where(rank == turn_ref[0:1, :], weight, 0.0).astype(jnp.bfloat16)
    out_ref[0] = jnp.dot(matrix, rows[...], preferred_element_type=jnp.float32).astype(jnp.bfloat16)


def combine(owners, routes, spread, turn, mine, theirs, first, count, tokens):
    width = mine.shape[2]
    return pl.pallas_call(
        combine_kernel,
        grid_spec=pltpu.PrefetchScalarGridSpec(
            num_scalar_prefetch=1,
            grid=(count,),
            in_specs=[
                pl.BlockSpec((1, tokens, 256), lambda i, o: (o[8 + first + i], 0, 0)),
                pl.BlockSpec((128, 2 * SLOTS), lambda i, o: (0, 0)),
                pl.BlockSpec((8, 2 * SLOTS), lambda i, o: (0, 0)),
                pl.BlockSpec((1, SLOTS, width), lambda i, o: (first + i, 0, 0)),
                pl.BlockSpec((1, SLOTS, width), lambda i, o: (first % 4 + i, 0, 0)),
            ],
            out_specs=pl.BlockSpec((1, tokens, width), lambda i, o: (i, 0, 0)),
            scratch_shapes=[pltpu.VMEM((2 * SLOTS, width), jnp.bfloat16)],
        ),
        out_shape=jax.ShapeDtypeStruct((count, tokens, width), jnp.bfloat16),
        compiler_params=pltpu.CompilerParams(vmem_limit_bytes=40 << 20),
        cost_estimate=pl.CostEstimate(
            flops=count * 2 * tokens * 2 * SLOTS * (width + 256),
            bytes_accessed=count * (tokens * width + 2 * SLOTS * width + tokens * 256) * 2,
            transcendentals=0,
        ),
        name="combine",
    )(owners, routes, spread, turn, mine, theirs)


def wide(value):
    return value.astype(jnp.float32)


def shards(expert_out, expert_ids, gate_levels, residual, attn_gain, wq_a, latent_gain, wq_b):
    half = lax.axis_index("dp")
    place = lax.axis_index("expert")
    lane = lax.axis_index("tensor")
    tokens = expert_ids.shape[0]
    columns = residual.shape[1]

    owners = jnp.asarray(owner_table())[half, place]
    holders = jnp.asarray(holder_table())[half, place]
    experts = (holders[:, None] * HOLD + jnp.arange(HOLD, dtype=jnp.int32)[None, :]).reshape(-1)
    experts = jnp.concatenate([experts, jnp.full((128 - experts.shape[0],), -1, jnp.int32)])
    experts = jnp.broadcast_to(experts.astype(jnp.float32)[None, :], (8, 128))

    packed = jnp.concatenate([expert_ids.T, gate_levels.T], axis=0)
    packed = lax.all_gather(packed, "expert", axis=0)

    part = wq_b.shape[0] // 2
    down_mine = lax.dynamic_slice_in_dim(wq_a.T, half * part, part, 0)
    up_mine = lax.dynamic_slice_in_dim(wq_b, half * part, part, 0)
    down_mine = lax.all_gather(down_mine, "expert", axis=0, tiled=True)
    up_mine = lax.all_gather(up_mine, "expert", axis=0, tiled=True)
    other = [(0, 1), (1, 0)]
    down_theirs = lax.ppermute(down_mine, "dp", other)
    up_theirs = lax.ppermute(up_mine, "dp", other)
    gain = latent_gain.reshape(RING, 2, part).transpose(1, 0, 2)
    gain = jnp.concatenate([gain[half], gain[1 - half]], axis=0).reshape(-1)

    slots = expert_out.transpose(0, 2, 1, 3).reshape(SLOTS, RING, columns)
    relayed = [relay(slots, owners[g], *GROUPS[g]) for g in range(4)]
    first = [[swap(relayed[g][i], g, 0) for g in range(4)] for i in range(2)]

    position = jnp.arange(tokens, dtype=jnp.int32)
    earlier = (position[:, None] > position[None, :]).astype(jnp.bfloat16)
    routes = route(packed, experts, earlier, tokens)
    slot = np.arange(SLOTS)
    turn = jnp.asarray(np.broadcast_to(np.tile(slot % CAP, 2)[None, :], (8, 2 * SLOTS)).astype(np.float32))
    lanes = np.arange(128)[:, None]
    spread = [
        jnp.asarray(
            np.concatenate(
                [lanes == (slot // CAP)[None, :], lanes == (slot // CAP)[None, :] + HOLD * (g + 1)], axis=1
            ).astype(np.float32)
        ).astype(jnp.bfloat16)
        for g in range(4)
    ]

    def summed(g, start, received):
        return combine(owners[g], routes, spread[g], turn, relayed[g][2], received, start, 2, tokens)

    pass_a = [summed(g, 0, first[0][g]) for g in range(4)]
    second_a = [swap(pass_a[g], g, 1) for g in range(4)]
    pass_b = [summed(g, 2, first[0][g]) for g in range(4)]
    second_b = [swap(pass_b[g], g, 1) for g in range(4)]
    kept_a = [summed(g, 4, first[1][g]) for g in range(4)]
    kept_b = [summed(g, 6, first[1][g]) for g in range(4)]
    third = [
        swap((wide(kept_a[g]) + wide(second_a[g])).astype(jnp.bfloat16), g, 2) for g in range(4)
    ]
    fourth = [
        swap(
            (wide(kept_b[g][0]) + wide(second_b[g][0]) + wide(third[g][0])).astype(jnp.bfloat16), g, 3
        )
        for g in range(4)
    ]
    combined = jnp.concatenate(
        [
            wide(kept_b[g][1]) + wide(second_b[g][1]) + wide(third[g][1]) + wide(fourth[g])
            for g in range(4)
        ],
        axis=1,
    )
    stream = (wide(residual) + combined).astype(jnp.bfloat16)
    stream_wide = wide(stream)
    squares = lax.psum(jnp.sum(stream_wide * stream_wide, axis=1), "tensor")
    scaled = (stream_wide * attn_gain).astype(jnp.bfloat16)
    over_rows = (((1,), (1,)), ((), ()))
    latent = jnp.concatenate(
        [
            lax.dot_general(scaled, weights, over_rows, preferred_element_type=jnp.float32)
            for weights in (down_mine, down_theirs)
        ],
        axis=1,
    ).astype(jnp.bfloat16)
    count = lax.axis_size("tensor")
    rows = tokens // count
    latent = latent.reshape(count, rows, QL)

    def turned(value, shift):
        return lax.ppermute(value, "tensor", [(y, (y + shift) % count) for y in range(count)])

    total = wide(lax.dynamic_index_in_dim(latent, lane, 0, keepdims=False))
    for shift in (2, 1, 3):
        piece = lax.dynamic_index_in_dim(latent, (lane + shift) % count, 0, keepdims=False)
        total = total + wide(turned(piece, shift))
    inv_scale = lax.rsqrt(squares / D + EPSILON)
    normed = (stream_wide * inv_scale[:, None] * attn_gain).astype(jnp.bfloat16)
    total = total * lax.dynamic_slice_in_dim(inv_scale, lane * rows, rows, 0)[:, None]
    latent_scale = lax.rsqrt(jnp.sum(total * total, axis=1) / QL + EPSILON)
    compressed = (total * latent_scale[:, None] * gain).astype(jnp.bfloat16)
    everyone = jnp.zeros((count, rows, QL), jnp.bfloat16)
    everyone = lax.dynamic_update_index_in_dim(everyone, compressed, lane, 0)
    for shift in (2, 1, 3):
        everyone = lax.dynamic_update_index_in_dim(
            everyone, turned(compressed, shift), (lane - shift) % count, 0
        )
    everyone = everyone.reshape(tokens, QL)
    middle = QL // 2
    queries = jnp.dot(everyone[:, :middle], up_mine, preferred_element_type=jnp.float32) + jnp.dot(
        everyone[:, middle:], up_theirs, preferred_element_type=jnp.float32
    )
    return (stream, normed, queries.astype(jnp.bfloat16))


def solution(mesh):
    return jax.shard_map(
        shards,
        mesh=mesh,
        in_specs=(
            P(("dp", "expert"), None, None, "tensor"),
            P(("dp", "expert"), None),
            P(("dp", "expert"), None),
            P(("dp", "expert"), "tensor"),
            P("tensor"),
            P("tensor", "expert"),
            P(),
            P("expert", "tensor"),
        ),
        out_specs=(
            P(("dp", "expert"), "tensor"),
            P(("dp", "expert"), "tensor"),
            P(("dp", "expert"), "tensor"),
        ),
        check_vma=False,
    )
```

time: 1260 us -> 317 us (0.25)
  local copies, waits for them, and re-layouts: 591 us -> 14.6 us
  waiting for transfers between devices: 357 us -> 28.2 us
  Pallas kernels: 0 us -> 102 us
  other arithmetic: 127 us -> 26.9 us
  matrix products: 76.1 us -> 13.7 us
  starting transfers between devices: 0.16 us -> 57.3 us
  loops' own time: 43.8 us -> 0 us
    gather x80 -> x0, local copies, waits for them, and re-layouts: 533 us -> none  [block_ranks(): return jnp.take_along_axis(before, owner_ids, axis=1).astype(jnp.int32)]
    reduce_scatter x1 -> x0, waiting for transfers between devices: 184 us -> none  [shards(): lax.psum_scatter(blocks.reshape(lax.axis_size('expert') * tok_rows, colum...]
    all_gather x2, waiting for transfers between devices: 123 us -> 0.02 us  [the longest x1 0.02 us: shards(): down_mine = lax.all_gather(down_mine, 'expert', axis=0, tiled=True)]
    pallas_call x0 -> x21, Pallas kernels: none -> 102 us  [the longest x16 56 us: combine(): pl.pallas_call(combine_kernel, grid_spec=pltpu.PrefetchScalarGridSpec(num...]
    reduce_sum x35 -> x2, other arithmetic: 102 us -> 4.12 us  [the longest x1 2.61 us: shards(): squares = lax.psum(jnp.sum(stream_wide * stream_wide, axis=1), 'tensor')]
    dot_general x34 -> x4, matrix products: 76.1 us -> 13.7 us  [the longest x2 5.05 us: shards(): lax.dot_general(scaled, weights, over_rows, preferred_element_type=jnp.fl...]
    ppermute x0 -> x32, starting transfers between devices: none -> 57.2 us  [the longest x24 31.7 us: swap(): return lax.ppermute(value, ('dp', 'expert'), pairs)]
    psum x1 -> x0, waiting for transfers between devices: 49.5 us -> none  [shards(): lax.psum(partial_value.astype(jnp.bfloat16), 'tensor').astype(jnp.float32)]
  transfers between devices with their start and end apart: 4 -> 34, of which waited for: 4 -> 6; matrix products, arithmetic and copies ran while one was open for 1% -> 11% of each run, Pallas kernels for 0% -> 32%
where the time goes in v1:
time: 317 us; the launch traced here: 316 us
  Pallas kernels  102 us (32%)
  blocking collectives  58.5 us (18%)
  starting transfers between devices  57.3 us (18%)
  waiting for transfers between devices  28.2 us (9%)
  other arithmetic  26.9 us (8%)
  between operations  14.8 us (5%)
  local copies, waits for them, and re-layouts  14.6 us (5%)
  matrix products  13.7 us (4%)
    pallas_call x16, Pallas kernels, combine(): pl.pallas_call(combine_kernel, grid_spec=pltpu.PrefetchScalarGridSpec(num...  56 us
    all_gather x1, blocking collectives, shards(): packed = lax.all_gather(packed, 'expert', axis=0)  38.9 us
    ppermute x24, starting transfers between devices, swap(): return lax.ppermute(value, ('dp', 'expert'), pairs)  31.7 us
    pallas_call x1, Pallas kernels, route(): pl.pallas_call(route_kernel, grid=(RING,), in_specs=[pl.BlockSpec((1, 16,...  23.8 us
    pallas_call x4, Pallas kernels, relay(): pl.pallas_call(relay_kernel, grid_spec=pltpu.PrefetchScalarGridSpec(num_s...  22.3 us
    psum x1, blocking collectives, shards(): squares = lax.psum(jnp.sum(stream_wide * stream_wide, axis=1), 'tensor')  19.7 us
    ppermute x6, waiting for transfers between devices, turned(): lax.ppermute(value, 'tensor', [(y, (y + shift) % count) for y in range(co...  16 us
    ppermute x1, starting transfers between devices, shards(): down_theirs = lax.ppermute(down_mine, 'dp', other)  14.5 us
  transfers between devices with their start and end apart: 34, of which 6 were waited for; matrix products, arithmetic and copies ran while one was open for 11% of the time, Pallas kernels for 32%

profile of v1, /device:TPU:1, one launch (start us, length us, event | category | flops | bytes accessed | tf_op | source)
XLA Modules:
  0.0 316.0 jit_solution(15675782777876665403)
XLA Ops:
  10.5 5.3 %relay.6 = (bf16[4,320,384]{2,1,0:T(8,128)(2,1)}, bf16[4,320,384]{2,1,0:T(8,128)(2,1)}, bf16[8,320,384]{2,1,0:T(8,128)(2,1)S(1)}) custom-call(s32[16]{0:T(128)S(1)} %get-tuple-element.40.owner_ref, bf16[320,16,1792]{2,1,0:T(8,128)(2,1)} %bitcast.64), custom_call_target="tpu_custom_call" | custom-call | bytes 7864320 | tf_op jit(solution)/shard_map/relay/pallas_call | solution.py:84
  19.6 5.2 %relay.7 = (bf16[4,320,384]{2,1,0:T(8,128)(2,1)}, bf16[4,320,384]{2,1,0:T(8,128)(2,1)S(1)}, bf16[8,320,384]{2,1,0:T(8,128)(2,1)S(1)}) custom-call(s32[16]{0:T(128)S(1)} %get-tuple-element.39.owner_ref, bf16[320,16,1792]{2,1,0:T(8,128)(2,1)} %bitcast.65), custom_call_target="tpu_custom_call" | custom-call | bytes 7864320 | tf_op jit(solution)/shard_map/relay/pallas_call | solution.py:84
  26.1 3.6 %collective-permute-start.19 = (bf16[4,320,384]{2,1,0:T(8,128)(2,1)}, bf16[4,320,384]{2,1,0:T(8,128)(2,1)}, u32[]{:S(2)}, u32[]{:S(2)}) collective-permute-start(bf16[4,320,384]{2,1,0:T(8,128)(2,1)} %get-tuple-element.26), channel_id=1, source_target_pairs={{0,12},{4,8},{8,4},{12,0},{16,28},{20,24},{24,20},{28,16},{32,44},... | collective-permute-start | bytes 2949128 | tf_op jit(solution)/shard_map/ppermute | solution.py:68
  29.7 5.9 %relay.4 = (bf16[4,320,512]{2,1,0:T(8,128)(2,1)}, bf16[4,320,512]{2,1,0:T(8,128)(2,1)S(1)}, bf16[8,320,512]{2,1,0:T(8,128)(2,1)S(1)}) custom-call(s32[16]{0:T(128)S(1)} %get-tuple-element.38.owner_ref, bf16[320,16,1792]{2,1,0:T(8,128)(2,1)} %bitcast.66), custom_call_target="tpu_custom_call" | custom-call | bytes 10485760 | tf_op jit(solution)/shard_map/relay/pallas_call | solution.py:84
  36.8 5.9 %relay.5 = (bf16[4,320,512]{2,1,0:T(8,128)(2,1)}, bf16[4,320,512]{2,1,0:T(8,128)(2,1)S(1)}, bf16[8,320,512]{2,1,0:T(8,128)(2,1)S(1)}) custom-call(s32[16]{0:T(128)S(1)} %get-tuple-element.41.owner_ref, bf16[320,16,1792]{2,1,0:T(8,128)(2,1)} %bitcast.67), custom_call_target="tpu_custom_call" | custom-call | bytes 10485760 | tf_op jit(solution)/shard_map/relay/pallas_call | solution.py:84
  48.5 38.9 %all-gather = s32[256,512]{1,0:T(8,128)S(1)} all-gather(s32[16,512]{1,0:T(8,128)S(1)} %pad_add_fusion), channel_id=2, replica_groups=mesh['dp'=2,'expert'=16,'tensor'=4] {'expert'}, dimensions={0}, use_global_device_ids=true | all-gather | bytes 557056 | tf_op jit(solution)/shard_map/all_gather | solution.py:194
  91.0 23.8 %route.1.route_ref = bf16[16,512,256]{2,1,0:T(8,128)(2,1)S(1)} custom-call(s32[16,16,512]{2,1,0:T(8,128)S(1)} %bitcast.63, f32[8,128]{1,0:T(8,128)S(1)} %broadcast_in_dim.31.expert_ref, bf16[512,512]{1,0:T(8,128)(2,1)S(1)} %fusion.15.earlier_ref), custom_call_target="tpu_custom_call" | custom-call | flops 4294967296 | bytes 4194304 | tf_op jit(solution)/shard_map/route/pallas_call | solution.py:121
  114.8 4.3 %combine.27 = bf16[2,512,384]{2,1,0:T(8,128)(2,1)} custom-call(s32[16]{0:T(128)S(1)} %get-tuple-element.40.owner_ref, bf16[16,512,256]{2,1,0:T(8,128)(2,1)S(1)} %route.1.route_ref, bf16[128,640]{1,0:T(8,128)(2,1)S(1)} %copy-done.19, f32[8,640]{1,0:T(8,128)S(1)} %copy-done.11, bf16[8,320,384]{2,1,0:T(8,128)(2,1)S(1)} %copy-done.9, ...), custom_call_target="tpu_custom_call" | custom-call | flops 838860800 | bytes 2293760 | tf_op jit(solution)/shard_map/combine/pallas_call | solution.py:150
  130.6 3.4 %combine.24 = bf16[2,512,384]{2,1,0:T(8,128)(2,1)S(1)} custom-call(s32[16]{0:T(128)S(1)} %get-tuple-element.40.owner_ref, bf16[16,512,256]{2,1,0:T(8,128)(2,1)S(1)} %copy-done.3, bf16[128,640]{1,0:T(8,128)(2,1)S(1)} %copy-done.20, f32[8,640]{1,0:T(8,128)S(1)} %copy-done.11, bf16[8,320,384]{2,1,0:T(8,128)(2,1)S(1)} %copy-done.10, ...), custom_call_target="tpu_custom_call" | custom-call | flops 838860800 | bytes 2293760 | tf_op jit(solution)/shard_map/combine/pallas_call | solution.py:150
  140.6 3.3 %combine.19 = bf16[2,512,512]{2,1,0:T(8,128)(2,1)S(1)} custom-call(s32[16]{0:T(128)S(1)} %get-tuple-element.38.owner_ref, bf16[16,512,256]{2,1,0:T(8,128)(2,1)S(1)} %copy-done.3, bf16[128,640]{1,0:T(8,128)(2,1)S(1)} %copy-done.17, f32[8,640]{1,0:T(8,128)S(1)} %copy-done.11, bf16[8,320,512]{2,1,0:T(8,128)(2,1)S(1)} %get-tuple-element.15.mine_ref, ...), custom_call_target="tpu_custom_call" | custom-call | flops 1006632960 | bytes 2883584 | tf_op jit(solution)/shard_map/combine/pallas_call | solution.py:150
  149.2 4.4 %combine.17 = bf16[2,512,512]{2,1,0:T(8,128)(2,1)} custom-call(s32[16]{0:T(128)S(1)} %get-tuple-element.38.owner_ref, bf16[16,512,256]{2,1,0:T(8,128)(2,1)S(1)} %copy-done.3, bf16[128,640]{1,0:T(8,128)(2,1)S(1)} %copy-done.17, f32[8,640]{1,0:T(8,128)S(1)} %copy-done.11, bf16[8,320,512]{2,1,0:T(8,128)(2,1)S(1)} %get-tuple-element.15.mine_ref, ...), custom_call_target="tpu_custom_call" | custom-call | flops 1006632960 | bytes 2883584 | tf_op jit(solution)/shard_map/combine/pallas_call | solution.py:150
  153.6 3.3 %combine.23 = bf16[2,512,512]{2,1,0:T(8,128)(2,1)S(1)} custom-call(s32[16]{0:T(128)S(1)} %get-tuple-element.41.owner_ref, bf16[16,512,256]{2,1,0:T(8,128)(2,1)S(1)} %copy-done.3, bf16[128,640]{1,0:T(8,128)(2,1)S(1)} %copy-done.16, f32[8,640]{1,0:T(8,128)S(1)} %copy-done.11, bf16[8,320,512]{2,1,0:T(8,128)(2,1)S(1)} %copy-done.5, ...), custom_call_target="tpu_custom_call" | custom-call | flops 1006632960 | bytes 2883584 | tf_op jit(solution)/shard_map/combine/pallas_call | solution.py:150
  161.3 4.1 %combine.21 = bf16[2,512,512]{2,1,0:T(8,128)(2,1)} custom-call(s32[16]{0:T(128)S(1)} %get-tuple-element.41.owner_ref, bf16[16,512,256]{2,1,0:T(8,128)(2,1)S(1)} %copy-done.3, bf16[128,640]{1,0:T(8,128)(2,1)S(1)} %copy-done.16, f32[8,640]{1,0:T(8,128)S(1)} %copy-done.11, bf16[8,320,512]{2,1,0:T(8,128)(2,1)S(1)} %copy-done.5, ...), custom_call_target="tpu_custom_call" | custom-call | flops 1006632960 | bytes 2883584 | tf_op jit(solution)/shard_map/combine/pallas_call | solution.py:150
  165.5 3.3 %combine.18 = bf16[2,512,512]{2,1,0:T(8,128)(2,1)S(1)} custom-call(s32[16]{0:T(128)S(1)} %get-tuple-element.38.owner_ref, bf16[16,512,256]{2,1,0:T(8,128)(2,1)S(1)} %copy-done.3, bf16[128,640]{1,0:T(8,128)(2,1)S(1)} %copy-done.17, f32[8,640]{1,0:T(8,128)S(1)} %copy-done.11, bf16[8,320,512]{2,1,0:T(8,128)(2,1)S(1)} %get-tuple-element.15.mine_ref, ...), custom_call_target="tpu_custom_call" | custom-call | flops 1006632960 | bytes 2883584 | tf_op jit(solution)/shard_map/combine/pallas_call | solution.py:150
  168.8 3.3 %combine.22 = bf16[2,512,512]{2,1,0:T(8,128)(2,1)S(1)} custom-call(s32[16]{0:T(128)S(1)} %get-tuple-element.41.owner_ref, bf16[16,512,256]{2,1,0:T(8,128)(2,1)S(1)} %copy-done.3, bf16[128,640]{1,0:T(8,128)(2,1)S(1)} %copy-done.16, f32[8,640]{1,0:T(8,128)S(1)} %copy-done.11, bf16[8,320,512]{2,1,0:T(8,128)(2,1)S(1)} %copy-done.5, ...), custom_call_target="tpu_custom_call" | custom-call | flops 1006632960 | bytes 2883584 | tf_op jit(solution)/shard_map/combine/pallas_call | solution.py:150
  184.2 7.8 %collective-permute-done.20 = bf16[2,512,384]{2,1,0:T(8,128)(2,1)S(1)} collective-permute-done((bf16[2,512,384]{2,1,0:T(8,128)(2,1)S(1)}, bf16[2,512,384]{2,1,0:T(8,128)(2,1)S(1)}, u32[]{:S(2)}, u32[]{:S(2)}) %collective-permute-start.20) | collective-permute-done | bytes 786464 | tf_op jit(solution)/shard_map/ppermute | solution.py:68
  202.9 3.3 %combine.20 = bf16[2,512,512]{2,1,0:T(8,128)(2,1)S(1)} custom-call(s32[16]{0:T(128)S(1)} %get-tuple-element.41.owner_ref, bf16[16,512,256]{2,1,0:T(8,128)(2,1)S(1)} %copy-done.3, bf16[128,640]{1,0:T(8,128)(2,1)S(1)} %copy-done.16, f32[8,640]{1,0:T(8,128)S(1)} %copy-done.11, bf16[8,320,512]{2,1,0:T(8,128)(2,1)S(1)} %copy-done.5, ...), custom_call_target="tpu_custom_call" | custom-call | flops 1006632960 | bytes 2883584 | tf_op jit(solution)/shard_map/combine/pallas_call | solution.py:150
  206.4 14.5 %collective-permute-start.24 = (bf16[768,1792]{1,0:T(8,128)(2,1)}, bf16[768,1792]{1,0:T(8,128)(2,1)}, u32[]{:S(2)}, u32[]{:S(2)}) collective-permute-start(bf16[768,1792]{1,0:T(8,128)(2,1)} %all-gather.4.cloned.1.call-done), channel_id=1, source_target_pairs={{0,64},{64,0},{1,65},{65,1},{2,66},{66,2},{3,67},{67,3},{4,68},{68... | collective-permute-start | bytes 8257544 | tf_op jit(solution)/shard_map/ppermute | solution.py:202
  247.2 3.4 %fusion.12 = bf16[512,768]{1,0:T(8,128)(2,1)S(1)} fusion(bf16[768,1792]{1,0:T(8,128)(2,1)} %collective-permute-done.24, bf16[512,1792]{1,0:T(8,128)(2,1)S(1)} %get-tuple-element.32, f32[1792]{0:T(1024)S(1)} %copy-done.34), kind=kOutput, calls=%fused_computation.25 | convolution fusion | flops 1412431872 | bytes 5381120 | tf_op jit(solution)/shard_map/dot_general | solution.py:258
  257.8 19.7 %psum.7 = f32[512]{0:T(512)S(1)} all-reduce(f32[512]{0:T(512)S(1)} %get-tuple-element.31), channel_id=1, replica_groups=mesh['dp'=2,'expert'=16,'tensor'=4] {'tensor'}, use_global_device_ids=true, to_apply=%region_1.0 | all-reduce | flops 512 | bytes 4096 | tf_op jit(solution)/shard_map/psum | solution.py:253
  284.4 5.8 %collective-permute-done.28 = bf16[128,1536]{1,0:T(8,128)(2,1)S(1)} collective-permute-done((bf16[128,1536]{1,0:T(8,128)(2,1)S(1)}, bf16[128,1536]{1,0:T(8,128)(2,1)S(1)}, u32[]{:S(2)}, u32[]{:S(2)}) %collective-permute-start.28) | collective-permute-done | bytes 393248 | tf_op jit(solution)/shard_map/ppermute | solution.py:268
  290.3 10.1 %collective-permute-done.29 = bf16[128,1536]{1,0:T(8,128)(2,1)S(1)} collective-permute-done((bf16[128,1536]{1,0:T(8,128)(2,1)S(1)}, bf16[128,1536]{1,0:T(8,128)(2,1)S(1)}, u32[]{:S(2)}, u32[]{:S(2)}) %collective-permute-start.29) | collective-permute-done | bytes 393248 | tf_op jit(solution)/shard_map/ppermute | solution.py:268
  300.5 4.6 %fusion.16 = f32[512,3072]{1,0:T(8,128)S(1)} fusion(bf16[768,3072]{1,0:T(8,128)(2,1)} %collective-permute-done.31, bf16[512,1536]{1,0:T(8,128)(2,1)S(1)} %bitcast.72), kind=kOutput, calls=%fused_computation.32 | convolution fusion | flops 2415919104 | bytes 11796480 | tf_op jit(solution)/shard_map/dot_general | solution.py:287
  305.2 4.0 %add_convert_fusion = bf16[512,3072]{1,0:T(8,128)(2,1)} fusion(f32[512,3072]{1,0:T(8,128)S(1)} %fusion.16, bf16[768,3072]{1,0:T(8,128)(2,1)S(1)} %bitcast.79, bf16[512,1536]{1,0:T(8,128)(2,1)S(1)} %bitcast.73), kind=kOutput, calls=%fused_computation | convolution fusion | flops 2419064832 | bytes 14942208 | tf_op jit(solution)/shard_map/dot_general | solution.py:287
  (191 shorter events, 109.8 us)
Async XLA Ops:
  7.2 199.2 %all-gather.4.cloned.1.call-start = ((), (), s32[]{:S(2)}) async-start(), calls=%async_computation | async-start | bytes 2924544 | tf_op jit(solution)/shard_map/all_gather | solution.py:199
  8.9 231.3 %all-gather.6.cloned.1.call-start = ((), (), s32[]{:S(2)}) async-start(), calls=%async_computation.1 | async-start | bytes 5013504 | tf_op jit(solution)/shard_map/all_gather | solution.py:200
  17.1 70.3 %collective-permute-start.13 = (bf16[4,320,384]{2,1,0:T(8,128)(2,1)}, bf16[4,320,384]{2,1,0:T(8,128)(2,1)}, u32[]{:S(2)}, u32[]{:S(2)}) collective-permute-start(bf16[4,320,384]{2,1,0:T(8,128)(2,1)} %get-tuple-element.23), channel_id=1, source_target_pairs={{0,4},{4,0},{8,12},{12,8},{16,20},{20,16},{24,28},{28,24},{32,36},... | collective-permute-start | bytes 2949128 | tf_op jit(solution)/shard_map/ppermute | solution.py:68
  19.6 68.0 %collective-permute-start.12 = (bf16[4,320,384]{2,1,0:T(8,128)(2,1)}, bf16[4,320,384]{2,1,0:T(8,128)(2,1)}, u32[]{:S(2)}, u32[]{:S(2)}) collective-permute-start(bf16[4,320,384]{2,1,0:T(8,128)(2,1)} %get-tuple-element.22), channel_id=1, source_target_pairs={{0,4},{4,0},{8,12},{12,8},{16,20},{20,16},{24,28},{28,24},{32,36},... | collective-permute-start | bytes 2949128 | tf_op jit(solution)/shard_map/ppermute | solution.py:68
  26.1 63.0 %collective-permute-start.19 = (bf16[4,320,384]{2,1,0:T(8,128)(2,1)}, bf16[4,320,384]{2,1,0:T(8,128)(2,1)}, u32[]{:S(2)}, u32[]{:S(2)}) collective-permute-start(bf16[4,320,384]{2,1,0:T(8,128)(2,1)} %get-tuple-element.26), channel_id=1, source_target_pairs={{0,12},{4,8},{8,4},{12,0},{16,28},{20,24},{24,20},{28,16},{32,44},... | collective-permute-start | bytes 2949128 | tf_op jit(solution)/shard_map/ppermute | solution.py:68
  35.6 83.6 %collective-permute-start.1 = (bf16[4,320,512]{2,1,0:T(8,128)(2,1)}, bf16[4,320,512]{2,1,0:T(8,128)(2,1)}, u32[]{:S(2)}, u32[]{:S(2)}) collective-permute-start(bf16[4,320,512]{2,1,0:T(8,128)(2,1)} %get-tuple-element.17), channel_id=1, source_target_pairs={{0,16},{4,20},{8,24},{12,28},{16,0},{20,4},{24,8},{28,12},{32,48},... | collective-permute-start | bytes 3932168 | tf_op jit(solution)/shard_map/ppermute | solution.py:68
  45.2 99.0 %collective-permute-start.7 = (bf16[4,320,512]{2,1,0:T(8,128)(2,1)}, bf16[4,320,512]{2,1,0:T(8,128)(2,1)}, u32[]{:S(2)}, u32[]{:S(2)}) collective-permute-start(bf16[4,320,512]{2,1,0:T(8,128)(2,1)} %get-tuple-element.20), channel_id=1, source_target_pairs={{0,48},{4,52},{8,56},{12,60},{16,32},{20,36},{24,40},{28,44},{32,1... | collective-permute-start | bytes 3932168 | tf_op jit(solution)/shard_map/ppermute | solution.py:68
  87.4 73.1 %collective-permute-start = (bf16[4,320,512]{2,1,0:T(8,128)(2,1)}, bf16[4,320,512]{2,1,0:T(8,128)(2,1)}, u32[]{:S(2)}, u32[]{:S(2)}) collective-permute-start(bf16[4,320,512]{2,1,0:T(8,128)(2,1)} %copy-done.21), channel_id=1, source_target_pairs={{0,16},{4,20},{8,24},{12,28},{16,0},{20,4},{24,8},{28,12},{32,48},... | collective-permute-start | bytes 3932168 | tf_op jit(solution)/shard_map/ppermute | solution.py:68
  87.6 72.9 %collective-permute-start.6 = (bf16[4,320,512]{2,1,0:T(8,128)(2,1)}, bf16[4,320,512]{2,1,0:T(8,128)(2,1)}, u32[]{:S(2)}, u32[]{:S(2)}) collective-permute-start(bf16[4,320,512]{2,1,0:T(8,128)(2,1)} %copy-done.22), channel_id=1, source_target_pairs={{0,48},{4,52},{8,56},{12,60},{16,32},{20,36},{24,40},{28,44},{32,1... | collective-permute-start | bytes 3932168 | tf_op jit(solution)/shard_map/ppermute | solution.py:68
  89.1 54.8 %collective-permute-start.18 = (bf16[4,320,384]{2,1,0:T(8,128)(2,1)}, bf16[4,320,384]{2,1,0:T(8,128)(2,1)}, u32[]{:S(2)}, u32[]{:S(2)}) collective-permute-start(bf16[4,320,384]{2,1,0:T(8,128)(2,1)} %copy-done.23), channel_id=1, source_target_pairs={{0,12},{4,8},{8,4},{12,0},{16,28},{20,24},{24,20},{28,16},{32,44},... | collective-permute-start | bytes 2949128 | tf_op jit(solution)/shard_map/ppermute | solution.py:68
  119.2 37.8 %collective-permute-start.15 = (bf16[2,512,384]{2,1,0:T(8,128)(2,1)}, bf16[2,512,384]{2,1,0:T(8,128)(2,1)}, u32[]{:S(2)}, u32[]{:S(2)}) collective-permute-start(bf16[2,512,384]{2,1,0:T(8,128)(2,1)} %combine.27), channel_id=1, source_target_pairs={{0,12},{4,8},{8,4},{12,0},{16,28},{20,24},{24,20},{28,16},{32,44},... | collective-permute-start | bytes 2359304 | tf_op jit(solution)/shard_map/ppermute | solution.py:68
  143.9 28.3 %collective-permute-start.21 = (bf16[2,512,384]{2,1,0:T(8,128)(2,1)S(1)}, bf16[2,512,384]{2,1,0:T(8,128)(2,1)}, u32[]{:S(2)}, u32[]{:S(2)}) collective-permute-start(bf16[2,512,384]{2,1,0:T(8,128)(2,1)S(1)} %combine.31), channel_id=1, source_target_pairs={{0,16},{4,20},{8,24},{12,28},{16,0},{20,4},{24,8},{28,12},{32,48},... | collective-permute-start | bytes 2359304 | tf_op jit(solution)/shard_map/ppermute | solution.py:68
  144.3 30.0 %collective-permute-start.3 = (bf16[2,512,512]{2,1,0:T(8,128)(2,1)S(1)}, bf16[2,512,512]{2,1,0:T(8,128)(2,1)}, u32[]{:S(2)}, u32[]{:S(2)}) collective-permute-start(bf16[2,512,512]{2,1,0:T(8,128)(2,1)S(1)} %combine.19), channel_id=1, source_target_pairs={{0,48},{4,52},{8,56},{12,60},{16,32},{20,36},{24,40},{28,44},{32,1... | collective-permute-start | bytes 3145736 | tf_op jit(solution)/shard_map/ppermute | solution.py:68
  157.0 21.4 %collective-permute-start.14 = (bf16[2,512,384]{2,1,0:T(8,128)(2,1)S(1)}, bf16[2,512,384]{2,1,0:T(8,128)(2,1)S(1)}, u32[]{:S(2)}, u32[]{:S(2)}) collective-permute-start(bf16[2,512,384]{2,1,0:T(8,128)(2,1)S(1)} %combine.25), channel_id=1, source_target_pairs={{0,12},{4,8},{8,4},{12,0},{16,28},{20,24},{24,20},{28,16},{32,44},... | collective-permute-start | bytes 2359304 | tf_op jit(solution)/shard_map/ppermute | solution.py:68
  178.4 46.2 %collective-permute-start.2 = (bf16[2,512,512]{2,1,0:T(8,128)(2,1)}, bf16[2,512,512]{2,1,0:T(8,128)(2,1)}, u32[]{:S(2)}, u32[]{:S(2)}) collective-permute-start(bf16[2,512,512]{2,1,0:T(8,128)(2,1)} %combine.17), channel_id=1, source_target_pairs={{0,48},{4,52},{8,56},{12,60},{16,32},{20,36},{24,40},{28,44},{32,1... | collective-permute-start | bytes 3145736 | tf_op jit(solution)/shard_map/ppermute | solution.py:68
  179.6 45.1 %collective-permute-start.4 = (bf16[2,512,512]{2,1,0:T(8,128)(2,1)}, bf16[2,512,512]{2,1,0:T(8,128)(2,1)}, u32[]{:S(2)}, u32[]{:S(2)}) collective-permute-start(bf16[2,512,512]{2,1,0:T(8,128)(2,1)} %add_convert_fusion.2), channel_id=1, source_target_pairs={{0,4},{4,0},{8,12},{12,8},{16,20},{20,16},{24,28},{28,24},{32,36},... | collective-permute-start | bytes 3145736 | tf_op jit(solution)/shard_map/ppermute | solution.py:68
  181.1 25.2 %collective-permute-start.17 = (bf16[512,384]{1,0:T(8,128)(2,1)S(1)}, bf16[512,384]{1,0:T(8,128)(2,1)}, u32[]{:S(2)}, u32[]{:S(2)}) collective-permute-start(bf16[512,384]{1,0:T(8,128)(2,1)S(1)} %fusion.24), channel_id=1, source_target_pairs={{0,48},{4,52},{8,56},{12,60},{16,32},{20,36},{24,40},{28,44},{32,1... | collective-permute-start | bytes 1179656 | tf_op jit(solution)/shard_map/ppermute | solution.py:68
  192.0 35.7 %collective-permute-start.8 = (bf16[2,512,512]{2,1,0:T(8,128)(2,1)}, bf16[2,512,512]{2,1,0:T(8,128)(2,1)}, u32[]{:S(2)}, u32[]{:S(2)}) collective-permute-start(bf16[2,512,512]{2,1,0:T(8,128)(2,1)} %combine.21), channel_id=1, source_target_pairs={{0,4},{4,0},{8,12},{12,8},{16,20},{20,16},{24,28},{28,24},{32,36},... | collective-permute-start | bytes 3145736 | tf_op jit(solution)/shard_map/ppermute | solution.py:68
  193.4 34.3 %collective-permute-start.10 = (bf16[2,512,512]{2,1,0:T(8,128)(2,1)}, bf16[2,512,512]{2,1,0:T(8,128)(2,1)}, u32[]{:S(2)}, u32[]{:S(2)}) collective-permute-start(bf16[2,512,512]{2,1,0:T(8,128)(2,1)} %add_convert_fusion.1), channel_id=1, source_target_pairs={{0,12},{4,8},{8,4},{12,0},{16,28},{20,24},{24,20},{28,16},{32,44},... | collective-permute-start | bytes 3145736 | tf_op jit(solution)/shard_map/ppermute | solution.py:68
  206.4 40.8 %collective-permute-start.24 = (bf16[768,1792]{1,0:T(8,128)(2,1)}, bf16[768,1792]{1,0:T(8,128)(2,1)}, u32[]{:S(2)}, u32[]{:S(2)}) collective-permute-start(bf16[768,1792]{1,0:T(8,128)(2,1)} %all-gather.4.cloned.1.call-done), channel_id=1, source_target_pairs={{0,64},{64,0},{1,65},{65,1},{2,66},{66,2},{3,67},{67,3},{4,68},{68... | collective-permute-start | bytes 8257544 | tf_op jit(solution)/shard_map/ppermute | solution.py:202
  240.3 60.2 %collective-permute-start.31 = (bf16[768,3072]{1,0:T(8,128)(2,1)}, bf16[768,3072]{1,0:T(8,128)(2,1)}, u32[]{:S(2)}, u32[]{:S(2)}) collective-permute-start(bf16[768,3072]{1,0:T(8,128)(2,1)} %all-gather.6.cloned.1.call-done), channel_id=1, source_target_pairs={{0,64},{64,0},{1,65},{65,1},{2,66},{66,2},{3,67},{67,3},{4,68},{68... | collective-permute-start | bytes 14155784 | tf_op jit(solution)/shard_map/ppermute | solution.py:203
  252.5 25.0 %collective-permute-start.25 = (bf16[128,1536]{1,0:T(8,128)(2,1)}, bf16[128,1536]{1,0:T(8,128)(2,1)S(1)}, u32[]{:S(2)}, u32[]{:S(2)}) collective-permute-start(bf16[128,1536]{1,0:T(8,128)(2,1)} %get-tuple-element.33), channel_id=1, source_target_pairs={{0,2},{1,3},{2,0},{3,1},{4,6},{5,7},{6,4},{7,5},{8,10},{9,11},{10,... | collective-permute-start | bytes 1179656 | tf_op jit(solution)/shard_map/ppermute | solution.py:268
  254.9 22.6 %collective-permute-start.26 = (bf16[128,1536]{1,0:T(8,128)(2,1)}, bf16[128,1536]{1,0:T(8,128)(2,1)}, u32[]{:S(2)}, u32[]{:S(2)}) collective-permute-start(bf16[128,1536]{1,0:T(8,128)(2,1)} %get-tuple-element.34), channel_id=1, source_target_pairs={{0,1},{1,2},{2,3},{3,0},{4,5},{5,6},{6,7},{7,4},{8,9},{9,10},{10,1... | collective-permute-start | bytes 1179656 | tf_op jit(solution)/shard_map/ppermute | solution.py:268
  255.7 21.9 %collective-permute-start.27 = (bf16[128,1536]{1,0:T(8,128)(2,1)}, bf16[128,1536]{1,0:T(8,128)(2,1)}, u32[]{:S(2)}, u32[]{:S(2)}) collective-permute-start(bf16[128,1536]{1,0:T(8,128)(2,1)} %get-tuple-element.35), channel_id=1, source_target_pairs={{0,3},{1,0},{2,1},{3,2},{4,7},{5,4},{6,5},{7,6},{8,11},{9,8},{10,9... | collective-permute-start | bytes 1179656 | tf_op jit(solution)/shard_map/ppermute | solution.py:268
  (49 other events, 419.8 us)
Sparse Core Ops, SparseCore 0:
  10.2 56.5 all-gather.3
  68.9 74.8 all-gather.5

commit v2 on v1

v2 whole, which is shorter than its diff:
```python
import functools

import jax
import jax.numpy as jnp
import numpy as np
from jax import lax
from jax.experimental import pallas as pl
from jax.experimental.pallas import tpu as pltpu
from jax.sharding import PartitionSpec as P

D = 7168
QL = 1536
CAP = 20
HOLD = 16
SLOTS = HOLD * CAP
SIDE = 4
RING = 16
ROUTE_SCALE = 2.5
EPSILON = 1e-06
STEP = 4.0
VMEM = 60 << 20

ORDERS = ("PQpq", "QpqP", "pqPQ", "qPQp")
GROUPS = 2
EVEN = (1, 0, 3, 2)
ODD = (3, 2, 1, 0)


def partner(kind, place):
    slow, fast = divmod(place, SIDE)
    if kind == "P":
        slow = EVEN[slow]
    elif kind == "Q":
        slow = ODD[slow]
    elif kind == "p":
        fast = EVEN[fast]
    else:
        fast = ODD[fast]
    return slow * SIDE + fast


def order_of(group, half):
    return ORDERS[2 * group + half]


def keep(order, step, place):
    if step == 4:
        return [place]
    return keep(order, step + 1, partner(order[step], place)) + keep(order, step + 1, place)


def owner_table():
    return np.array(
        [[[keep(order_of(g, h), 0, e) for g in range(GROUPS)] for e in range(RING)] for h in range(2)],
        np.int32,
    )


def holder_table():
    return np.array(
        [
            [[e] + [partner(order_of(g, h)[0], e) for g in range(GROUPS)] for e in range(RING)]
            for h in range(2)
        ],
        np.int32,
    )


def gathered(place, steps):
    if not steps:
        return [place]
    return gathered(place, steps[:-1]) + gathered(partner(steps[-1], place), steps[:-1])


def spot_table():
    places = [gathered(e, ORDERS[0]) for e in range(RING)]
    owners = owner_table()
    return np.array(
        [
            [[[places[e].index(o) for o in owners[h, e, g]] for g in range(GROUPS)] for e in range(RING)]
            for h in range(2)
        ],
        np.int32,
    )


def swap(value, group, step):
    pairs = [
        (half * RING + e, half * RING + partner(order_of(group, half)[step], e))
        for half in range(2)
        for e in range(RING)
    ]
    return lax.ppermute(value, ("dp", "expert"), pairs)


RING_STEPS = ((EVEN, ODD), (ODD, EVEN))
QUARTERS = np.array([[0, 2, 3, 1], [0, 1, 2, 3]], np.int32)


def turn_to(value, step):
    pairs = [(h * 4 + y, h * 4 + RING_STEPS[h][step][y]) for h in range(2) for y in range(4)]
    return lax.ppermute(value, ("dp", "tensor"), pairs)


def relay_kernel(move_ref, x_ref, first_ref, second_ref, keep_ref):
    for b in range(x_ref.shape[0] // RING):
        rows = slice(b * RING, (b + 1) * RING)
        block = x_ref[rows].reshape(RING * RING, x_ref.shape[2])
        moved = jnp.dot(move_ref[...], block, preferred_element_type=jnp.float32).astype(jnp.bfloat16)
        moved = moved.reshape(RING, RING, x_ref.shape[2])
        first_ref[:, rows] = moved[0:4]
        second_ref[:, rows] = moved[4:8]
        keep_ref[:, rows] = moved[8:16]


def relay(slots, move, group):
    width = slots.shape[2] // GROUPS
    rows = SLOTS // 2
    out = lambda n: pl.BlockSpec((n, rows, width), lambda i: (0, i, 0))
    return pl.pallas_call(
        relay_kernel,
        grid=(SLOTS // rows,),
        in_specs=[
            pl.BlockSpec((RING * RING, RING * RING), lambda i: (0, 0)),
            pl.BlockSpec((rows, RING, width), lambda i: (i, 0, group)),
        ],
        out_specs=[out(4), out(4), out(8)],
        out_shape=[jax.ShapeDtypeStruct((n, SLOTS, width), jnp.bfloat16) for n in (4, 4, 8)],
        compiler_params=pltpu.CompilerParams(vmem_limit_bytes=VMEM),
        cost_estimate=pl.CostEstimate(
            flops=2 * RING * SLOTS * RING * RING * width,
            bytes_accessed=4 * RING * SLOTS * width,
            transcendentals=0,
        ),
        name="relay",
    )(move, slots)


def route_kernel(packed_ref, expert_ref, later_ref, out_ref):
    tokens = packed_ref.shape[2]
    rows = expert_ref.shape[0]
    experts = expert_ref[...]
    for i in range(packed_ref.shape[0]):
        table = packed_ref[i].astype(jnp.float32)
        levels = table[8:16]
        weight = ROUTE_SCALE * levels / jnp.sum(levels, axis=0, keepdims=True)
        named = jnp.zeros((rows, tokens), jnp.float32)
        weighed = jnp.zeros((rows, tokens), jnp.float32)
        for k in range(8):
            hit = experts == table[k : k + 1]
            named = jnp.where(hit, 1.0, named)
            weighed = jnp.where(hit, weight[k : k + 1], weighed)
        rank = jnp.dot(named.astype(jnp.bfloat16), later_ref[...], preferred_element_type=jnp.float32)
        out_ref[i] = jnp.concatenate([weighed, rank], axis=0).T.astype(jnp.bfloat16)


def route(packed, experts, later, tokens):
    rows = experts.shape[0]
    count = 8
    return pl.pallas_call(
        route_kernel,
        grid=(RING // count,),
        in_specs=[
            pl.BlockSpec((count, 16, tokens), lambda i: (i, 0, 0)),
            pl.BlockSpec((rows, tokens), lambda i: (0, 0)),
            pl.BlockSpec((tokens, tokens), lambda i: (0, 0)),
        ],
        out_specs=pl.BlockSpec((count, tokens, 2 * rows), lambda i: (i, 0, 0)),
        out_shape=jax.ShapeDtypeStruct((RING, tokens, 2 * rows), jnp.bfloat16),
        compiler_params=pltpu.CompilerParams(vmem_limit_bytes=VMEM),
        cost_estimate=pl.CostEstimate(
            flops=RING * 2 * tokens * tokens * 256, bytes_accessed=RING * tokens * 256, transcendentals=0
        ),
        name="route",
    )(packed, experts, later)


def combine_kernel(spot_ref, route_ref, spread_ref, turn_ref, mine_ref, theirs_ref, *rest, outs):
    rows = rest[-1]
    rows[0:SLOTS] = mine_ref[0]
    rows[SLOTS : 2 * SLOTS] = theirs_ref[0]
    level = jnp.dot(route_ref[0], spread_ref[...], preferred_element_type=jnp.float32) - turn_ref[0:1, :]
    matrix = jnp.where(jnp.abs(level - 1.25) < 1.5, level, 0.0).astype(jnp.bfloat16)
    value = jnp.dot(matrix, rows[...], preferred_element_type=jnp.float32)
    if len(rest) > 1 + outs:
        value += wide(rest[0][0])
    value = value.astype(jnp.bfloat16)
    if outs == 1:
        rest[-2][0] = value
    else:
        for i in range(outs):

            @pl.when(pl.program_id(0) == i)
            def _():
                rest[i - 1 - outs][...] = value


def combine(spots, routes, spread, turn, mine, theirs, first, count, tokens, more=()):
    width = mine.shape[2]
    lanes = routes.shape[2]
    outs = count if more else 1
    if more:
        out_specs = [pl.BlockSpec((tokens, width), lambda i, o: (0, 0))] * count
        out_shape = [jax.ShapeDtypeStruct((tokens, width), jnp.bfloat16)] * count
    else:
        out_specs = pl.BlockSpec((1, tokens, width), lambda i, o: (i, 0, 0))
        out_shape = jax.ShapeDtypeStruct((count, tokens, width), jnp.bfloat16)
    return pl.pallas_call(
        functools.partial(combine_kernel, outs=outs),
        grid_spec=pltpu.PrefetchScalarGridSpec(
            num_scalar_prefetch=1,
            grid=(count,),
            in_specs=[
                pl.BlockSpec((1, tokens, lanes), lambda i, o: (o[8 + first + i], 0, 0)),
                pl.BlockSpec((lanes, 2 * SLOTS), lambda i, o: (0, 0)),
                pl.BlockSpec((8, 2 * SLOTS), lambda i, o: (0, 0)),
                pl.BlockSpec((1, SLOTS, width), lambda i, o: (first + i, 0, 0)),
                pl.BlockSpec((1, SLOTS, width), lambda i, o: (first % 4 + i, 0, 0)),
            ]
            + [pl.BlockSpec((1, tokens, width), lambda i, o: (i, 0, 0))] * len(more),
            out_specs=out_specs,
            scratch_shapes=[pltpu.VMEM((2 * SLOTS, width), jnp.bfloat16)],
        ),
        out_shape=out_shape,
        compiler_params=pltpu.CompilerParams(vmem_limit_bytes=VMEM),
        cost_estimate=pl.CostEstimate(
            flops=count * 2 * tokens * 2 * SLOTS * (width + 256),
            bytes_accessed=count * (tokens * width + 2 * SLOTS * width + tokens * lanes) * 2,
            transcendentals=0,
        ),
        name="combine",
    )(spots, routes, spread, turn, mine, theirs, *more)


def add_kernel(left_ref, right_ref, out_ref):
    out_ref[...] = (wide(left_ref[...]) + wide(right_ref[...])).astype(jnp.bfloat16)


def add(left, right):
    rows, width = left.shape
    block = pl.BlockSpec((rows // 2, width), lambda i: (i, 0))
    return pl.pallas_call(
        add_kernel,
        grid=(2,),
        in_specs=[block, block],
        out_specs=block,
        out_shape=jax.ShapeDtypeStruct(left.shape, jnp.bfloat16),
        compiler_params=pltpu.CompilerParams(vmem_limit_bytes=VMEM),
        cost_estimate=pl.CostEstimate(flops=rows * width, bytes_accessed=6 * rows * width, transcendentals=0),
        name="add",
    )(left, right)


def wide(value):
    return value.astype(jnp.float32)


def with_squares(values, squares):
    high = squares.astype(jnp.bfloat16)
    low = (squares - wide(high)).astype(jnp.bfloat16)
    lane = lax.broadcasted_iota(jnp.int32, (squares.shape[0], 128), 1)
    pieces = jnp.where(lane == 0, wide(high), jnp.where(lane == 1, wide(low), 0.0))
    return jnp.concatenate([values.astype(jnp.bfloat16), pieces.astype(jnp.bfloat16)], axis=1)


def finish_kernel(half_ref, base_ref, left_ref, right_ref, gain_ref, down_ref, *rest):
    stream_ref, latent_ref, scaled = rest[-3:]
    width = left_ref.shape[1]
    step = pl.program_id(0)
    block = down_ref.shape[0]

    @pl.when(step == 0)
    def _():
        left = (base_ref[:, :width] + wide(left_ref[...])).astype(jnp.bfloat16)
        right = (base_ref[:, width:] + wide(right_ref[...])).astype(jnp.bfloat16)
        stream = jnp.concatenate([left, right], axis=1)
        stream_ref[...] = stream
        stream = wide(stream)
        scaled[...] = (stream * gain_ref[...]).astype(jnp.bfloat16)
        squares = jnp.sum(stream * stream, axis=1, keepdims=True)
        nothing = jnp.zeros((squares.shape[0], 128), jnp.float32)
        latent_ref[:, QL:] = with_squares(nothing, squares)[:, 128:]

    value = lax.dot_general(
        scaled[...], down_ref[...], (((1,), (1,)), ((), ())), preferred_element_type=jnp.float32
    )
    latent_ref[:, pl.ds(pl.multiple_of(step * block, block), block)] = value.astype(jnp.bfloat16)


def finish(half, base, left, right, gain, down, stream=None):
    tokens, columns = base.shape
    count = tokens // 2
    block = QL // 2
    part = lambda width: pl.BlockSpec((count, width), lambda n, h: (h[0], 0))
    in_specs = [
        part(columns),
        part(columns // 2),
        part(columns // 2),
        pl.BlockSpec((1, columns), lambda n, h: (0, 0)),
        pl.BlockSpec((block, columns), lambda n, h: (n, 0)),
    ]
    args = [half, base, left, right, gain, down]
    aliases = {}
    if stream is not None:
        in_specs.append(pl.BlockSpec(memory_space=pl.ANY))
        aliases = {len(args): 0}
        args.append(stream)
    return pl.pallas_call(
        finish_kernel,
        grid_spec=pltpu.PrefetchScalarGridSpec(
            num_scalar_prefetch=1,
            grid=(QL // block,),
            in_specs=in_specs,
            out_specs=[part(columns), pl.BlockSpec((count, QL + 128), lambda n, h: (0, 0))],
            scratch_shapes=[pltpu.VMEM((count, columns), jnp.bfloat16)],
        ),
        out_shape=[
            jax.ShapeDtypeStruct((tokens, columns), jnp.bfloat16),
            jax.ShapeDtypeStruct((count, QL + 128), jnp.bfloat16),
        ],
        input_output_aliases=aliases,
        compiler_params=pltpu.CompilerParams(vmem_limit_bytes=VMEM),
        cost_estimate=pl.CostEstimate(
            flops=2 * count * columns * QL, bytes_accessed=2 * columns * QL + 8 * count * columns, transcendentals=0
        ),
        name="finish",
    )(*args)


def fold_kernel(odd_ref, mine_ref, theirs_ref, send_ref, keep_ref):
    rows = send_ref.shape[0]

    def both(which):
        spot = pl.ds(pl.multiple_of(which * rows, rows), rows)
        value = wide(mine_ref[spot, :]) + wide(theirs_ref[spot, :])
        return value[:, :QL], value[:, QL : QL + 1] + value[:, QL + 1 : QL + 2]

    send_ref[...] = with_squares(*both(1 - odd_ref[0]))
    values, squares = both(odd_ref[0])
    keep_ref[:, :QL] = values
    keep_ref[:, QL:] = jnp.broadcast_to(squares, (rows, 128))


def fold(odd, mine, theirs):
    rows, lanes = mine.shape[0] // 2, mine.shape[1]
    whole = pl.BlockSpec(memory_space=pltpu.VMEM)
    return pl.pallas_call(
        fold_kernel,
        in_specs=[pl.BlockSpec(memory_space=pltpu.SMEM), whole, whole],
        out_specs=[whole, whole],
        out_shape=[
            jax.ShapeDtypeStruct((rows, lanes), jnp.bfloat16),
            jax.ShapeDtypeStruct((rows, lanes), jnp.float32),
        ],
        compiler_params=pltpu.CompilerParams(vmem_limit_bytes=VMEM),
        cost_estimate=pl.CostEstimate(flops=8 * rows * lanes, bytes_accessed=14 * rows * lanes, transcendentals=0),
        name="fold",
    )(odd, mine, theirs)


def compress_kernel(mine_ref, theirs_ref, gain_ref, out_ref):
    value = mine_ref[...]
    more = wide(theirs_ref[...])
    squares = value[:, QL : QL + 1] + more[:, QL : QL + 1] + more[:, QL + 1 : QL + 2]
    latent = (value[:, :QL] + more[:, :QL]) * lax.rsqrt(squares / D + EPSILON)
    scale = lax.rsqrt(jnp.sum(latent * latent, axis=1, keepdims=True) / QL + EPSILON)
    out_ref[...] = with_squares(latent * scale * gain_ref[...], squares)


def compress(mine, theirs, gain):
    whole = pl.BlockSpec(memory_space=pltpu.VMEM)
    rows, lanes = theirs.shape
    return pl.pallas_call(
        compress_kernel,
        in_specs=[whole, whole, whole],
        out_specs=whole,
        out_shape=jax.ShapeDtypeStruct(theirs.shape, jnp.bfloat16),
        compiler_params=pltpu.CompilerParams(vmem_limit_bytes=VMEM),
        cost_estimate=pl.CostEstimate(flops=8 * rows * lanes, bytes_accessed=8 * rows * lanes, transcendentals=rows),
        name="compress",
    )(mine, theirs, gain)


def lift_kernel(half_ref, x_ref, weight_ref, stream_ref, gain_ref, *rest):
    queries_ref, normed_ref = rest[-2:]

    @pl.when(pl.program_id(0) == 0)
    def _():
        squares = wide(x_ref[:, QL : QL + 1]) + wide(x_ref[:, QL + 1 : QL + 2])
        scale = lax.rsqrt(squares / D + EPSILON)
        normed_ref[...] = (wide(stream_ref[...]) * scale * gain_ref[...]).astype(jnp.bfloat16)

    value = jnp.dot(x_ref[:, :QL], weight_ref[...], preferred_element_type=jnp.float32)
    queries_ref[...] = value.astype(jnp.bfloat16)


def lift(half, x, weights, stream, gain, before=()):
    count, lanes = x.shape
    depth, columns = weights.shape
    tokens, width = stream.shape
    block = columns // 2
    row = pl.BlockSpec((count, width), lambda n, h: (h[0], 0))
    return pl.pallas_call(
        lift_kernel,
        grid_spec=pltpu.PrefetchScalarGridSpec(
            num_scalar_prefetch=1,
            grid=(columns // block,),
            in_specs=[
                pl.BlockSpec((count, lanes), lambda n, h: (0, 0)),
                pl.BlockSpec((depth, block), lambda n, h: (0, n)),
                row,
                pl.BlockSpec((1, width), lambda n, h: (0, 0)),
            ]
            + [pl.BlockSpec(memory_space=pl.ANY)] * len(before),
            out_specs=[pl.BlockSpec((count, block), lambda n, h: (h[0], n)), row],
        ),
        out_shape=[
            jax.ShapeDtypeStruct((tokens, columns), jnp.bfloat16),
            jax.ShapeDtypeStruct((tokens, width), jnp.bfloat16),
        ],
        input_output_aliases={5: 0, 6: 1} if before else {},
        compiler_params=pltpu.CompilerParams(vmem_limit_bytes=VMEM),
        cost_estimate=pl.CostEstimate(
            flops=2 * count * depth * columns,
            bytes_accessed=2 * depth * columns + 2 * count * columns,
            transcendentals=0,
        ),
        name="lift",
    )(half, x, weights, stream, gain, *before)


def shards(expert_out, expert_ids, gate_levels, residual, attn_gain, wq_a, latent_gain, wq_b):
    half = lax.axis_index("dp")
    place = lax.axis_index("expert")
    quarter = jnp.asarray(QUARTERS)[half, lax.axis_index("tensor")]
    upper, odd = quarter // 2, quarter % 2
    tokens = expert_ids.shape[0]
    columns = residual.shape[1]
    width = columns // GROUPS

    part = wq_b.shape[0] // 2

    def spread_out(value):
        return lax.all_gather(value, ("dp", "expert"), axis=0, tiled=True)

    down = spread_out(lax.dynamic_slice_in_dim(wq_a.T, half * part, part, 0))
    up_part = lax.dynamic_slice_in_dim(wq_b, half * part, part, 0)
    gain = latent_gain.reshape(RING, 2, part).transpose(1, 0, 2).reshape(1, QL)

    owners = jnp.asarray(owner_table())[half, place]
    spots = jnp.asarray(spot_table())[half, place]
    holders = jnp.asarray(holder_table())[half, place]
    experts = (holders[:, None] * HOLD + jnp.arange(HOLD, dtype=jnp.int32)[None, :]).reshape(-1)
    experts = jnp.concatenate([experts, jnp.full((64 - experts.shape[0],), -1, jnp.int32)])
    experts = jnp.broadcast_to(experts.astype(jnp.float32)[:, None], (64, tokens))

    spot = jnp.arange(RING * RING, dtype=jnp.int32)
    slots = expert_out.transpose(0, 2, 1, 3).reshape(SLOTS, RING, columns)
    relayed = []
    for g in range(GROUPS):
        source = (spot % RING) * RING + jnp.repeat(owners[g], RING)
        move = (source[:, None] == spot[None, :]).astype(jnp.bfloat16)
        relayed.append(relay(slots, move, g))
    packed = [jnp.concatenate([expert_ids.T, gate_levels.T], axis=0)]
    for i, kind in enumerate(ORDERS[0]):
        received = lax.ppermute(packed[-1], "expert", [(e, partner(kind, e)) for e in range(RING)])
        if i in (1, 2):
            received, _ = lax.optimization_barrier((received, relayed[i - 1][0]))
        packed.append(jnp.concatenate([packed[-1], received], axis=0))
    first = []
    for g in range(GROUPS):
        left, right, _ = lax.optimization_barrier((relayed[g][0], relayed[g][1], packed[2 * g + 2]))
        first.append([swap(left, g, 0), swap(right, g, 0)])

    position = jnp.arange(tokens, dtype=jnp.int32)
    later = (position[:, None] < position[None, :]).astype(jnp.bfloat16)
    routes = route(packed[-1].reshape(RING, 16, tokens), experts, later, tokens)
    slot = np.arange(SLOTS)
    turn = np.broadcast_to(STEP * np.tile(slot % CAP, 2)[None, :], (8, 2 * SLOTS))
    turn = jnp.asarray(turn.astype(np.float32))
    lanes = np.arange(64)[:, None]
    spread = []
    for g in range(GROUPS):
        expert = (slot // CAP)[None, :]
        hit = np.concatenate([lanes == expert, lanes == expert + HOLD * (g + 1)], axis=1)
        spread.append(jnp.asarray(np.concatenate([hit, STEP * hit], axis=0).astype(np.float32)).astype(jnp.bfloat16))

    def summed(g, start, more=()):
        received = first[g][start // 4]
        return combine(spots[g], routes, spread[g], turn, relayed[g][2], received, start, 2, tokens, more)

    groups = range(GROUPS)
    passed = [[summed(g, 2 * i) for g in groups] for i in range(2)]
    second_a = [swap(passed[0][g], g, 1) for g in groups]
    second_b = [swap(passed[1][g], g, 1) for g in groups]
    kept_a = [summed(g, 4, (second_a[g],)) for g in groups]
    third_a = [swap(kept_a[g][0], g, 2) for g in groups]
    third_b = [swap(kept_a[g][1], g, 2) for g in groups]
    kept_b = [summed(g, 6, (second_b[g],)) for g in groups]
    last = [add(kept_b[g][0], third_a[g]) for g in groups]
    fourth = [swap(last[g], g, 3) for g in groups]
    up_part, *_ = lax.optimization_barrier((up_part, *last))
    up = spread_out(up_part)
    base = jnp.concatenate(
        [
            wide(residual[:, g * width : (g + 1) * width])
            + wide(kept_b[g][1])
            + wide(third_b[g])
            for g in range(GROUPS)
        ],
        axis=1,
    )

    here = upper.reshape(1)
    there = 1 - here
    wide_gain = attn_gain.reshape(1, columns)
    stream, latent_there = finish(there, base, *fourth, wide_gain, down)
    latent_theirs = turn_to(latent_there, 0)
    stream, latent_here = finish(here, base, *fourth, wide_gain, down, stream)
    latent_send, latent_keep = fold(odd.reshape(1), latent_here, latent_theirs)
    normed_mine = compress(latent_keep, turn_to(latent_send, 1), gain)
    normed_theirs = turn_to(normed_mine, 1)
    half_here = jnp.where(
        odd == 0,
        jnp.concatenate([normed_mine, normed_theirs], axis=0),
        jnp.concatenate([normed_theirs, normed_mine], axis=0),
    )
    half_there = turn_to(half_here, 0)
    queries, normed = lift(here, half_here, up, stream, wide_gain)
    queries, normed = lift(there, half_there, up, stream, wide_gain, (queries, normed))
    return (stream, normed, queries)


def solution(mesh):
    return jax.shard_map(
        shards,
        mesh=mesh,
        in_specs=(
            P(("dp", "expert"), None, None, "tensor"),
            P(("dp", "expert"), None),
            P(("dp", "expert"), None),
            P(("dp", "expert"), "tensor"),
            P("tensor"),
            P("tensor", "expert"),
            P(),
            P("expert", "tensor"),
        ),
        out_specs=(
            P(("dp", "expert"), "tensor"),
            P(("dp", "expert"), "tensor"),
            P(("dp", "expert"), "tensor"),
        ),
        check_vma=False,
    )
```

time: 317 us -> 289 us (0.912)
  waiting for transfers between devices: 28.2 us -> 118 us
  blocking collectives: 58.5 us -> 0 us
  starting transfers between devices: 57.3 us -> 25 us
  other arithmetic: 26.9 us -> 10.2 us
  matrix products: 13.7 us -> 0 us
    ppermute x24 -> x14, waiting for transfers between devices: 12.2 us -> 82.1 us  [swap(): return lax.ppermute(value, ('dp', 'expert'), pairs)]
    all_gather x1 -> x0, blocking collectives: 38.9 us -> none  [shards(): packed = lax.all_gather(packed, 'expert', axis=0)]
    ppermute x24 -> x14, starting transfers between devices: 31.7 us -> 10.3 us  [swap(): return lax.ppermute(value, ('dp', 'expert'), pairs)]
    ppermute x8, waiting for transfers between devices: 16 us -> 36.3 us  [the longest x4 30.3 us: turn_to(): return lax.ppermute(value, ('dp', 'tensor'), pairs)]
    psum x1 -> x0, blocking collectives: 19.7 us -> none  [shards(): squares = lax.psum(jnp.sum(stream_wide * stream_wide, axis=1), 'tensor')]
    dot_general x4 -> x0, matrix products: 13.7 us -> none  [the longest x2 5.05 us: shards(): lax.dot_general(scaled, weights, over_rows, preferred_element_type=jnp.fl...]
    convert_element_type x11 -> x4, other arithmetic: 13.5 us -> 2.35 us  [the longest x2 1.51 us: shards(): move = (source[:, None] == spot[None, :]).astype(jnp.bfloat16)]
    ppermute x8, starting transfers between devices: 25.6 us -> 14.6 us  [the longest x4 8.64 us: shards(): lax.ppermute(packed[-1], 'expert', [(e, partner(kind, e)) for e in range(...]
  transfers between devices with their start and end apart: 34 -> 24, of which waited for: 6 -> 12; matrix products, arithmetic and copies ran while one was open for 11% -> 6% of each run, Pallas kernels for 32% -> 33%
where the time goes in v2:
time: 289 us; the launch traced here: 288 us
  waiting for transfers between devices  118 us (41%)
  Pallas kernels  103 us (36%)
  starting transfers between devices  25 us (9%)
  between operations  16.9 us (6%)
  local copies, waits for them, and re-layouts  14.5 us (5%)
  other arithmetic  10.2 us (4%)
    ppermute x14, waiting for transfers between devices, swap(): return lax.ppermute(value, ('dp', 'expert'), pairs)  82.1 us
    pallas_call x8, Pallas kernels, combine(): pl.pallas_call(functools.partial(combine_kernel, outs=outs), grid_spec=pl...  47 us
    ppermute x4, waiting for transfers between devices, turn_to(): return lax.ppermute(value, ('dp', 'tensor'), pairs)  30.3 us
    pallas_call x2, Pallas kernels, relay(): pl.pallas_call(relay_kernel, grid=(SLOTS // rows,), in_specs=[pl.BlockSpe...  15.2 us
    pallas_call x2, Pallas kernels, lift(): pl.pallas_call(lift_kernel, grid_spec=pltpu.PrefetchScalarGridSpec(num_sc...  13.9 us
    pallas_call x2, Pallas kernels, finish(): pl.pallas_call(finish_kernel, grid_spec=pltpu.PrefetchScalarGridSpec(num_...  12.6 us
    ppermute x14, starting transfers between devices, swap(): return lax.ppermute(value, ('dp', 'expert'), pairs)  10.3 us
    ppermute x4, starting transfers between devices, shards(): lax.ppermute(packed[-1], 'expert', [(e, partner(kind, e)) for e in range(...  8.64 us
  transfers between devices with their start and end apart: 24, of which 12 were waited for; matrix products, arithmetic and copies ran while one was open for 6% of the time, Pallas kernels for 33%

profile of v2, /device:TPU:1, one launch (start us, length us, event | category | flops | bytes accessed | tf_op | source)
XLA Modules:
  0.0 288.3 jit_solution(10516424411153381470)
XLA Ops:
  16.2 7.6 %relay.2 = (bf16[4,320,896]{2,1,0:T(8,128)(2,1)}, bf16[4,320,896]{2,1,0:T(8,128)(2,1)}, bf16[8,320,896]{2,1,0:T(8,128)(2,1)}) custom-call(bf16[256,256]{1,0:T(8,128)(2,1)} %fusion.1.move_ref, bf16[320,16,1792]{2,1,0:T(8,128)(2,1)} %bitcast.26), custom_call_target="tpu_custom_call" | custom-call | flops 2348810240 | bytes 18350080 | tf_op jit(solution)/shard_map/relay/pallas_call | solution.py:120
  26.1 7.6 %relay.3 = (bf16[4,320,896]{2,1,0:T(8,128)(2,1)}, bf16[4,320,896]{2,1,0:T(8,128)(2,1)}, bf16[8,320,896]{2,1,0:T(8,128)(2,1)}) custom-call(bf16[256,256]{1,0:T(8,128)(2,1)} %fusion.2.move_ref, bf16[320,16,1792]{2,1,0:T(8,128)(2,1)} %bitcast.27), custom_call_target="tpu_custom_call" | custom-call | flops 2348810240 | bytes 18350080 | tf_op jit(solution)/shard_map/relay/pallas_call | solution.py:120
  40.7 3.5 %collective-permute-done.3 = s32[128,512]{1,0:T(8,128)S(1)} collective-permute-done((s32[128,512]{1,0:T(8,128)S(1)}, s32[128,512]{1,0:T(8,128)S(1)}, u32[]{:S(2)}, u32[]{:S(2)}) %collective-permute-start.3) | collective-permute-done | bytes 262176 | tf_op jit(solution)/shard_map/ppermute | solution.py:466
  52.5 4.9 %route.1.route_ref = bf16[16,512,128]{2,1,0:T(8,128)(2,1)} custom-call(s32[16,16,512]{2,1,0:T(8,128)} %bitcast.35, f32[64,512]{1,0:T(8,128)} %broadcast_in_dim.8.expert_ref, bf16[512,512]{1,0:T(8,128)(2,1)} %fusion.later_ref), custom_call_target="tpu_custom_call" | custom-call | flops 2147483648 | bytes 2097152 | tf_op jit(solution)/shard_map/route/pallas_call | solution.py:160
  57.4 22.4 %collective-permute-done.5.theirs_ref = bf16[4,320,896]{2,1,0:T(8,128)(2,1)} collective-permute-done((bf16[4,320,896]{2,1,0:T(8,128)(2,1)}, bf16[4,320,896]{2,1,0:T(8,128)(2,1)}, u32[]{:S(2)}, u32[]{:S(2)}) %collective-permute-start.5) | collective-permute-done | bytes 2293792 | tf_op jit(solution)/shard_map/ppermute | solution.py:93
  79.8 5.5 %combine.10 = bf16[2,512,896]{2,1,0:T(8,128)(2,1)} custom-call(s32[16]{0:T(128)} %get-tuple-element.77.spot_ref, bf16[16,512,128]{2,1,0:T(8,128)(2,1)} %route.1.route_ref, bf16[128,640]{1,0:T(8,128)(2,1)} %constant.93.spread_ref, f32[8,640]{1,0:T(8,128)} %constant.87.clone.turn_ref, bf16[8,320,896]{2,1,0:T(8,128)(2,1)} %get-tuple-element.38.mine_ref, ...), custom_call_target="tpu_custom_call" | custom-call | flops 1509949440 | bytes 4390912 | tf_op jit(solution)/shard_map/combine/pallas_call | solution.py:208
  85.3 5.5 %combine.14 = bf16[2,512,896]{2,1,0:T(8,128)(2,1)} custom-call(s32[16]{0:T(128)} %get-tuple-element.78.spot_ref, bf16[16,512,128]{2,1,0:T(8,128)(2,1)} %route.1.route_ref, bf16[128,640]{1,0:T(8,128)(2,1)} %constant.94.spread_ref, f32[8,640]{1,0:T(8,128)} %constant.87.clone.turn_ref, bf16[8,320,896]{2,1,0:T(8,128)(2,1)} %get-tuple-element.44.mine_ref, ...), custom_call_target="tpu_custom_call" | custom-call | flops 1509949440 | bytes 4390912 | tf_op jit(solution)/shard_map/combine/pallas_call | solution.py:208
  90.8 5.5 %combine.8 = bf16[2,512,896]{2,1,0:T(8,128)(2,1)} custom-call(s32[16]{0:T(128)} %get-tuple-element.77.spot_ref, bf16[16,512,128]{2,1,0:T(8,128)(2,1)} %route.1.route_ref, bf16[128,640]{1,0:T(8,128)(2,1)} %constant.93.spread_ref, f32[8,640]{1,0:T(8,128)} %constant.87.clone.turn_ref, bf16[8,320,896]{2,1,0:T(8,128)(2,1)} %get-tuple-element.38.mine_ref, ...), custom_call_target="tpu_custom_call" | custom-call | flops 1509949440 | bytes 4390912 | tf_op jit(solution)/shard_map/combine/pallas_call | solution.py:208
  97.7 5.5 %combine.12 = bf16[2,512,896]{2,1,0:T(8,128)(2,1)} custom-call(s32[16]{0:T(128)} %get-tuple-element.78.spot_ref, bf16[16,512,128]{2,1,0:T(8,128)(2,1)} %route.1.route_ref, bf16[128,640]{1,0:T(8,128)(2,1)} %constant.94.spread_ref, f32[8,640]{1,0:T(8,128)} %constant.87.clone.turn_ref, bf16[8,320,896]{2,1,0:T(8,128)(2,1)} %get-tuple-element.44.mine_ref, ...), custom_call_target="tpu_custom_call" | custom-call | flops 1509949440 | bytes 4390912 | tf_op jit(solution)/shard_map/combine/pallas_call | solution.py:208
  103.2 13.6 %collective-permute-done.4.theirs_ref = bf16[4,320,896]{2,1,0:T(8,128)(2,1)S(1)} collective-permute-done((bf16[4,320,896]{2,1,0:T(8,128)(2,1)}, bf16[4,320,896]{2,1,0:T(8,128)(2,1)S(1)}, u32[]{:S(2)}, u32[]{:S(2)}) %collective-permute-start.4) | collective-permute-done | bytes 2293792 | tf_op jit(solution)/shard_map/ppermute | solution.py:93
  116.9 10.8 %collective-permute-done.7.rest_0_ = bf16[2,512,896]{2,1,0:T(8,128)(2,1)} collective-permute-done((bf16[2,512,896]{2,1,0:T(8,128)(2,1)}, bf16[2,512,896]{2,1,0:T(8,128)(2,1)}, u32[]{:S(2)}, u32[]{:S(2)}) %collective-permute-start.7) | collective-permute-done | bytes 1835040 | tf_op jit(solution)/shard_map/ppermute | solution.py:93
  127.7 6.3 %combine.11 = (bf16[512,896]{1,0:T(8,128)(2,1)}, bf16[512,896]{1,0:T(8,128)(2,1)}) custom-call(s32[16]{0:T(128)} %get-tuple-element.77.spot_ref, bf16[16,512,128]{2,1,0:T(8,128)(2,1)} %route.1.route_ref, bf16[128,640]{1,0:T(8,128)(2,1)} %constant.93.spread_ref, f32[8,640]{1,0:T(8,128)} %constant.87.clone.turn_ref, ...), custom_call_target="tpu_custom_call" | custom-call | flops 1509949440 | bytes 4390912 | tf_op jit(solution)/shard_map/combine/pallas_call | solution.py:208
  134.2 6.2 %combine.15 = (bf16[512,896]{1,0:T(8,128)(2,1)}, bf16[512,896]{1,0:T(8,128)(2,1)}) custom-call(s32[16]{0:T(128)} %get-tuple-element.78.spot_ref, bf16[16,512,128]{2,1,0:T(8,128)(2,1)} %route.1.route_ref, bf16[128,640]{1,0:T(8,128)(2,1)} %constant.94.spread_ref, f32[8,640]{1,0:T(8,128)} %constant.87.clone.turn_ref, ...), custom_call_target="tpu_custom_call" | custom-call | flops 1509949440 | bytes 4390912 | tf_op jit(solution)/shard_map/combine/pallas_call | solution.py:208
  142.2 16.5 %collective-permute-done.6.rest_0_ = bf16[2,512,896]{2,1,0:T(8,128)(2,1)} collective-permute-done((bf16[2,512,896]{2,1,0:T(8,128)(2,1)}, bf16[2,512,896]{2,1,0:T(8,128)(2,1)}, u32[]{:S(2)}, u32[]{:S(2)}) %collective-permute-start.6) | collective-permute-done | bytes 1835040 | tf_op jit(solution)/shard_map/ppermute | solution.py:93
  158.7 6.3 %combine.9 = (bf16[512,896]{1,0:T(8,128)(2,1)}, bf16[512,896]{1,0:T(8,128)(2,1)}) custom-call(s32[16]{0:T(128)} %get-tuple-element.77.spot_ref, bf16[16,512,128]{2,1,0:T(8,128)(2,1)} %route.1.route_ref, bf16[128,640]{1,0:T(8,128)(2,1)} %constant.93.spread_ref, f32[8,640]{1,0:T(8,128)} %constant.87.clone.turn_ref, ...), custom_call_target="tpu_custom_call" | custom-call | flops 1509949440 | bytes 4390912 | tf_op jit(solution)/shard_map/combine/pallas_call | solution.py:208
  165.0 6.3 %combine.13 = (bf16[512,896]{1,0:T(8,128)(2,1)}, bf16[512,896]{1,0:T(8,128)(2,1)}) custom-call(s32[16]{0:T(128)} %get-tuple-element.78.spot_ref, bf16[16,512,128]{2,1,0:T(8,128)(2,1)} %route.1.route_ref, bf16[128,640]{1,0:T(8,128)(2,1)} %constant.94.spread_ref, f32[8,640]{1,0:T(8,128)} %constant.87.clone.turn_ref, ...), custom_call_target="tpu_custom_call" | custom-call | flops 1509949440 | bytes 4390912 | tf_op jit(solution)/shard_map/combine/pallas_call | solution.py:208
  183.9 17.0 %collective-permute-done.8 = bf16[512,896]{1,0:T(8,128)(2,1)} collective-permute-done((bf16[512,896]{1,0:T(8,128)(2,1)}, bf16[512,896]{1,0:T(8,128)(2,1)}, u32[]{:S(2)}, u32[]{:S(2)}) %collective-permute-start.8) | collective-permute-done | bytes 917536 | tf_op jit(solution)/shard_map/ppermute | solution.py:93
  209.0 6.5 %finish.2 = (bf16[512,1792]{1,0:T(8,128)(2,1)}, bf16[256,1664]{1,0:T(8,128)(2,1)}) custom-call(s32[1]{0:T(128)S(6)} %sub.8.half_ref, f32[512,1792]{1,0:T(8,128)} %pad_maximum_fusion.base_ref, bf16[512,896]{1,0:T(8,128)(2,1)} %copy-done.3, bf16[512,896]{1,0:T(8,128)(2,1)} %copy-done.4, f32[1,1792]{1,0:T(1,128)} %reshape.82.gain_ref, ...), custom_call_target="tpu_custom_call" | custom-call | flops 1409286144 | bytes 9175040 | tf_op jit(solution)/shard_map/finish/pallas_call | solution.py:308
  218.2 6.0 %finish.3 = (bf16[512,1792]{1,0:T(8,128)(2,1)}, bf16[256,1664]{1,0:T(8,128)(2,1)}) custom-call(s32[1]{0:T(128)} %bitcast.1.half_ref, f32[512,1792]{1,0:T(8,128)} %pad_maximum_fusion.base_ref, bf16[512,896]{1,0:T(8,128)(2,1)} %copy-done.3, bf16[512,896]{1,0:T(8,128)(2,1)} %copy-done.4, f32[1,1792]{1,0:T(1,128)} %reshape.82.gain_ref, ...), custom_call_target="tpu_custom_call", output_to_operand_aliasing={{0}: (6, {})} | custom-call | flops 1409286144 | bytes 9175040 | tf_op jit(solution)/shard_map/finish/pallas_call | solution.py:308
  224.3 8.8 %collective-permute-done.18.theirs_ref = bf16[256,1664]{1,0:T(8,128)(2,1)S(1)} collective-permute-done((bf16[256,1664]{1,0:T(8,128)(2,1)}, bf16[256,1664]{1,0:T(8,128)(2,1)S(1)}, u32[]{:S(2)}, u32[]{:S(2)}) %collective-permute-start.18) | collective-permute-done | bytes 852000 | tf_op jit(solution)/shard_map/ppermute | solution.py:102
  237.9 6.3 %collective-permute-done.19.theirs_ref = bf16[128,1664]{1,0:T(8,128)(2,1)S(1)} collective-permute-done((bf16[128,1664]{1,0:T(8,128)(2,1)}, bf16[128,1664]{1,0:T(8,128)(2,1)S(1)}, u32[]{:S(2)}, u32[]{:S(2)}) %collective-permute-start.19) | collective-permute-done | bytes 426016 | tf_op jit(solution)/shard_map/ppermute | solution.py:102
  247.5 11.9 %collective-permute-done.20 = bf16[128,1664]{1,0:T(8,128)(2,1)S(1)} collective-permute-done((bf16[128,1664]{1,0:T(8,128)(2,1)}, bf16[128,1664]{1,0:T(8,128)(2,1)S(1)}, u32[]{:S(2)}, u32[]{:S(2)}) %collective-permute-start.20) | collective-permute-done | bytes 426016 | tf_op jit(solution)/shard_map/ppermute | solution.py:102
  263.6 6.9 %lift.2 = (bf16[512,3072]{1,0:T(8,128)(2,1)}, bf16[512,1792]{1,0:T(8,128)(2,1)}) custom-call(s32[1]{0:T(128)} %bitcast.1.half_ref, bf16[256,1664]{1,0:T(8,128)(2,1)} %copy-done.5, bf16[1536,3072]{1,0:T(8,128)(2,1)} %all-gather.5.cloned.1.call-done.weight_ref, bf16[512,1792]{1,0:T(8,128)(2,1)} %get-tuple-element.31.stream_ref, f32[1,1792]{1,0:T(1,128)} %reshape.82.gain_ref), custom_call_target="tpu_custom_call" | custom-call | flops 2415919104 | bytes 11010048 | tf_op jit(solution)/shard_map/lift/pallas_call | solution.py:403
  274.6 6.9 %lift.3 = (bf16[512,3072]{1,0:T(8,128)(2,1)}, bf16[512,1792]{1,0:T(8,128)(2,1)}) custom-call(s32[1]{0:T(128)S(6)} %sub.8.half_ref, bf16[256,1664]{1,0:T(8,128)(2,1)} %copy-done.10, bf16[1536,3072]{1,0:T(8,128)(2,1)} %all-gather.5.cloned.1.call-done.weight_ref, ...), custom_call_target="tpu_custom_call", output_to_operand_aliasing={{0}: (5, {}), {1}: (6, {})} | custom-call | flops 2415919104 | bytes 11010048 | tf_op jit(solution)/shard_map/lift/pallas_call | solution.py:403
  (117 shorter events, 67.2 us)
Async XLA Ops:
  7.2 200.6 %all-gather.3.cloned.1.call-start = ((), (), s32[]{:S(2)}) async-start(), calls=%async_computation | async-start | bytes 5677056 | tf_op jit(solution)/shard_map/all_gather | solution.py:444
  8.9 254.7 %all-gather.5.cloned.1.call-start = ((), (), s32[]{:S(2)}) async-start(), calls=%async_computation.1 | async-start | bytes 9732096 | tf_op jit(solution)/shard_map/all_gather | solution.py:444
  9.7 14.0 %collective-permute-start = (s32[16,512]{1,0:T(8,128)S(1)}, s32[16,512]{1,0:T(8,128)S(1)}, u32[]{:S(2)}, u32[]{:S(2)}) collective-permute-start(s32[16,512]{1,0:T(8,128)S(1)} %pad_add_fusion.2), channel_id=1, source_target_pairs={{0,16},{4,20},{8,24},{12,28},{16,0},{20,4},{24,8},{28,12},{32,48},... | collective-permute-start | bytes 98312 | tf_op jit(solution)/shard_map/ppermute | solution.py:466
  23.8 10.0 %collective-permute-start.1 = (s32[32,512]{1,0:T(8,128)S(1)}, s32[32,512]{1,0:T(8,128)S(1)}, u32[]{:S(2)}, u32[]{:S(2)}) collective-permute-start(s32[32,512]{1,0:T(8,128)S(1)} %pad_add_fusion.1), channel_id=1, source_target_pairs={{0,48},{4,52},{8,56},{12,60},{16,32},{20,36},{24,40},{28,44},{32,1... | collective-permute-start | bytes 196616 | tf_op jit(solution)/shard_map/ppermute | solution.py:466
  33.7 3.9 %collective-permute-start.2 = (s32[64,512]{1,0:T(8,128)S(1)}, s32[64,512]{1,0:T(8,128)S(1)}, u32[]{:S(2)}, u32[]{:S(2)}) collective-permute-start(s32[64,512]{1,0:T(8,128)S(1)} %pad_add_fusion), channel_id=1, source_target_pairs={{0,4},{4,0},{8,12},{12,8},{16,20},{20,16},{24,28},{28,24},{32,36},... | collective-permute-start | bytes 393224 | tf_op jit(solution)/shard_map/ppermute | solution.py:466
  37.7 6.5 %collective-permute-start.3 = (s32[128,512]{1,0:T(8,128)S(1)}, s32[128,512]{1,0:T(8,128)S(1)}, u32[]{:S(2)}, u32[]{:S(2)}) collective-permute-start(s32[128,512]{1,0:T(8,128)S(1)} %get-tuple-element.67), channel_id=1, source_target_pairs={{0,12},{4,8},{8,4},{12,0},{16,28},{20,24},{24,20},{28,16},{32,44},... | collective-permute-start | bytes 786440 | tf_op jit(solution)/shard_map/ppermute | solution.py:466
  40.2 39.6 %collective-permute-start.5 = (bf16[4,320,896]{2,1,0:T(8,128)(2,1)}, bf16[4,320,896]{2,1,0:T(8,128)(2,1)}, u32[]{:S(2)}, u32[]{:S(2)}) collective-permute-start(bf16[4,320,896]{2,1,0:T(8,128)(2,1)} %get-tuple-element.41), channel_id=1, source_target_pairs={{0,16},{4,20},{8,24},{12,28},{16,0},{20,4},{24,8},{28,12},{32,48},... | collective-permute-start | bytes 6881288 | tf_op jit(solution)/shard_map/ppermute | solution.py:93
  44.2 41.1 %collective-permute-start.10 = (bf16[4,320,896]{2,1,0:T(8,128)(2,1)}, bf16[4,320,896]{2,1,0:T(8,128)(2,1)}, u32[]{:S(2)}, u32[]{:S(2)}) collective-permute-start(bf16[4,320,896]{2,1,0:T(8,128)(2,1)} %get-tuple-element.47), channel_id=1, source_target_pairs={{0,4},{4,0},{8,12},{12,8},{16,20},{20,16},{24,28},{28,24},{32,36},... | collective-permute-start | bytes 6881288 | tf_op jit(solution)/shard_map/ppermute | solution.py:93
  46.8 69.9 %collective-permute-start.4 = (bf16[4,320,896]{2,1,0:T(8,128)(2,1)}, bf16[4,320,896]{2,1,0:T(8,128)(2,1)S(1)}, u32[]{:S(2)}, u32[]{:S(2)}) collective-permute-start(bf16[4,320,896]{2,1,0:T(8,128)(2,1)} %get-tuple-element.40), channel_id=1, source_target_pairs={{0,16},{4,20},{8,24},{12,28},{16,0},{20,4},{24,8},{28,12},{32,48},... | collective-permute-start | bytes 6881288 | tf_op jit(solution)/shard_map/ppermute | solution.py:93
  50.2 84.0 %collective-permute-start.9 = (bf16[4,320,896]{2,1,0:T(8,128)(2,1)}, bf16[4,320,896]{2,1,0:T(8,128)(2,1)}, u32[]{:S(2)}, u32[]{:S(2)}) collective-permute-start(bf16[4,320,896]{2,1,0:T(8,128)(2,1)} %get-tuple-element.46), channel_id=1, source_target_pairs={{0,4},{4,0},{8,12},{12,8},{16,20},{20,16},{24,28},{28,24},{32,36},... | collective-permute-start | bytes 6881288 | tf_op jit(solution)/shard_map/ppermute | solution.py:93
  85.3 42.4 %collective-permute-start.7 = (bf16[2,512,896]{2,1,0:T(8,128)(2,1)}, bf16[2,512,896]{2,1,0:T(8,128)(2,1)}, u32[]{:S(2)}, u32[]{:S(2)}) collective-permute-start(bf16[2,512,896]{2,1,0:T(8,128)(2,1)} %combine.10), channel_id=1, source_target_pairs={{0,48},{4,52},{8,56},{12,60},{16,32},{20,36},{24,40},{28,44},{32,1... | collective-permute-start | bytes 5505032 | tf_op jit(solution)/shard_map/ppermute | solution.py:93
  90.8 43.4 %collective-permute-start.12 = (bf16[2,512,896]{2,1,0:T(8,128)(2,1)}, bf16[2,512,896]{2,1,0:T(8,128)(2,1)}, u32[]{:S(2)}, u32[]{:S(2)}) collective-permute-start(bf16[2,512,896]{2,1,0:T(8,128)(2,1)} %combine.14), channel_id=1, source_target_pairs={{0,12},{4,8},{8,4},{12,0},{16,28},{20,24},{24,20},{28,16},{32,44},... | collective-permute-start | bytes 5505032 | tf_op jit(solution)/shard_map/ppermute | solution.py:93
  96.2 62.4 %collective-permute-start.6 = (bf16[2,512,896]{2,1,0:T(8,128)(2,1)}, bf16[2,512,896]{2,1,0:T(8,128)(2,1)}, u32[]{:S(2)}, u32[]{:S(2)}) collective-permute-start(bf16[2,512,896]{2,1,0:T(8,128)(2,1)} %combine.8), channel_id=1, source_target_pairs={{0,48},{4,52},{8,56},{12,60},{16,32},{20,36},{24,40},{28,44},{32,1... | collective-permute-start | bytes 5505032 | tf_op jit(solution)/shard_map/ppermute | solution.py:93
  116.7 48.3 %collective-permute-start.11 = (bf16[2,512,896]{2,1,0:T(8,128)(2,1)}, bf16[2,512,896]{2,1,0:T(8,128)(2,1)}, u32[]{:S(2)}, u32[]{:S(2)}) collective-permute-start(bf16[2,512,896]{2,1,0:T(8,128)(2,1)} %combine.12), channel_id=1, source_target_pairs={{0,12},{4,8},{8,4},{12,0},{16,28},{20,24},{24,20},{28,16},{32,44},... | collective-permute-start | bytes 5505032 | tf_op jit(solution)/shard_map/ppermute | solution.py:93
  134.0 37.3 %collective-permute-start.14 = (bf16[512,896]{1,0:T(8,128)(2,1)}, bf16[512,896]{1,0:T(8,128)(2,1)S(1)}, u32[]{:S(2)}, u32[]{:S(2)}) collective-permute-start(bf16[512,896]{1,0:T(8,128)(2,1)} %get-tuple-element.51), channel_id=1, source_target_pairs={{0,4},{4,0},{8,12},{12,8},{16,20},{20,16},{24,28},{28,24},{32,36},... | collective-permute-start | bytes 2752520 | tf_op jit(solution)/shard_map/ppermute | solution.py:93
  140.4 34.1 %collective-permute-start.16 = (bf16[512,896]{1,0:T(8,128)(2,1)}, bf16[512,896]{1,0:T(8,128)(2,1)S(1)}, u32[]{:S(2)}, u32[]{:S(2)}) collective-permute-start(bf16[512,896]{1,0:T(8,128)(2,1)} %get-tuple-element.53), channel_id=1, source_target_pairs={{0,16},{4,20},{8,24},{12,28},{16,0},{20,4},{24,8},{28,12},{32,48},... | collective-permute-start | bytes 2752520 | tf_op jit(solution)/shard_map/ppermute | solution.py:93
  177.8 23.1 %collective-permute-start.8 = (bf16[512,896]{1,0:T(8,128)(2,1)}, bf16[512,896]{1,0:T(8,128)(2,1)}, u32[]{:S(2)}, u32[]{:S(2)}) collective-permute-start(bf16[512,896]{1,0:T(8,128)(2,1)} %get-tuple-element.43), channel_id=1, source_target_pairs={{0,4},{4,0},{8,12},{12,8},{16,20},{20,16},{24,28},{28,24},{32,36},... | collective-permute-start | bytes 2752520 | tf_op jit(solution)/shard_map/ppermute | solution.py:93
  180.1 22.7 %collective-permute-start.13 = (bf16[512,896]{1,0:T(8,128)(2,1)}, bf16[512,896]{1,0:T(8,128)(2,1)}, u32[]{:S(2)}, u32[]{:S(2)}) collective-permute-start(bf16[512,896]{1,0:T(8,128)(2,1)} %get-tuple-element.49), channel_id=1, source_target_pairs={{0,16},{4,20},{8,24},{12,28},{16,0},{20,4},{24,8},{28,12},{32,48},... | collective-permute-start | bytes 2752520 | tf_op jit(solution)/shard_map/ppermute | solution.py:93
  180.1 27.7 %collective-permute-start.15 = (bf16[512,896]{1,0:T(8,128)(2,1)}, bf16[512,896]{1,0:T(8,128)(2,1)S(1)}, u32[]{:S(2)}, u32[]{:S(2)}) collective-permute-start(bf16[512,896]{1,0:T(8,128)(2,1)} %add.131), channel_id=1, source_target_pairs={{0,12},{4,8},{8,4},{12,0},{16,28},{20,24},{24,20},{28,16},{32,44},... | collective-permute-start | bytes 2752520 | tf_op jit(solution)/shard_map/ppermute | solution.py:93
  180.1 27.7 %collective-permute-start.17 = (bf16[512,896]{1,0:T(8,128)(2,1)}, bf16[512,896]{1,0:T(8,128)(2,1)S(1)}, u32[]{:S(2)}, u32[]{:S(2)}) collective-permute-start(bf16[512,896]{1,0:T(8,128)(2,1)} %add.132), channel_id=1, source_target_pairs={{0,48},{4,52},{8,56},{12,60},{16,32},{20,36},{24,40},{28,44},{32,1... | collective-permute-start | bytes 2752520 | tf_op jit(solution)/shard_map/ppermute | solution.py:93
  215.5 17.6 %collective-permute-start.18 = (bf16[256,1664]{1,0:T(8,128)(2,1)}, bf16[256,1664]{1,0:T(8,128)(2,1)S(1)}, u32[]{:S(2)}, u32[]{:S(2)}) collective-permute-start(bf16[256,1664]{1,0:T(8,128)(2,1)} %get-tuple-element.57), channel_id=1, source_target_pairs={{0,1},{1,0},{2,3},{3,2},{64,67},{65,66},{66,65},{67,64},{4,5},{5,4... | collective-permute-start | bytes 2555912 | tf_op jit(solution)/shard_map/ppermute | solution.py:102
  236.8 7.5 %collective-permute-start.19 = (bf16[128,1664]{1,0:T(8,128)(2,1)}, bf16[128,1664]{1,0:T(8,128)(2,1)S(1)}, u32[]{:S(2)}, u32[]{:S(2)}) collective-permute-start(bf16[128,1664]{1,0:T(8,128)(2,1)} %get-tuple-element.59), channel_id=1, source_target_pairs={{0,3},{1,2},{2,1},{3,0},{64,65},{65,64},{66,67},{67,66},{4,7},{5,6... | collective-permute-start | bytes 1277960 | tf_op jit(solution)/shard_map/ppermute | solution.py:102
  247.4 12.0 %collective-permute-start.20 = (bf16[128,1664]{1,0:T(8,128)(2,1)}, bf16[128,1664]{1,0:T(8,128)(2,1)S(1)}, u32[]{:S(2)}, u32[]{:S(2)}) collective-permute-start(bf16[128,1664]{1,0:T(8,128)(2,1)} %compress.1), channel_id=1, source_target_pairs={{0,3},{1,2},{2,1},{3,0},{64,65},{65,64},{66,67},{67,66},{4,7},{5,6... | collective-permute-start | bytes 1277960 | tf_op jit(solution)/shard_map/ppermute | solution.py:102
  260.8 12.8 %collective-permute-start.21 = (bf16[256,1664]{1,0:T(8,128)(2,1)S(1)}, bf16[256,1664]{1,0:T(8,128)(2,1)S(1)}, u32[]{:S(2)}, u32[]{:S(2)}) collective-permute-start(bf16[256,1664]{1,0:T(8,128)(2,1)S(1)} %maximum_select_fusion.x_ref), channel_id=1, source_target_pairs={{0,1},{1,0},{2,3},{3,2},{64,67},{65,66},{66,65},{67,64},{4,5},{5,4... | collective-permute-start | bytes 2555912 | tf_op jit(solution)/shard_map/ppermute | solution.py:102
  (18 other events, 246.6 us)
Sparse Core Ops, SparseCore 0:
  10.3 56.0 all-gather.2
  177.9 56.1 all-gather.4

commit v3 on v2

--- a/solution.py
+++ b/solution.py
@@ -94,7 +94,7 @@
 
 
 RING_STEPS = ((EVEN, ODD), (ODD, EVEN))
-QUARTERS = np.array([[0, 2, 3, 1], [0, 1, 2, 3]], np.int32)
+QUARTERS = np.array([[0, 2, 3, 1], [0, 1, 3, 2]], np.int32)
 
 
 def turn_to(value, step):
@@ -263,122 +263,95 @@
     return jnp.concatenate([values.astype(jnp.bfloat16), pieces.astype(jnp.bfloat16)], axis=1)
 
 
-def finish_kernel(half_ref, base_ref, left_ref, right_ref, gain_ref, down_ref, *rest):
-    stream_ref, latent_ref, scaled = rest[-3:]
+def finish_kernel(place_ref, base_ref, left_ref, right_ref, gain_ref, down_ref, stream_ref, *rest):
+    parts, scaled, sums = rest[:4], rest[4], rest[5]
     width = left_ref.shape[1]
+    rows = parts[0].shape[0]
     step = pl.program_id(0)
     block = down_ref.shape[0]
 
     @pl.when(step == 0)
     def _():
-        left = (base_ref[:, :width] + wide(left_ref[...])).astype(jnp.bfloat16)
-        right = (base_ref[:, width:] + wide(right_ref[...])).astype(jnp.bfloat16)
-        stream = jnp.concatenate([left, right], axis=1)
-        stream_ref[...] = stream
-        stream = wide(stream)
-        scaled[...] = (stream * gain_ref[...]).astype(jnp.bfloat16)
-        squares = jnp.sum(stream * stream, axis=1, keepdims=True)
-        nothing = jnp.zeros((squares.shape[0], 128), jnp.float32)
-        latent_ref[:, QL:] = with_squares(nothing, squares)[:, 128:]
+        for i in range(4):
+            here = slice(i * rows, (i + 1) * rows)
+            left = (base_ref[here, :width] + wide(left_ref[here])).astype(jnp.bfloat16)
+            right = (base_ref[here, width:] + wide(right_ref[here])).astype(jnp.bfloat16)
+            stream = jnp.concatenate([left, right], axis=1)
+            stream_ref[here] = stream
+            stream = wide(stream)
+            squares = jnp.sum(stream * stream, axis=1, keepdims=True)
+            nothing = jnp.zeros((rows, 128), jnp.float32)
+            rank = 2 * jnp.where(place_ref[0] == i // 2, 0, 1) + jnp.where(place_ref[1] == i % 2, 0, 1)
+            spot = pl.ds(pl.multiple_of(rank * rows, rows), rows)
+            scaled[spot, :] = (stream * gain_ref[...]).astype(jnp.bfloat16)
+            sums[spot, :] = with_squares(nothing, squares)[:, 128:]
+        for i in range(4):
+            parts[i][:, QL:] = sums[i * rows : (i + 1) * rows]
 
     value = lax.dot_general(
         scaled[...], down_ref[...], (((1,), (1,)), ((), ())), preferred_element_type=jnp.float32
-    )
-    latent_ref[:, pl.ds(pl.multiple_of(step * block, block), block)] = value.astype(jnp.bfloat16)
-
-
-def finish(half, base, left, right, gain, down, stream=None):
+    ).astype(jnp.bfloat16)
+    lanes = pl.ds(pl.multiple_of(step * block, block), block)
+    for i in range(4):
+        parts[i][:, lanes] = value[i * rows : (i + 1) * rows]
+
+
+def finish(place, base, left, right, gain, down):
     tokens, columns = base.shape
-    count = tokens // 2
-    block = QL // 2
-    part = lambda width: pl.BlockSpec((count, width), lambda n, h: (h[0], 0))
-    in_specs = [
-        part(columns),
-        part(columns // 2),
-        part(columns // 2),
-        pl.BlockSpec((1, columns), lambda n, h: (0, 0)),
-        pl.BlockSpec((block, columns), lambda n, h: (n, 0)),
-    ]
-    args = [half, base, left, right, gain, down]
-    aliases = {}
-    if stream is not None:
-        in_specs.append(pl.BlockSpec(memory_space=pl.ANY))
-        aliases = {len(args): 0}
-        args.append(stream)
+    rows = tokens // 4
+    block = QL // 3
+    whole = lambda *shape: pl.BlockSpec(shape, lambda n, p: (0, 0))
     return pl.pallas_call(
         finish_kernel,
         grid_spec=pltpu.PrefetchScalarGridSpec(
             num_scalar_prefetch=1,
             grid=(QL // block,),
-            in_specs=in_specs,
-            out_specs=[part(columns), pl.BlockSpec((count, QL + 128), lambda n, h: (0, 0))],
-            scratch_shapes=[pltpu.VMEM((count, columns), jnp.bfloat16)],
-        ),
-        out_shape=[
-            jax.ShapeDtypeStruct((tokens, columns), jnp.bfloat16),
-            jax.ShapeDtypeStruct((count, QL + 128), jnp.bfloat16),
-        ],
-        input_output_aliases=aliases,
+            in_specs=[
+                whole(tokens, columns),
+                whole(tokens, columns // 2),
+                whole(tokens, columns // 2),
+                whole(1, columns),
+                pl.BlockSpec((block, columns), lambda n, p: (n, 0)),
+            ],
+            out_specs=[whole(tokens, columns)] + [whole(rows, QL + 128)] * 4,
+            scratch_shapes=[
+                pltpu.VMEM((tokens, columns), jnp.bfloat16),
+                pltpu.VMEM((tokens, 128), jnp.bfloat16),
+            ],
+        ),
+        out_shape=[jax.ShapeDtypeStruct((tokens, columns), jnp.bfloat16)]
+        + [jax.ShapeDtypeStruct((rows, QL + 128), jnp.bfloat16)] * 4,
         compiler_params=pltpu.CompilerParams(vmem_limit_bytes=VMEM),
         cost_estimate=pl.CostEstimate(
-            flops=2 * count * columns * QL, bytes_accessed=2 * columns * QL + 8 * count * columns, transcendentals=0
+            flops=2 * tokens * columns * QL,
+            bytes_accessed=2 * columns * QL + 10 * tokens * columns,
+            transcendentals=0,
         ),
         name="finish",
-    )(*args)
-
-
-def fold_kernel(odd_ref, mine_ref, theirs_ref, send_ref, keep_ref):
-    rows = send_ref.shape[0]
-
-    def both(which):
-        spot = pl.ds(pl.multiple_of(which * rows, rows), rows)
-        value = wide(mine_ref[spot, :]) + wide(theirs_ref[spot, :])
-        return value[:, :QL], value[:, QL : QL + 1] + value[:, QL + 1 : QL + 2]
-
-    send_ref[...] = with_squares(*both(1 - odd_ref[0]))
-    values, squares = both(odd_ref[0])
-    keep_ref[:, :QL] = values
-    keep_ref[:, QL:] = jnp.broadcast_to(squares, (rows, 128))
-
-
-def fold(odd, mine, theirs):
-    rows, lanes = mine.shape[0] // 2, mine.shape[1]
-    whole = pl.BlockSpec(memory_space=pltpu.VMEM)
-    return pl.pallas_call(
-        fold_kernel,
-        in_specs=[pl.BlockSpec(memory_space=pltpu.SMEM), whole, whole],
-        out_specs=[whole, whole],
-        out_shape=[
-            jax.ShapeDtypeStruct((rows, lanes), jnp.bfloat16),
-            jax.ShapeDtypeStruct((rows, lanes), jnp.float32),
-        ],
-        compiler_params=pltpu.CompilerParams(vmem_limit_bytes=VMEM),
-        cost_estimate=pl.CostEstimate(flops=8 * rows * lanes, bytes_accessed=14 * rows * lanes, transcendentals=0),
-        name="fold",
-    )(odd, mine, theirs)
-
-
-def compress_kernel(mine_ref, theirs_ref, gain_ref, out_ref):
-    value = mine_ref[...]
-    more = wide(theirs_ref[...])
-    squares = value[:, QL : QL + 1] + more[:, QL : QL + 1] + more[:, QL + 1 : QL + 2]
-    latent = (value[:, :QL] + more[:, :QL]) * lax.rsqrt(squares / D + EPSILON)
+    )(place, base, left, right, gain, down)
+
+
+def compress_kernel(*refs):
+    gain_ref, out_ref = refs[-2:]
+    latent = sum(wide(ref[:, :QL]) for ref in refs[:-2])
+    squares = sum(wide(ref[:, QL : QL + 1]) + wide(ref[:, QL + 1 : QL + 2]) for ref in refs[:-2])
+    latent = latent * lax.rsqrt(squares / D + EPSILON)
     scale = lax.rsqrt(jnp.sum(latent * latent, axis=1, keepdims=True) / QL + EPSILON)
     out_ref[...] = with_squares(latent * scale * gain_ref[...], squares)
 
 
-def compress(mine, theirs, gain):
+def compress(parts, gain):
     whole = pl.BlockSpec(memory_space=pltpu.VMEM)
-    rows, lanes = theirs.shape
+    rows, lanes = parts[0].shape
     return pl.pallas_call(
         compress_kernel,
-        in_specs=[whole, whole, whole],
+        in_specs=[whole] * (len(parts) + 1),
         out_specs=whole,
-        out_shape=jax.ShapeDtypeStruct(theirs.shape, jnp.bfloat16),
-        compiler_params=pltpu.CompilerParams(vmem_limit_bytes=VMEM),
-        cost_estimate=pl.CostEstimate(flops=8 * rows * lanes, bytes_accessed=8 * rows * lanes, transcendentals=rows),
+        out_shape=jax.ShapeDtypeStruct((rows, lanes), jnp.bfloat16),
+        compiler_params=pltpu.CompilerParams(vmem_limit_bytes=VMEM),
+        cost_estimate=pl.CostEstimate(flops=8 * rows * lanes, bytes_accessed=10 * rows * lanes, transcendentals=rows),
         name="compress",
-    )(mine, theirs, gain)
+    )(*parts, gain)
 
 
 def lift_kernel(half_ref, x_ref, weight_ref, stream_ref, gain_ref, *rest):
@@ -454,21 +427,24 @@
     experts = jnp.concatenate([experts, jnp.full((64 - experts.shape[0],), -1, jnp.int32)])
     experts = jnp.broadcast_to(experts.astype(jnp.float32)[:, None], (64, tokens))
 
+    packed = [jnp.concatenate([expert_ids.T, gate_levels.T], axis=0)]
+
+    def double(kind, beside=()):
+        received = lax.ppermute(packed[-1], "expert", [(e, partner(kind, e)) for e in range(RING)])
+        received, *_ = lax.optimization_barrier((received, *beside))
+        packed.append(jnp.concatenate([packed[-1], received], axis=0))
+
+    double(ORDERS[0][0])
+    double(ORDERS[0][1])
     spot = jnp.arange(RING * RING, dtype=jnp.int32)
     slots = expert_out.transpose(0, 2, 1, 3).reshape(SLOTS, RING, columns)
-    relayed = []
+    relayed, first = [], []
     for g in range(GROUPS):
         source = (spot % RING) * RING + jnp.repeat(owners[g], RING)
         move = (source[:, None] == spot[None, :]).astype(jnp.bfloat16)
+        move, _ = lax.optimization_barrier((move, packed[2 + g]))
         relayed.append(relay(slots, move, g))
-    packed = [jnp.concatenate([expert_ids.T, gate_levels.T], axis=0)]
-    for i, kind in enumerate(ORDERS[0]):
-        received = lax.ppermute(packed[-1], "expert", [(e, partner(kind, e)) for e in range(RING)])
-        if i in (1, 2):
-            received, _ = lax.optimization_barrier((received, relayed[i - 1][0]))
-        packed.append(jnp.concatenate([packed[-1], received], axis=0))
-    first = []
-    for g in range(GROUPS):
+        double(ORDERS[0][2 + g], relayed[g][:1])
         left, right, _ = lax.optimization_barrier((relayed[g][0], relayed[g][1], packed[2 * g + 2]))
         first.append([swap(left, g, 0), swap(right, g, 0)])
 
@@ -497,7 +473,10 @@
     third_a = [swap(kept_a[g][0], g, 2) for g in groups]
     third_b = [swap(kept_a[g][1], g, 2) for g in groups]
     kept_b = [summed(g, 6, (second_b[g],)) for g in groups]
-    last = [add(kept_b[g][0], third_a[g]) for g in groups]
+    last = []
+    for g in groups:
+        arrived, _ = lax.optimization_barrier((third_a[g], third_b[g]))
+        last.append(add(kept_b[g][0], arrived))
     fourth = [swap(last[g], g, 3) for g in groups]
     up_part, *_ = lax.optimization_barrier((up_part, *last))
     up = spread_out(up_part)
@@ -514,11 +493,13 @@
     here = upper.reshape(1)
     there = 1 - here
     wide_gain = attn_gain.reshape(1, columns)
-    stream, latent_there = finish(there, base, *fourth, wide_gain, down)
-    latent_theirs = turn_to(latent_there, 0)
-    stream, latent_here = finish(here, base, *fourth, wide_gain, down, stream)
-    latent_send, latent_keep = fold(odd.reshape(1), latent_here, latent_theirs)
-    normed_mine = compress(latent_keep, turn_to(latent_send, 1), gain)
+    count = lax.axis_size("tensor")
+    across = [(y, (y + 2) % count) for y in range(count)]
+    place_here = jnp.stack([upper, odd])
+    stream, own, beside, near, far = finish(place_here, base, *fourth, wide_gain, down)
+    far = lax.ppermute(far, "tensor", across)
+    near = turn_to(near, 0)
+    normed_mine = compress((own, turn_to(beside, 1), near, far), gain)
     normed_theirs = turn_to(normed_mine, 1)
     half_here = jnp.where(
         odd == 0,

time: 289 us -> 265 us (0.917)
  waiting for transfers between devices: 118 us -> 97.2 us
  Pallas kernels: 103 us -> 98.2 us
  starting transfers between devices: 25 us -> 29.1 us
  local copies, waits for them, and re-layouts: 14.5 us -> 10.9 us
    ppermute x14, waiting for transfers between devices: 82.1 us -> 71.8 us  [swap(): return lax.ppermute(value, ('dp', 'expert'), pairs)]
    ppermute x4, waiting for transfers between devices: 30.3 us -> 23.3 us  [turn_to(): return lax.ppermute(value, ('dp', 'tensor'), pairs)]
    ppermute x4 -> x5, waiting for transfers between devices: 6.05 us -> 2.09 us  [the longest x4 2.09 us: double(): lax.ppermute(packed[-1], 'expert', [(e, partner(kind, e)) for e in range(...]
    ppermute x14, starting transfers between devices: 10.3 us -> 13.4 us  [swap(): return lax.ppermute(value, ('dp', 'expert'), pairs)]
    pallas_call x2 -> x1, Pallas kernels: 12.6 us -> 9.59 us  [finish(): pl.pallas_call(finish_kernel, grid_spec=pltpu.PrefetchScalarGridSpec(num_...]
    unnamed x40 -> x32, local copies, waits for them, and re-layouts: 7.08 us -> 4.23 us
    ppermute x4 -> x5, starting transfers between devices: 8.64 us -> 8.59 us  [the longest x4 7.86 us: double(): lax.ppermute(packed[-1], 'expert', [(e, partner(kind, e)) for e in range(...]
  transfers between devices with their start and end apart: 24 -> 25, of which waited for: 12 -> 12; matrix products, arithmetic and copies ran while one was open for 6% -> 7% of each run, Pallas kernels for 33% -> 35%
where the time goes in v3:
time: 265 us; the launch traced here: 264 us
  Pallas kernels  98.2 us (37%)
  waiting for transfers between devices  97.2 us (37%)
  starting transfers between devices  29.1 us (11%)
  between operations  16.8 us (6%)
  other arithmetic  11.8 us (4%)
  local copies, waits for them, and re-layouts  10.9 us (4%)
    ppermute x14, waiting for transfers between devices, swap(): return lax.ppermute(value, ('dp', 'expert'), pairs)  71.8 us
    pallas_call x8, Pallas kernels, combine(): pl.pallas_call(functools.partial(combine_kernel, outs=outs), grid_spec=pl...  47.1 us
    ppermute x4, waiting for transfers between devices, turn_to(): return lax.ppermute(value, ('dp', 'tensor'), pairs)  23.3 us
    pallas_call x2, Pallas kernels, relay(): pl.pallas_call(relay_kernel, grid=(SLOTS // rows,), in_specs=[pl.BlockSpe...  15.2 us
    pallas_call x2, Pallas kernels, lift(): pl.pallas_call(lift_kernel, grid_spec=pltpu.PrefetchScalarGridSpec(num_sc...  13.9 us
    ppermute x14, starting transfers between devices, swap(): return lax.ppermute(value, ('dp', 'expert'), pairs)  13.4 us
    pallas_call x1, Pallas kernels, finish(): pl.pallas_call(finish_kernel, grid_spec=pltpu.PrefetchScalarGridSpec(num_...  9.59 us
    ppermute x4, starting transfers between devices, double(): lax.ppermute(packed[-1], 'expert', [(e, partner(kind, e)) for e in range(...  7.86 us
  transfers between devices with their start and end apart: 25, of which 12 were waited for; matrix products, arithmetic and copies ran while one was open for 7% of the time, Pallas kernels for 35%

profile of v3, /device:TPU:1, one launch (start us, length us, event | category | flops | bytes accessed | tf_op | source)
XLA Modules:
  0.0 264.1 jit_solution(12335420230333498039)
XLA Ops:
  22.5 7.7 %relay.2 = (bf16[4,320,896]{2,1,0:T(8,128)(2,1)}, bf16[4,320,896]{2,1,0:T(8,128)(2,1)}, bf16[8,320,896]{2,1,0:T(8,128)(2,1)}) custom-call(bf16[256,256]{1,0:T(8,128)(2,1)} %fusion.1.move_ref, bf16[320,16,1792]{2,1,0:T(8,128)(2,1)} %bitcast.26), custom_call_target="tpu_custom_call" | custom-call | flops 2348810240 | bytes 18350080 | tf_op jit(solution)/shard_map/relay/pallas_call | solution.py:120
  35.0 7.6 %relay.3 = (bf16[4,320,896]{2,1,0:T(8,128)(2,1)}, bf16[4,320,896]{2,1,0:T(8,128)(2,1)}, bf16[8,320,896]{2,1,0:T(8,128)(2,1)}) custom-call(bf16[256,256]{1,0:T(8,128)(2,1)} %fusion.2.move_ref, bf16[320,16,1792]{2,1,0:T(8,128)(2,1)} %bitcast.27), custom_call_target="tpu_custom_call" | custom-call | flops 2348810240 | bytes 18350080 | tf_op jit(solution)/shard_map/relay/pallas_call | solution.py:120
  48.8 4.9 %route.1.route_ref = bf16[16,512,128]{2,1,0:T(8,128)(2,1)} custom-call(s32[16,16,512]{2,1,0:T(8,128)} %bitcast.35, f32[64,512]{1,0:T(8,128)} %broadcast_in_dim.8.expert_ref, bf16[512,512]{1,0:T(8,128)(2,1)} %fusion.later_ref), custom_call_target="tpu_custom_call" | custom-call | flops 2147483648 | bytes 2097152 | tf_op jit(solution)/shard_map/route/pallas_call | solution.py:160
  53.7 18.7 %collective-permute-done.5.theirs_ref = bf16[4,320,896]{2,1,0:T(8,128)(2,1)} collective-permute-done((bf16[4,320,896]{2,1,0:T(8,128)(2,1)}, bf16[4,320,896]{2,1,0:T(8,128)(2,1)}, u32[]{:S(2)}, u32[]{:S(2)}) %collective-permute-start.5) | collective-permute-done | bytes 2293792 | tf_op jit(solution)/shard_map/ppermute | solution.py:93
  72.4 5.5 %combine.10 = bf16[2,512,896]{2,1,0:T(8,128)(2,1)} custom-call(s32[16]{0:T(128)} %get-tuple-element.83.spot_ref, bf16[16,512,128]{2,1,0:T(8,128)(2,1)} %route.1.route_ref, bf16[128,640]{1,0:T(8,128)(2,1)} %constant.93.spread_ref, f32[8,640]{1,0:T(8,128)} %constant.87.clone.turn_ref, bf16[8,320,896]{2,1,0:T(8,128)(2,1)} %get-tuple-element.43.mine_ref, ...), custom_call_target="tpu_custom_call" | custom-call | flops 1509949440 | bytes 4390912 | tf_op jit(solution)/shard_map/combine/pallas_call | solution.py:208
  78.2 4.1 %collective-permute-done.10.theirs_ref = bf16[4,320,896]{2,1,0:T(8,128)(2,1)} collective-permute-done((bf16[4,320,896]{2,1,0:T(8,128)(2,1)}, bf16[4,320,896]{2,1,0:T(8,128)(2,1)}, u32[]{:S(2)}, u32[]{:S(2)}) %collective-permute-start.10) | collective-permute-done | bytes 2293792 | tf_op jit(solution)/shard_map/ppermute | solution.py:93
  82.3 5.5 %combine.14 = bf16[2,512,896]{2,1,0:T(8,128)(2,1)} custom-call(s32[16]{0:T(128)} %get-tuple-element.84.spot_ref, bf16[16,512,128]{2,1,0:T(8,128)(2,1)} %route.1.route_ref, bf16[128,640]{1,0:T(8,128)(2,1)} %constant.94.spread_ref, f32[8,640]{1,0:T(8,128)} %constant.87.clone.turn_ref, bf16[8,320,896]{2,1,0:T(8,128)(2,1)} %get-tuple-element.49.mine_ref, ...), custom_call_target="tpu_custom_call" | custom-call | flops 1509949440 | bytes 4390912 | tf_op jit(solution)/shard_map/combine/pallas_call | solution.py:208
  87.8 5.5 %combine.8 = bf16[2,512,896]{2,1,0:T(8,128)(2,1)} custom-call(s32[16]{0:T(128)} %get-tuple-element.83.spot_ref, bf16[16,512,128]{2,1,0:T(8,128)(2,1)} %route.1.route_ref, bf16[128,640]{1,0:T(8,128)(2,1)} %constant.93.spread_ref, f32[8,640]{1,0:T(8,128)} %constant.87.clone.turn_ref, bf16[8,320,896]{2,1,0:T(8,128)(2,1)} %get-tuple-element.43.mine_ref, ...), custom_call_target="tpu_custom_call" | custom-call | flops 1509949440 | bytes 4390912 | tf_op jit(solution)/shard_map/combine/pallas_call | solution.py:208
  93.3 5.5 %combine.12 = bf16[2,512,896]{2,1,0:T(8,128)(2,1)} custom-call(s32[16]{0:T(128)} %get-tuple-element.84.spot_ref, bf16[16,512,128]{2,1,0:T(8,128)(2,1)} %route.1.route_ref, bf16[128,640]{1,0:T(8,128)(2,1)} %constant.94.spread_ref, f32[8,640]{1,0:T(8,128)} %constant.87.clone.turn_ref, bf16[8,320,896]{2,1,0:T(8,128)(2,1)} %get-tuple-element.49.mine_ref, ...), custom_call_target="tpu_custom_call" | custom-call | flops 1509949440 | bytes 4390912 | tf_op jit(solution)/shard_map/combine/pallas_call | solution.py:208
  98.7 10.6 %collective-permute-done.4.theirs_ref = bf16[4,320,896]{2,1,0:T(8,128)(2,1)S(1)} collective-permute-done((bf16[4,320,896]{2,1,0:T(8,128)(2,1)}, bf16[4,320,896]{2,1,0:T(8,128)(2,1)S(1)}, u32[]{:S(2)}, u32[]{:S(2)}) %collective-permute-start.4) | collective-permute-done | bytes 2293792 | tf_op jit(solution)/shard_map/ppermute | solution.py:93
  109.4 10.8 %collective-permute-done.7.rest_0_ = bf16[2,512,896]{2,1,0:T(8,128)(2,1)} collective-permute-done((bf16[2,512,896]{2,1,0:T(8,128)(2,1)}, bf16[2,512,896]{2,1,0:T(8,128)(2,1)}, u32[]{:S(2)}, u32[]{:S(2)}) %collective-permute-start.7) | collective-permute-done | bytes 1835040 | tf_op jit(solution)/shard_map/ppermute | solution.py:93
  120.3 6.3 %combine.11 = (bf16[512,896]{1,0:T(8,128)(2,1)}, bf16[512,896]{1,0:T(8,128)(2,1)}) custom-call(s32[16]{0:T(128)} %get-tuple-element.83.spot_ref, bf16[16,512,128]{2,1,0:T(8,128)(2,1)} %route.1.route_ref, bf16[128,640]{1,0:T(8,128)(2,1)} %constant.93.spread_ref, f32[8,640]{1,0:T(8,128)} %constant.87.clone.turn_ref, ...), custom_call_target="tpu_custom_call" | custom-call | flops 1509949440 | bytes 4390912 | tf_op jit(solution)/shard_map/combine/pallas_call | solution.py:208
  129.3 6.3 %combine.15 = (bf16[512,896]{1,0:T(8,128)(2,1)}, bf16[512,896]{1,0:T(8,128)(2,1)}) custom-call(s32[16]{0:T(128)} %get-tuple-element.84.spot_ref, bf16[16,512,128]{2,1,0:T(8,128)(2,1)} %route.1.route_ref, bf16[128,640]{1,0:T(8,128)(2,1)} %constant.94.spread_ref, f32[8,640]{1,0:T(8,128)} %constant.87.clone.turn_ref, ...), custom_call_target="tpu_custom_call" | custom-call | flops 1509949440 | bytes 4390912 | tf_op jit(solution)/shard_map/combine/pallas_call | solution.py:208
  137.8 21.8 %collective-permute-done.6.rest_0_ = bf16[2,512,896]{2,1,0:T(8,128)(2,1)} collective-permute-done((bf16[2,512,896]{2,1,0:T(8,128)(2,1)}, bf16[2,512,896]{2,1,0:T(8,128)(2,1)}, u32[]{:S(2)}, u32[]{:S(2)}) %collective-permute-start.6) | collective-permute-done | bytes 1835040 | tf_op jit(solution)/shard_map/ppermute | solution.py:93
  162.6 6.3 %combine.9 = (bf16[512,896]{1,0:T(8,128)(2,1)}, bf16[512,896]{1,0:T(8,128)(2,1)}) custom-call(s32[16]{0:T(128)} %get-tuple-element.83.spot_ref, bf16[16,512,128]{2,1,0:T(8,128)(2,1)} %route.1.route_ref, bf16[128,640]{1,0:T(8,128)(2,1)} %constant.93.spread_ref, f32[8,640]{1,0:T(8,128)} %constant.87.clone.turn_ref, ...), custom_call_target="tpu_custom_call" | custom-call | flops 1509949440 | bytes 4390912 | tf_op jit(solution)/shard_map/combine/pallas_call | solution.py:208
  168.8 6.3 %combine.13 = (bf16[512,896]{1,0:T(8,128)(2,1)}, bf16[512,896]{1,0:T(8,128)(2,1)}) custom-call(s32[16]{0:T(128)} %get-tuple-element.84.spot_ref, bf16[16,512,128]{2,1,0:T(8,128)(2,1)} %route.1.route_ref, bf16[128,640]{1,0:T(8,128)(2,1)} %constant.94.spread_ref, f32[8,640]{1,0:T(8,128)} %constant.87.clone.turn_ref, ...), custom_call_target="tpu_custom_call" | custom-call | flops 1509949440 | bytes 4390912 | tf_op jit(solution)/shard_map/combine/pallas_call | solution.py:208
  190.3 5.3 %collective-permute-done.15.left_ref = bf16[512,896]{1,0:T(8,128)(2,1)} collective-permute-done((bf16[512,896]{1,0:T(8,128)(2,1)}, bf16[512,896]{1,0:T(8,128)(2,1)}, u32[]{:S(2)}, u32[]{:S(2)}) %collective-permute-start.15) | collective-permute-done | bytes 917536 | tf_op jit(solution)/shard_map/ppermute | solution.py:93
  196.0 9.6 %finish.1 = (bf16[512,1792]{1,0:T(8,128)(2,1)}, bf16[128,1664]{1,0:T(8,128)(2,1)}, bf16[128,1664]{1,0:T(8,128)(2,1)}, bf16[128,1664]{1,0:T(8,128)(2,1)}, bf16[128,1664]{1,0:T(8,128)(2,1)}) custom-call(s32[2]{0:T(128)} %pad_add_fusion.3.place_ref, f32[512,1792]{1,0:T(8,128)} %pad_maximum_fusion.base_ref, bf16[512,896]{1,0:T(8,128)(2,1)} %collective-permute-done.15.left_ref, ...), custom_call_target="tpu_custom_call" | custom-call | flops 2818572288 | bytes 14680064 | tf_op jit(solution)/shard_map/finish/pallas_call | solution.py:304
  210.6 7.2 %collective-permute-done.18.refs_1_ = bf16[128,1664]{1,0:T(8,128)(2,1)S(1)} collective-permute-done((bf16[128,1664]{1,0:T(8,128)(2,1)}, bf16[128,1664]{1,0:T(8,128)(2,1)S(1)}, u32[]{:S(2)}, u32[]{:S(2)}) %collective-permute-start.18) | collective-permute-done | bytes 426016 | tf_op jit(solution)/shard_map/ppermute | solution.py:102
  217.8 5.8 %collective-permute-done.19.refs_2_ = bf16[128,1664]{1,0:T(8,128)(2,1)S(1)} collective-permute-done((bf16[128,1664]{1,0:T(8,128)(2,1)}, bf16[128,1664]{1,0:T(8,128)(2,1)S(1)}, u32[]{:S(2)}, u32[]{:S(2)}) %collective-permute-start.19) | collective-permute-done | bytes 426016 | tf_op jit(solution)/shard_map/ppermute | solution.py:102
  227.2 7.2 %collective-permute-done.21 = bf16[128,1664]{1,0:T(8,128)(2,1)S(1)} collective-permute-done((bf16[128,1664]{1,0:T(8,128)(2,1)}, bf16[128,1664]{1,0:T(8,128)(2,1)S(1)}, u32[]{:S(2)}, u32[]{:S(2)}) %collective-permute-start.21) | collective-permute-done | bytes 426016 | tf_op jit(solution)/shard_map/ppermute | solution.py:102
  235.8 3.5 %collective-permute-start.22 = (bf16[256,1664]{1,0:T(8,128)(2,1)S(1)}, bf16[256,1664]{1,0:T(8,128)(2,1)S(1)}, u32[]{:S(2)}, u32[]{:S(2)}) collective-permute-start(bf16[256,1664]{1,0:T(8,128)(2,1)S(1)} %maximum_select_fusion.x_ref), channel_id=1, source_target_pairs={{0,1},{1,0},{2,3},{3,2},{64,67},{65,66},{66,65},{67,64},{4,5},{5,4... | collective-permute-start | bytes 2555912 | tf_op jit(solution)/shard_map/ppermute | solution.py:102
  239.3 7.0 %lift.2 = (bf16[512,3072]{1,0:T(8,128)(2,1)}, bf16[512,1792]{1,0:T(8,128)(2,1)}) custom-call(s32[1]{0:T(128)} %bitcast.1.half_ref, bf16[256,1664]{1,0:T(8,128)(2,1)} %copy-done.3, bf16[1536,3072]{1,0:T(8,128)(2,1)} %all-gather.5.cloned.1.call-done.weight_ref, bf16[512,1792]{1,0:T(8,128)(2,1)} %get-tuple-element.34.stream_ref, f32[1,1792]{1,0:T(1,128)} %reshape.76.gain_ref), custom_call_target="tpu_custom_call" | custom-call | flops 2415919104 | bytes 11010048 | tf_op jit(solution)/shard_map/lift/pallas_call | solution.py:376
  250.3 6.9 %lift.3 = (bf16[512,3072]{1,0:T(8,128)(2,1)}, bf16[512,1792]{1,0:T(8,128)(2,1)}) custom-call(s32[1]{0:T(128)S(6)} %sub.8.half_ref, bf16[256,1664]{1,0:T(8,128)(2,1)} %copy-done.6, bf16[1536,3072]{1,0:T(8,128)(2,1)} %all-gather.5.cloned.1.call-done.weight_ref, ...), custom_call_target="tpu_custom_call", output_to_operand_aliasing={{0}: (5, {}), {1}: (6, {})} | custom-call | flops 2415919104 | bytes 11010048 | tf_op jit(solution)/shard_map/lift/pallas_call | solution.py:376
  (110 shorter events, 61.4 us)
Async XLA Ops:
  7.2 188.8 %all-gather.3.cloned.1.call-start = ((), (), s32[]{:S(2)}) async-start(), calls=%async_computation | async-start | bytes 5677056 | tf_op jit(solution)/shard_map/all_gather | solution.py:417
  8.9 230.4 %all-gather.5.cloned.1.call-start = ((), (), s32[]{:S(2)}) async-start(), calls=%async_computation.1 | async-start | bytes 9732096 | tf_op jit(solution)/shard_map/all_gather | solution.py:417
  9.7 5.7 %collective-permute-start = (s32[16,512]{1,0:T(8,128)S(1)}, s32[16,512]{1,0:T(8,128)S(1)}, u32[]{:S(2)}, u32[]{:S(2)}) collective-permute-start(s32[16,512]{1,0:T(8,128)S(1)} %pad_add_fusion.2), channel_id=1, source_target_pairs={{0,16},{4,20},{8,24},{12,28},{16,0},{20,4},{24,8},{28,12},{32,48},... | collective-permute-start | bytes 98312 | tf_op jit(solution)/shard_map/ppermute | solution.py:433
  21.2 9.0 %collective-permute-start.2 = (s32[64,512]{1,0:T(8,128)S(1)}, s32[64,512]{1,0:T(8,128)S(1)}, u32[]{:S(2)}, u32[]{:S(2)}) collective-permute-start(s32[64,512]{1,0:T(8,128)S(1)} %pad_add_fusion), channel_id=1, source_target_pairs={{0,4},{4,0},{8,12},{12,8},{16,20},{20,16},{24,28},{28,24},{32,36},... | collective-permute-start | bytes 393224 | tf_op jit(solution)/shard_map/ppermute | solution.py:433
  30.2 12.4 %collective-permute-start.3 = (s32[128,512]{1,0:T(8,128)S(1)}, s32[128,512]{1,0:T(8,128)S(1)}, u32[]{:S(2)}, u32[]{:S(2)}) collective-permute-start(s32[128,512]{1,0:T(8,128)S(1)} %get-tuple-element.73), channel_id=1, source_target_pairs={{0,12},{4,8},{8,4},{12,0},{16,28},{20,24},{24,20},{28,16},{32,44},... | collective-permute-start | bytes 786440 | tf_op jit(solution)/shard_map/ppermute | solution.py:433
  32.8 39.6 %collective-permute-start.5 = (bf16[4,320,896]{2,1,0:T(8,128)(2,1)}, bf16[4,320,896]{2,1,0:T(8,128)(2,1)}, u32[]{:S(2)}, u32[]{:S(2)}) collective-permute-start(bf16[4,320,896]{2,1,0:T(8,128)(2,1)} %get-tuple-element.46), channel_id=1, source_target_pairs={{0,16},{4,20},{8,24},{12,28},{16,0},{20,4},{24,8},{28,12},{32,48},... | collective-permute-start | bytes 6881288 | tf_op jit(solution)/shard_map/ppermute | solution.py:93
  42.7 39.7 %collective-permute-start.10 = (bf16[4,320,896]{2,1,0:T(8,128)(2,1)}, bf16[4,320,896]{2,1,0:T(8,128)(2,1)}, u32[]{:S(2)}, u32[]{:S(2)}) collective-permute-start(bf16[4,320,896]{2,1,0:T(8,128)(2,1)} %get-tuple-element.52), channel_id=1, source_target_pairs={{0,4},{4,0},{8,12},{12,8},{16,20},{20,16},{24,28},{28,24},{32,36},... | collective-permute-start | bytes 6881288 | tf_op jit(solution)/shard_map/ppermute | solution.py:93
  43.7 65.7 %collective-permute-start.4 = (bf16[4,320,896]{2,1,0:T(8,128)(2,1)}, bf16[4,320,896]{2,1,0:T(8,128)(2,1)S(1)}, u32[]{:S(2)}, u32[]{:S(2)}) collective-permute-start(bf16[4,320,896]{2,1,0:T(8,128)(2,1)} %get-tuple-element.45), channel_id=1, source_target_pairs={{0,16},{4,20},{8,24},{12,28},{16,0},{20,4},{24,8},{28,12},{32,48},... | collective-permute-start | bytes 6881288 | tf_op jit(solution)/shard_map/ppermute | solution.py:93
  46.3 81.6 %collective-permute-start.9 = (bf16[4,320,896]{2,1,0:T(8,128)(2,1)}, bf16[4,320,896]{2,1,0:T(8,128)(2,1)}, u32[]{:S(2)}, u32[]{:S(2)}) collective-permute-start(bf16[4,320,896]{2,1,0:T(8,128)(2,1)} %get-tuple-element.51), channel_id=1, source_target_pairs={{0,4},{4,0},{8,12},{12,8},{16,20},{20,16},{24,28},{28,24},{32,36},... | collective-permute-start | bytes 6881288 | tf_op jit(solution)/shard_map/ppermute | solution.py:93
  77.9 42.4 %collective-permute-start.7 = (bf16[2,512,896]{2,1,0:T(8,128)(2,1)}, bf16[2,512,896]{2,1,0:T(8,128)(2,1)}, u32[]{:S(2)}, u32[]{:S(2)}) collective-permute-start(bf16[2,512,896]{2,1,0:T(8,128)(2,1)} %combine.10), channel_id=1, source_target_pairs={{0,48},{4,52},{8,56},{12,60},{16,32},{20,36},{24,40},{28,44},{32,1... | collective-permute-start | bytes 5505032 | tf_op jit(solution)/shard_map/ppermute | solution.py:93
  87.8 41.5 %collective-permute-start.12 = (bf16[2,512,896]{2,1,0:T(8,128)(2,1)}, bf16[2,512,896]{2,1,0:T(8,128)(2,1)}, u32[]{:S(2)}, u32[]{:S(2)}) collective-permute-start(bf16[2,512,896]{2,1,0:T(8,128)(2,1)} %combine.14), channel_id=1, source_target_pairs={{0,12},{4,8},{8,4},{12,0},{16,28},{20,24},{24,20},{28,16},{32,44},... | collective-permute-start | bytes 5505032 | tf_op jit(solution)/shard_map/ppermute | solution.py:93
  93.3 66.4 %collective-permute-start.6 = (bf16[2,512,896]{2,1,0:T(8,128)(2,1)}, bf16[2,512,896]{2,1,0:T(8,128)(2,1)}, u32[]{:S(2)}, u32[]{:S(2)}) collective-permute-start(bf16[2,512,896]{2,1,0:T(8,128)(2,1)} %combine.8), channel_id=1, source_target_pairs={{0,48},{4,52},{8,56},{12,60},{16,32},{20,36},{24,40},{28,44},{32,1... | collective-permute-start | bytes 5505032 | tf_op jit(solution)/shard_map/ppermute | solution.py:93
  109.4 59.5 %collective-permute-start.11 = (bf16[2,512,896]{2,1,0:T(8,128)(2,1)}, bf16[2,512,896]{2,1,0:T(8,128)(2,1)}, u32[]{:S(2)}, u32[]{:S(2)}) collective-permute-start(bf16[2,512,896]{2,1,0:T(8,128)(2,1)} %combine.12), channel_id=1, source_target_pairs={{0,12},{4,8},{8,4},{12,0},{16,28},{20,24},{24,20},{28,16},{32,44},... | collective-permute-start | bytes 5505032 | tf_op jit(solution)/shard_map/ppermute | solution.py:93
  126.6 48.5 %collective-permute-start.8 = (bf16[512,896]{1,0:T(8,128)(2,1)}, bf16[512,896]{1,0:T(8,128)(2,1)S(1)}, u32[]{:S(2)}, u32[]{:S(2)}) collective-permute-start(bf16[512,896]{1,0:T(8,128)(2,1)} %get-tuple-element.48), channel_id=1, source_target_pairs={{0,4},{4,0},{8,12},{12,8},{16,20},{20,16},{24,28},{28,24},{32,36},... | collective-permute-start | bytes 2752520 | tf_op jit(solution)/shard_map/ppermute | solution.py:93
  127.9 47.2 %collective-permute-start.14 = (bf16[512,896]{1,0:T(8,128)(2,1)}, bf16[512,896]{1,0:T(8,128)(2,1)S(1)}, u32[]{:S(2)}, u32[]{:S(2)}) collective-permute-start(bf16[512,896]{1,0:T(8,128)(2,1)} %get-tuple-element.56), channel_id=1, source_target_pairs={{0,4},{4,0},{8,12},{12,8},{16,20},{20,16},{24,28},{28,24},{32,36},... | collective-permute-start | bytes 2752520 | tf_op jit(solution)/shard_map/ppermute | solution.py:93
  135.6 42.7 %collective-permute-start.13 = (bf16[512,896]{1,0:T(8,128)(2,1)}, bf16[512,896]{1,0:T(8,128)(2,1)}, u32[]{:S(2)}, u32[]{:S(2)}) collective-permute-start(bf16[512,896]{1,0:T(8,128)(2,1)} %get-tuple-element.54), channel_id=1, source_target_pairs={{0,16},{4,20},{8,24},{12,28},{16,0},{20,4},{24,8},{28,12},{32,48},... | collective-permute-start | bytes 2752520 | tf_op jit(solution)/shard_map/ppermute | solution.py:93
  159.6 18.8 %collective-permute-start.16 = (bf16[512,896]{1,0:T(8,128)(2,1)}, bf16[512,896]{1,0:T(8,128)(2,1)}, u32[]{:S(2)}, u32[]{:S(2)}) collective-permute-start(bf16[512,896]{1,0:T(8,128)(2,1)} %get-tuple-element.59), channel_id=1, source_target_pairs={{0,16},{4,20},{8,24},{12,28},{16,0},{20,4},{24,8},{28,12},{32,48},... | collective-permute-start | bytes 2752520 | tf_op jit(solution)/shard_map/ppermute | solution.py:93
  180.9 14.7 %collective-permute-start.15 = (bf16[512,896]{1,0:T(8,128)(2,1)}, bf16[512,896]{1,0:T(8,128)(2,1)}, u32[]{:S(2)}, u32[]{:S(2)}) collective-permute-start(bf16[512,896]{1,0:T(8,128)(2,1)} %add.133), channel_id=1, source_target_pairs={{0,12},{4,8},{8,4},{12,0},{16,28},{20,24},{24,20},{28,16},{32,44},... | collective-permute-start | bytes 2752520 | tf_op jit(solution)/shard_map/ppermute | solution.py:93
  181.0 15.0 %collective-permute-start.17 = (bf16[512,896]{1,0:T(8,128)(2,1)}, bf16[512,896]{1,0:T(8,128)(2,1)}, u32[]{:S(2)}, u32[]{:S(2)}) collective-permute-start(bf16[512,896]{1,0:T(8,128)(2,1)} %add.134), channel_id=1, source_target_pairs={{0,48},{4,52},{8,56},{12,60},{16,32},{20,36},{24,40},{28,44},{32,1... | collective-permute-start | bytes 2752520 | tf_op jit(solution)/shard_map/ppermute | solution.py:93
  205.6 12.2 %collective-permute-start.18 = (bf16[128,1664]{1,0:T(8,128)(2,1)}, bf16[128,1664]{1,0:T(8,128)(2,1)S(1)}, u32[]{:S(2)}, u32[]{:S(2)}) collective-permute-start(bf16[128,1664]{1,0:T(8,128)(2,1)} %get-tuple-element.63), channel_id=1, source_target_pairs={{0,3},{1,2},{2,1},{3,0},{64,65},{65,64},{66,67},{67,66},{4,7},{5,6... | collective-permute-start | bytes 1277960 | tf_op jit(solution)/shard_map/ppermute | solution.py:102
  206.9 16.7 %collective-permute-start.19 = (bf16[128,1664]{1,0:T(8,128)(2,1)}, bf16[128,1664]{1,0:T(8,128)(2,1)S(1)}, u32[]{:S(2)}, u32[]{:S(2)}) collective-permute-start(bf16[128,1664]{1,0:T(8,128)(2,1)} %get-tuple-element.64), channel_id=1, source_target_pairs={{0,1},{1,0},{2,3},{3,2},{64,67},{65,66},{66,65},{67,64},{4,5},{5,4... | collective-permute-start | bytes 1277960 | tf_op jit(solution)/shard_map/ppermute | solution.py:102
  209.1 14.6 %collective-permute-start.20 = (bf16[128,1664]{1,0:T(8,128)(2,1)}, bf16[128,1664]{1,0:T(8,128)(2,1)S(1)}, u32[]{:S(2)}, u32[]{:S(2)}) collective-permute-start(bf16[128,1664]{1,0:T(8,128)(2,1)} %get-tuple-element.65), channel_id=1, source_target_pairs={{0,2},{1,3},{2,0},{3,1},{4,6},{5,7},{6,4},{7,5},{8,10},{9,11},{10,... | collective-permute-start | bytes 1277960 | tf_op jit(solution)/shard_map/ppermute | solution.py:500
  227.2 7.2 %collective-permute-start.21 = (bf16[128,1664]{1,0:T(8,128)(2,1)}, bf16[128,1664]{1,0:T(8,128)(2,1)S(1)}, u32[]{:S(2)}, u32[]{:S(2)}) collective-permute-start(bf16[128,1664]{1,0:T(8,128)(2,1)} %compress.1), channel_id=1, source_target_pairs={{0,3},{1,2},{2,1},{3,0},{64,65},{65,64},{66,67},{67,66},{4,7},{5,6... | collective-permute-start | bytes 1277960 | tf_op jit(solution)/shard_map/ppermute | solution.py:102
  235.8 13.6 %collective-permute-start.22 = (bf16[256,1664]{1,0:T(8,128)(2,1)S(1)}, bf16[256,1664]{1,0:T(8,128)(2,1)S(1)}, u32[]{:S(2)}, u32[]{:S(2)}) collective-permute-start(bf16[256,1664]{1,0:T(8,128)(2,1)S(1)} %maximum_select_fusion.x_ref), channel_id=1, source_target_pairs={{0,1},{1,0},{2,3},{3,2},{64,67},{65,66},{66,65},{67,64},{4,5},{5,4... | collective-permute-start | bytes 2555912 | tf_op jit(solution)/shard_map/ppermute | solution.py:102
  (15 other events, 232.2 us)
Sparse Core Ops, SparseCore 0:
  10.3 55.6 all-gather.2
  181.0 52.9 all-gather.4

commit v4 on v3

--- a/solution.py
+++ b/solution.py
@@ -175,38 +175,40 @@
     )(packed, experts, later)
 
 
-def combine_kernel(spot_ref, route_ref, spread_ref, turn_ref, mine_ref, theirs_ref, *rest, outs):
-    rows = rest[-1]
+def combine_kernel(spot_ref, route_ref, spread_ref, turn_ref, mine_ref, theirs_ref, *rest, more, outs):
+    added, results, rows = rest[:more], rest[more : more + outs], rest[-1]
     rows[0:SLOTS] = mine_ref[0]
     rows[SLOTS : 2 * SLOTS] = theirs_ref[0]
     level = jnp.dot(route_ref[0], spread_ref[...], preferred_element_type=jnp.float32) - turn_ref[0:1, :]
     matrix = jnp.where(jnp.abs(level - 1.25) < 1.5, level, 0.0).astype(jnp.bfloat16)
     value = jnp.dot(matrix, rows[...], preferred_element_type=jnp.float32)
-    if len(rest) > 1 + outs:
-        value += wide(rest[0][0])
-    value = value.astype(jnp.bfloat16)
-    if outs == 1:
-        rest[-2][0] = value
-    else:
-        for i in range(outs):
-
-            @pl.when(pl.program_id(0) == i)
-            def _():
-                rest[i - 1 - outs][...] = value
-
-
-def combine(spots, routes, spread, turn, mine, theirs, first, count, tokens, more=()):
+    if not more:
+        results[0][0] = value.astype(jnp.bfloat16)
+        return
+    value += wide(added[0][0])
+    for i in range(outs):
+
+        @pl.when(pl.program_id(0) == i)
+        def _():
+            total = value
+            for one in added[1:2] if i == 0 else added[2:]:
+                total = total + wide(one[...])
+            results[i][...] = total.astype(results[i].dtype)
+
+
+def combine(spots, routes, spread, turn, mine, theirs, first, count, tokens, more=(), group=None):
     width = mine.shape[2]
     lanes = routes.shape[2]
     outs = count if more else 1
     if more:
         out_specs = [pl.BlockSpec((tokens, width), lambda i, o: (0, 0))] * count
-        out_shape = [jax.ShapeDtypeStruct((tokens, width), jnp.bfloat16)] * count
+        kinds = (jnp.bfloat16, jnp.bfloat16 if group is None else jnp.float32)
+        out_shape = [jax.ShapeDtypeStruct((tokens, width), kind) for kind in kinds]
     else:
         out_specs = pl.BlockSpec((1, tokens, width), lambda i, o: (i, 0, 0))
         out_shape = jax.ShapeDtypeStruct((count, tokens, width), jnp.bfloat16)
     return pl.pallas_call(
-        functools.partial(combine_kernel, outs=outs),
+        functools.partial(combine_kernel, more=len(more), outs=outs),
         grid_spec=pltpu.PrefetchScalarGridSpec(
             num_scalar_prefetch=1,
             grid=(count,),
@@ -217,7 +219,9 @@
                 pl.BlockSpec((1, SLOTS, width), lambda i, o: (first + i, 0, 0)),
                 pl.BlockSpec((1, SLOTS, width), lambda i, o: (first % 4 + i, 0, 0)),
             ]
-            + [pl.BlockSpec((1, tokens, width), lambda i, o: (i, 0, 0))] * len(more),
+            + [pl.BlockSpec((1, tokens, width), lambda i, o: (i, 0, 0))] * len(more[:1])
+            + [pl.BlockSpec((tokens, width), lambda i, o: (0, 0))] * len(more[1:3])
+            + [pl.BlockSpec((tokens, width), lambda i, o: (0, group))] * len(more[3:]),
             out_specs=out_specs,
             scratch_shapes=[pltpu.VMEM((2 * SLOTS, width), jnp.bfloat16)],
         ),
@@ -232,25 +236,6 @@
     )(spots, routes, spread, turn, mine, theirs, *more)
 
 
-def add_kernel(left_ref, right_ref, out_ref):
-    out_ref[...] = (wide(left_ref[...]) + wide(right_ref[...])).astype(jnp.bfloat16)
-
-
-def add(left, right):
-    rows, width = left.shape
-    block = pl.BlockSpec((rows // 2, width), lambda i: (i, 0))
-    return pl.pallas_call(
-        add_kernel,
-        grid=(2,),
-        in_specs=[block, block],
-        out_specs=block,
-        out_shape=jax.ShapeDtypeStruct(left.shape, jnp.bfloat16),
-        compiler_params=pltpu.CompilerParams(vmem_limit_bytes=VMEM),
-        cost_estimate=pl.CostEstimate(flops=rows * width, bytes_accessed=6 * rows * width, transcendentals=0),
-        name="add",
-    )(left, right)
-
-
 def wide(value):
     return value.astype(jnp.float32)
 
@@ -263,9 +248,10 @@
     return jnp.concatenate([values.astype(jnp.bfloat16), pieces.astype(jnp.bfloat16)], axis=1)
 
 
-def finish_kernel(place_ref, base_ref, left_ref, right_ref, gain_ref, down_ref, stream_ref, *rest):
+def finish_kernel(
+    place_ref, left_base_ref, right_base_ref, left_ref, right_ref, gain_ref, down_ref, stream_ref, *rest
+):
     parts, scaled, sums = rest[:4], rest[4], rest[5]
-    width = left_ref.shape[1]
     rows = parts[0].shape[0]
     step = pl.program_id(0)
     block = down_ref.shape[0]
@@ -274,8 +260,8 @@
     def _():
         for i in range(4):
             here = slice(i * rows, (i + 1) * rows)
-            left = (base_ref[here, :width] + wide(left_ref[here])).astype(jnp.bfloat16)
-            right = (base_ref[here, width:] + wide(right_ref[here])).astype(jnp.bfloat16)
+            left = (left_base_ref[here] + wide(left_ref[here])).astype(jnp.bfloat16)
+            right = (right_base_ref[here] + wide(right_ref[here])).astype(jnp.bfloat16)
             stream = jnp.concatenate([left, right], axis=1)
             stream_ref[here] = stream
             stream = wide(stream)
@@ -296,8 +282,8 @@
         parts[i][:, lanes] = value[i * rows : (i + 1) * rows]
 
 
-def finish(place, base, left, right, gain, down):
-    tokens, columns = base.shape
+def finish(place, bases, left, right, gain, down):
+    tokens, columns = left.shape[0], gain.shape[1]
     rows = tokens // 4
     block = QL // 3
     whole = lambda *shape: pl.BlockSpec(shape, lambda n, p: (0, 0))
@@ -307,7 +293,8 @@
             num_scalar_prefetch=1,
             grid=(QL // block,),
             in_specs=[
-                whole(tokens, columns),
+                whole(tokens, columns // 2),
+                whole(tokens, columns // 2),
                 whole(tokens, columns // 2),
                 whole(tokens, columns // 2),
                 whole(1, columns),
@@ -328,7 +315,7 @@
             transcendentals=0,
         ),
         name="finish",
-    )(place, base, left, right, gain, down)
+    )(place, *bases, left, right, gain, down)
 
 
 def compress_kernel(*refs):
@@ -461,9 +448,9 @@
         hit = np.concatenate([lanes == expert, lanes == expert + HOLD * (g + 1)], axis=1)
         spread.append(jnp.asarray(np.concatenate([hit, STEP * hit], axis=0).astype(np.float32)).astype(jnp.bfloat16))
 
-    def summed(g, start, more=()):
+    def summed(g, start, more=(), group=None):
         received = first[g][start // 4]
-        return combine(spots[g], routes, spread[g], turn, relayed[g][2], received, start, 2, tokens, more)
+        return combine(spots[g], routes, spread[g], turn, relayed[g][2], received, start, 2, tokens, more, group)
 
     groups = range(GROUPS)
     passed = [[summed(g, 2 * i) for g in groups] for i in range(2)]
@@ -472,23 +459,12 @@
     kept_a = [summed(g, 4, (second_a[g],)) for g in groups]
     third_a = [swap(kept_a[g][0], g, 2) for g in groups]
     third_b = [swap(kept_a[g][1], g, 2) for g in groups]
-    kept_b = [summed(g, 6, (second_b[g],)) for g in groups]
-    last = []
-    for g in groups:
-        arrived, _ = lax.optimization_barrier((third_a[g], third_b[g]))
-        last.append(add(kept_b[g][0], arrived))
+    last, base = zip(
+        *[summed(g, 6, (second_b[g], third_a[g], third_b[g], residual), g) for g in groups], strict=True
+    )
     fourth = [swap(last[g], g, 3) for g in groups]
-    up_part, *_ = lax.optimization_barrier((up_part, *last))
+    up_part, _ = lax.optimization_barrier((up_part, last[-1]))
     up = spread_out(up_part)
-    base = jnp.concatenate(
-        [
-            wide(residual[:, g * width : (g + 1) * width])
-            + wide(kept_b[g][1])
-            + wide(third_b[g])
-            for g in range(GROUPS)
-        ],
-        axis=1,
-    )
 
     here = upper.reshape(1)
     there = 1 - here

time: 265 us -> 385 us (1.45)
  the two profiles are of different devices: /device:TPU:1 before, /device:TPU:0 now
where the time goes in v4:
time: 385 us; the launch traced here: 384 us
  waiting for transfers between devices  209 us (54%)
  Pallas kernels  96 us (25%)
  starting transfers between devices  35.5 us (9%)
  local copies, waits for them, and re-layouts  18.7 us (5%)
  between operations  16.8 us (4%)
  other arithmetic  7.3 us (2%)
    ppermute x14, waiting for transfers between devices, swap(): return lax.ppermute(value, ('dp', 'expert'), pairs)  177 us
    pallas_call x8, Pallas kernels, combine(): pl.pallas_call(functools.partial(combine_kernel, more=len(more), outs=out...  49.9 us
    ppermute x4, waiting for transfers between devices, turn_to(): return lax.ppermute(value, ('dp', 'tensor'), pairs)  22.6 us
    ppermute x14, starting transfers between devices, swap(): return lax.ppermute(value, ('dp', 'expert'), pairs)  17.6 us
    pallas_call x2, Pallas kernels, relay(): pl.pallas_call(relay_kernel, grid=(SLOTS // rows,), in_specs=[pl.BlockSpe...  15.2 us
    pallas_call x2, Pallas kernels, lift(): pl.pallas_call(lift_kernel, grid_spec=pltpu.PrefetchScalarGridSpec(num_sc...  13.9 us
    unnamed x48, local copies, waits for them, and re-layouts  11.9 us
    pallas_call x1, Pallas kernels, finish(): pl.pallas_call(finish_kernel, grid_spec=pltpu.PrefetchScalarGridSpec(num_...  9.62 us
  transfers between devices with their start and end apart: 25, of which 20 were waited for; matrix products, arithmetic and copies ran while one was open for 4% of the time, Pallas kernels for 23%

profile of v4, /device:TPU:0, one launch (start us, length us, event | category | flops | bytes accessed | tf_op | source)
XLA Modules:
  0.0 383.6 jit_solution(15156216413230023365)
XLA Ops:
  23.5 7.5 %relay.2 = (bf16[4,320,896]{2,1,0:T(8,128)(2,1)}, bf16[4,320,896]{2,1,0:T(8,128)(2,1)}, bf16[8,320,896]{2,1,0:T(8,128)(2,1)}) custom-call(bf16[256,256]{1,0:T(8,128)(2,1)} %fusion.1.move_ref, bf16[320,16,1792]{2,1,0:T(8,128)(2,1)} %bitcast.26), custom_call_target="tpu_custom_call" | custom-call | flops 2348810240 | bytes 18350080 | tf_op jit(solution)/shard_map/relay/pallas_call | solution.py:120
  34.0 7.7 %relay.3 = (bf16[4,320,896]{2,1,0:T(8,128)(2,1)}, bf16[4,320,896]{2,1,0:T(8,128)(2,1)}, bf16[8,320,896]{2,1,0:T(8,128)(2,1)}) custom-call(bf16[256,256]{1,0:T(8,128)(2,1)} %fusion.2.move_ref, bf16[320,16,1792]{2,1,0:T(8,128)(2,1)} %bitcast.27), custom_call_target="tpu_custom_call" | custom-call | flops 2348810240 | bytes 18350080 | tf_op jit(solution)/shard_map/relay/pallas_call | solution.py:120
  51.6 29.0 %collective-permute-done.11.theirs_ref = bf16[4,320,896]{2,1,0:T(8,128)(2,1)S(1)} collective-permute-done((bf16[4,320,896]{2,1,0:T(8,128)(2,1)}, bf16[4,320,896]{2,1,0:T(8,128)(2,1)S(1)}, u32[]{:S(2)}, u32[]{:S(2)}) %collective-permute-start.11) | collective-permute-done | bytes 2293792 | tf_op jit(solution)/shard_map/ppermute | solution.py:93
  89.2 5.5 %combine.12 = bf16[2,512,896]{2,1,0:T(8,128)(2,1)} custom-call(s32[16]{0:T(128)} %get-tuple-element.77.spot_ref, bf16[16,512,128]{2,1,0:T(8,128)(2,1)} %route.1.route_ref, bf16[128,640]{1,0:T(8,128)(2,1)} %constant.94.spread_ref, f32[8,640]{1,0:T(8,128)} %constant.87.clone.turn_ref, bf16[8,320,896]{2,1,0:T(8,128)(2,1)} %get-tuple-element.48.mine_ref, ...), custom_call_target="tpu_custom_call" | custom-call | flops 1509949440 | bytes 4390912 | tf_op jit(solution)/shard_map/combine/pallas_call | solution.py:210
  96.2 9.1 %collective-permute-done.10.theirs_ref = bf16[4,320,896]{2,1,0:T(8,128)(2,1)} collective-permute-done((bf16[4,320,896]{2,1,0:T(8,128)(2,1)}, bf16[4,320,896]{2,1,0:T(8,128)(2,1)}, u32[]{:S(2)}, u32[]{:S(2)}) %collective-permute-start.10) | collective-permute-done | bytes 2293792 | tf_op jit(solution)/shard_map/ppermute | solution.py:93
  105.3 18.3 %collective-permute-done.13.rest_0_ = bf16[2,512,896]{2,1,0:T(8,128)(2,1)S(1)} collective-permute-done((bf16[2,512,896]{2,1,0:T(8,128)(2,1)}, bf16[2,512,896]{2,1,0:T(8,128)(2,1)S(1)}, u32[]{:S(2)}, u32[]{:S(2)}) %collective-permute-start.13) | collective-permute-done | bytes 1835040 | tf_op jit(solution)/shard_map/ppermute | solution.py:93
  124.8 6.3 %combine.14 = (bf16[512,896]{1,0:T(8,128)(2,1)}, bf16[512,896]{1,0:T(8,128)(2,1)}) custom-call(s32[16]{0:T(128)} %get-tuple-element.77.spot_ref, bf16[16,512,128]{2,1,0:T(8,128)(2,1)} %route.1.route_ref, bf16[128,640]{1,0:T(8,128)(2,1)} %constant.94.spread_ref, f32[8,640]{1,0:T(8,128)} %constant.87.clone.turn_ref, ...), custom_call_target="tpu_custom_call" | custom-call | flops 1509949440 | bytes 4390912 | tf_op jit(solution)/shard_map/combine/pallas_call | solution.py:210
  133.9 9.4 %collective-permute-done.12.rest_0_ = bf16[2,512,896]{2,1,0:T(8,128)(2,1)} collective-permute-done((bf16[2,512,896]{2,1,0:T(8,128)(2,1)}, bf16[2,512,896]{2,1,0:T(8,128)(2,1)}, u32[]{:S(2)}, u32[]{:S(2)}) %collective-permute-start.12) | collective-permute-done | bytes 1835040 | tf_op jit(solution)/shard_map/ppermute | solution.py:93
  144.8 9.8 %collective-permute-done.15.rest_2_ = bf16[512,896]{1,0:T(8,128)(2,1)S(1)} collective-permute-done((bf16[512,896]{1,0:T(8,128)(2,1)}, bf16[512,896]{1,0:T(8,128)(2,1)S(1)}, u32[]{:S(2)}, u32[]{:S(2)}) %collective-permute-start.15) | collective-permute-done | bytes 917536 | tf_op jit(solution)/shard_map/ppermute | solution.py:93
  155.5 7.6 %combine.15 = (bf16[512,896]{1,0:T(8,128)(2,1)}, f32[512,896]{1,0:T(8,128)}) custom-call(s32[16]{0:T(128)} %get-tuple-element.77.spot_ref, bf16[16,512,128]{2,1,0:T(8,128)(2,1)} %route.1.route_ref, bf16[128,640]{1,0:T(8,128)(2,1)} %constant.94.spread_ref, f32[8,640]{1,0:T(8,128)} %constant.87.clone.turn_ref, ...), custom_call_target="tpu_custom_call" | custom-call | flops 1509949440 | bytes 4390912 | tf_op jit(solution)/shard_map/combine/pallas_call | solution.py:210
  165.3 31.1 %collective-permute-done.5.theirs_ref = bf16[4,320,896]{2,1,0:T(8,128)(2,1)S(1)} collective-permute-done((bf16[4,320,896]{2,1,0:T(8,128)(2,1)}, bf16[4,320,896]{2,1,0:T(8,128)(2,1)S(1)}, u32[]{:S(2)}, u32[]{:S(2)}) %collective-permute-start.5) | collective-permute-done | bytes 2293792 | tf_op jit(solution)/shard_map/ppermute | solution.py:93
  205.7 5.5 %combine.8 = bf16[2,512,896]{2,1,0:T(8,128)(2,1)} custom-call(s32[16]{0:T(128)} %get-tuple-element.78.spot_ref, bf16[16,512,128]{2,1,0:T(8,128)(2,1)} %route.1.route_ref, bf16[128,640]{1,0:T(8,128)(2,1)} %constant.93.spread_ref, f32[8,640]{1,0:T(8,128)} %constant.87.clone.turn_ref, bf16[8,320,896]{2,1,0:T(8,128)(2,1)} %get-tuple-element.41.mine_ref, ...), custom_call_target="tpu_custom_call" | custom-call | flops 1509949440 | bytes 4390912 | tf_op jit(solution)/shard_map/combine/pallas_call | solution.py:210
  212.0 28.0 %collective-permute-done.4.theirs_ref = bf16[4,320,896]{2,1,0:T(8,128)(2,1)} collective-permute-done((bf16[4,320,896]{2,1,0:T(8,128)(2,1)}, bf16[4,320,896]{2,1,0:T(8,128)(2,1)}, u32[]{:S(2)}, u32[]{:S(2)}) %collective-permute-start.4) | collective-permute-done | bytes 2293792 | tf_op jit(solution)/shard_map/ppermute | solution.py:93
  240.0 11.7 %collective-permute-done.7.rest_0_ = bf16[2,512,896]{2,1,0:T(8,128)(2,1)S(1)} collective-permute-done((bf16[2,512,896]{2,1,0:T(8,128)(2,1)}, bf16[2,512,896]{2,1,0:T(8,128)(2,1)S(1)}, u32[]{:S(2)}, u32[]{:S(2)}) %collective-permute-start.7) | collective-permute-done | bytes 1835040 | tf_op jit(solution)/shard_map/ppermute | solution.py:93
  253.0 6.3 %combine.10 = (bf16[512,896]{1,0:T(8,128)(2,1)}, bf16[512,896]{1,0:T(8,128)(2,1)}) custom-call(s32[16]{0:T(128)} %get-tuple-element.78.spot_ref, bf16[16,512,128]{2,1,0:T(8,128)(2,1)} %route.1.route_ref, bf16[128,640]{1,0:T(8,128)(2,1)} %constant.93.spread_ref, f32[8,640]{1,0:T(8,128)} %constant.87.clone.turn_ref, ...), custom_call_target="tpu_custom_call" | custom-call | flops 1509949440 | bytes 4390912 | tf_op jit(solution)/shard_map/combine/pallas_call | solution.py:210
  261.3 10.2 %collective-permute-done.6.rest_0_ = bf16[2,512,896]{2,1,0:T(8,128)(2,1)} collective-permute-done((bf16[2,512,896]{2,1,0:T(8,128)(2,1)}, bf16[2,512,896]{2,1,0:T(8,128)(2,1)}, u32[]{:S(2)}, u32[]{:S(2)}) %collective-permute-start.6) | collective-permute-done | bytes 1835040 | tf_op jit(solution)/shard_map/ppermute | solution.py:93
  272.9 9.8 %collective-permute-done.9.rest_2_ = bf16[512,896]{1,0:T(8,128)(2,1)S(1)} collective-permute-done((bf16[512,896]{1,0:T(8,128)(2,1)}, bf16[512,896]{1,0:T(8,128)(2,1)S(1)}, u32[]{:S(2)}, u32[]{:S(2)}) %collective-permute-start.9) | collective-permute-done | bytes 917536 | tf_op jit(solution)/shard_map/ppermute | solution.py:93
  283.6 7.7 %combine.11 = (bf16[512,896]{1,0:T(8,128)(2,1)}, f32[512,896]{1,0:T(8,128)}) custom-call(s32[16]{0:T(128)} %get-tuple-element.78.spot_ref, bf16[16,512,128]{2,1,0:T(8,128)(2,1)} %route.1.route_ref, bf16[128,640]{1,0:T(8,128)(2,1)} %constant.93.spread_ref, f32[8,640]{1,0:T(8,128)} %constant.87.clone.turn_ref, ...), custom_call_target="tpu_custom_call" | custom-call | flops 1509949440 | bytes 4390912 | tf_op jit(solution)/shard_map/combine/pallas_call | solution.py:210
  298.5 7.6 %collective-permute-done.16.left_ref = bf16[512,896]{1,0:T(8,128)(2,1)S(1)} collective-permute-done((bf16[512,896]{1,0:T(8,128)(2,1)}, bf16[512,896]{1,0:T(8,128)(2,1)S(1)}, u32[]{:S(2)}, u32[]{:S(2)}) %collective-permute-start.16) | collective-permute-done | bytes 917536 | tf_op jit(solution)/shard_map/ppermute | solution.py:93
  307.5 9.6 %finish.1 = (bf16[512,1792]{1,0:T(8,128)(2,1)}, bf16[128,1664]{1,0:T(8,128)(2,1)}, bf16[128,1664]{1,0:T(8,128)(2,1)}, bf16[128,1664]{1,0:T(8,128)(2,1)}, bf16[128,1664]{1,0:T(8,128)(2,1)}) custom-call(s32[2]{0:T(128)} %pad_add_fusion.3.place_ref, f32[512,896]{1,0:T(8,128)} %get-tuple-element.47.left_base_ref, f32[512,896]{1,0:T(8,128)} %get-tuple-element.54.right_base_ref, ...), custom_call_target="tpu_custom_call" | custom-call | flops 2818572288 | bytes 14680064 | tf_op jit(solution)/shard_map/finish/pallas_call | solution.py:290
  329.2 6.7 %collective-permute-done.20.refs_3_ = bf16[128,1664]{1,0:T(8,128)(2,1)S(1)} collective-permute-done((bf16[128,1664]{1,0:T(8,128)(2,1)}, bf16[128,1664]{1,0:T(8,128)(2,1)S(1)}, u32[]{:S(2)}, u32[]{:S(2)}) %collective-permute-start.20) | collective-permute-done | bytes 426016 | tf_op jit(solution)/shard_map/ppermute | solution.py:476
  343.8 10.9 %collective-permute-done.21 = bf16[128,1664]{1,0:T(8,128)(2,1)S(1)} collective-permute-done((bf16[128,1664]{1,0:T(8,128)(2,1)}, bf16[128,1664]{1,0:T(8,128)(2,1)S(1)}, u32[]{:S(2)}, u32[]{:S(2)}) %collective-permute-start.21) | collective-permute-done | bytes 426016 | tf_op jit(solution)/shard_map/ppermute | solution.py:102
  357.0 6.9 %lift.2 = (bf16[512,3072]{1,0:T(8,128)(2,1)}, bf16[512,1792]{1,0:T(8,128)(2,1)}) custom-call(s32[1]{0:T(128)} %bitcast.1.half_ref, bf16[256,1664]{1,0:T(8,128)(2,1)} %copy-done.4, bf16[1536,3072]{1,0:T(8,128)(2,1)} %all-gather.5.cloned.1.call-done.weight_ref, bf16[512,1792]{1,0:T(8,128)(2,1)} %get-tuple-element.32.stream_ref, f32[1,1792]{1,0:T(1,128)} %reshape.76.gain_ref), custom_call_target="tpu_custom_call" | custom-call | flops 2415919104 | bytes 11010048 | tf_op jit(solution)/shard_map/lift/pallas_call | solution.py:363
  369.8 7.0 %lift.3 = (bf16[512,3072]{1,0:T(8,128)(2,1)}, bf16[512,1792]{1,0:T(8,128)(2,1)}) custom-call(s32[1]{0:T(128)S(6)} %sub.8.half_ref, bf16[256,1664]{1,0:T(8,128)(2,1)} %copy-done.13, bf16[1536,3072]{1,0:T(8,128)(2,1)} %all-gather.5.cloned.1.call-done.weight_ref, ...), custom_call_target="tpu_custom_call", output_to_operand_aliasing={{0}: (5, {}), {1}: (6, {})} | custom-call | flops 2415919104 | bytes 11010048 | tf_op jit(solution)/shard_map/lift/pallas_call | solution.py:363
  (122 shorter events, 97.4 us)
Async XLA Ops:
  7.2 299.3 %all-gather.3.cloned.1.call-start = ((), (), s32[]{:S(2)}) async-start(), calls=%async_computation | async-start | bytes 5677056 | tf_op jit(solution)/shard_map/all_gather | solution.py:404
  8.9 347.3 %all-gather.5.cloned.1.call-start = ((), (), s32[]{:S(2)}) async-start(), calls=%async_computation.1 | async-start | bytes 9732096 | tf_op jit(solution)/shard_map/all_gather | solution.py:404
  15.7 5.5 %collective-permute-start.1 = (s32[32,512]{1,0:T(8,128)S(1)}, s32[32,512]{1,0:T(8,128)S(1)}, u32[]{:S(2)}, u32[]{:S(2)}) collective-permute-start(s32[32,512]{1,0:T(8,128)S(1)} %pad_add_fusion.1), channel_id=1, source_target_pairs={{0,48},{4,52},{8,56},{12,60},{16,32},{20,36},{24,40},{28,44},{32,1... | collective-permute-start | bytes 196616 | tf_op jit(solution)/shard_map/ppermute | solution.py:420
  21.9 9.1 %collective-permute-start.2 = (s32[64,512]{1,0:T(8,128)S(1)}, s32[64,512]{1,0:T(8,128)S(1)}, u32[]{:S(2)}, u32[]{:S(2)}) collective-permute-start(s32[64,512]{1,0:T(8,128)S(1)} %pad_add_fusion), channel_id=1, source_target_pairs={{0,4},{4,0},{8,12},{12,8},{16,20},{20,16},{24,28},{28,24},{32,36},... | collective-permute-start | bytes 393224 | tf_op jit(solution)/shard_map/ppermute | solution.py:420
  31.0 10.7 %collective-permute-start.3 = (s32[128,512]{1,0:T(8,128)S(1)}, s32[128,512]{1,0:T(8,128)S(1)}, u32[]{:S(2)}, u32[]{:S(2)}) collective-permute-start(s32[128,512]{1,0:T(8,128)S(1)} %get-tuple-element.67), channel_id=1, source_target_pairs={{0,12},{4,8},{8,4},{12,0},{16,28},{20,24},{24,20},{28,16},{32,44},... | collective-permute-start | bytes 786440 | tf_op jit(solution)/shard_map/ppermute | solution.py:420
  41.7 38.9 %collective-permute-start.11 = (bf16[4,320,896]{2,1,0:T(8,128)(2,1)}, bf16[4,320,896]{2,1,0:T(8,128)(2,1)S(1)}, u32[]{:S(2)}, u32[]{:S(2)}) collective-permute-start(bf16[4,320,896]{2,1,0:T(8,128)(2,1)} %get-tuple-element.51), channel_id=1, source_target_pairs={{0,4},{4,0},{8,12},{12,8},{16,20},{20,16},{24,28},{28,24},{32,36},... | collective-permute-start | bytes 6881288 | tf_op jit(solution)/shard_map/ppermute | solution.py:93
  43.7 61.6 %collective-permute-start.10 = (bf16[4,320,896]{2,1,0:T(8,128)(2,1)}, bf16[4,320,896]{2,1,0:T(8,128)(2,1)}, u32[]{:S(2)}, u32[]{:S(2)}) collective-permute-start(bf16[4,320,896]{2,1,0:T(8,128)(2,1)} %get-tuple-element.50), channel_id=1, source_target_pairs={{0,4},{4,0},{8,12},{12,8},{16,20},{20,16},{24,28},{28,24},{32,36},... | collective-permute-start | bytes 6881288 | tf_op jit(solution)/shard_map/ppermute | solution.py:93
  87.5 36.1 %collective-permute-start.13 = (bf16[2,512,896]{2,1,0:T(8,128)(2,1)}, bf16[2,512,896]{2,1,0:T(8,128)(2,1)S(1)}, u32[]{:S(2)}, u32[]{:S(2)}) collective-permute-start(bf16[2,512,896]{2,1,0:T(8,128)(2,1)} %combine.13), channel_id=1, source_target_pairs={{0,12},{4,8},{8,4},{12,0},{16,28},{20,24},{24,20},{28,16},{32,44},... | collective-permute-start | bytes 5505032 | tf_op jit(solution)/shard_map/ppermute | solution.py:93
  94.7 48.7 %collective-permute-start.12 = (bf16[2,512,896]{2,1,0:T(8,128)(2,1)}, bf16[2,512,896]{2,1,0:T(8,128)(2,1)}, u32[]{:S(2)}, u32[]{:S(2)}) collective-permute-start(bf16[2,512,896]{2,1,0:T(8,128)(2,1)} %combine.12), channel_id=1, source_target_pairs={{0,12},{4,8},{8,4},{12,0},{16,28},{20,24},{24,20},{28,16},{32,44},... | collective-permute-start | bytes 5505032 | tf_op jit(solution)/shard_map/ppermute | solution.py:93
  131.2 13.6 %collective-permute-start.14 = (bf16[512,896]{1,0:T(8,128)(2,1)}, bf16[512,896]{1,0:T(8,128)(2,1)S(1)}, u32[]{:S(2)}, u32[]{:S(2)}) collective-permute-start(bf16[512,896]{1,0:T(8,128)(2,1)} %get-tuple-element.52), channel_id=1, source_target_pairs={{0,16},{4,20},{8,24},{12,28},{16,0},{20,4},{24,8},{28,12},{32,48},... | collective-permute-start | bytes 2752520 | tf_op jit(solution)/shard_map/ppermute | solution.py:93
  131.7 22.9 %collective-permute-start.15 = (bf16[512,896]{1,0:T(8,128)(2,1)}, bf16[512,896]{1,0:T(8,128)(2,1)S(1)}, u32[]{:S(2)}, u32[]{:S(2)}) collective-permute-start(bf16[512,896]{1,0:T(8,128)(2,1)} %get-tuple-element.53), channel_id=1, source_target_pairs={{0,16},{4,20},{8,24},{12,28},{16,0},{20,4},{24,8},{28,12},{32,48},... | collective-permute-start | bytes 2752520 | tf_op jit(solution)/shard_map/ppermute | solution.py:93
  163.2 33.2 %collective-permute-start.5 = (bf16[4,320,896]{2,1,0:T(8,128)(2,1)}, bf16[4,320,896]{2,1,0:T(8,128)(2,1)S(1)}, u32[]{:S(2)}, u32[]{:S(2)}) collective-permute-start(bf16[4,320,896]{2,1,0:T(8,128)(2,1)} %get-tuple-element.44), channel_id=1, source_target_pairs={{0,16},{4,20},{8,24},{12,28},{16,0},{20,4},{24,8},{28,12},{32,48},... | collective-permute-start | bytes 6881288 | tf_op jit(solution)/shard_map/ppermute | solution.py:93
  163.8 76.2 %collective-permute-start.4 = (bf16[4,320,896]{2,1,0:T(8,128)(2,1)}, bf16[4,320,896]{2,1,0:T(8,128)(2,1)}, u32[]{:S(2)}, u32[]{:S(2)}) collective-permute-start(bf16[4,320,896]{2,1,0:T(8,128)(2,1)} %get-tuple-element.43), channel_id=1, source_target_pairs={{0,16},{4,20},{8,24},{12,28},{16,0},{20,4},{24,8},{28,12},{32,48},... | collective-permute-start | bytes 6881288 | tf_op jit(solution)/shard_map/ppermute | solution.py:93
  203.2 48.5 %collective-permute-start.7 = (bf16[2,512,896]{2,1,0:T(8,128)(2,1)}, bf16[2,512,896]{2,1,0:T(8,128)(2,1)S(1)}, u32[]{:S(2)}, u32[]{:S(2)}) collective-permute-start(bf16[2,512,896]{2,1,0:T(8,128)(2,1)} %combine.9), channel_id=1, source_target_pairs={{0,48},{4,52},{8,56},{12,60},{16,32},{20,36},{24,40},{28,44},{32,1... | collective-permute-start | bytes 5505032 | tf_op jit(solution)/shard_map/ppermute | solution.py:93
  211.2 60.3 %collective-permute-start.6 = (bf16[2,512,896]{2,1,0:T(8,128)(2,1)}, bf16[2,512,896]{2,1,0:T(8,128)(2,1)}, u32[]{:S(2)}, u32[]{:S(2)}) collective-permute-start(bf16[2,512,896]{2,1,0:T(8,128)(2,1)} %combine.8), channel_id=1, source_target_pairs={{0,48},{4,52},{8,56},{12,60},{16,32},{20,36},{24,40},{28,44},{32,1... | collective-permute-start | bytes 5505032 | tf_op jit(solution)/shard_map/ppermute | solution.py:93
  259.2 13.6 %collective-permute-start.8 = (bf16[512,896]{1,0:T(8,128)(2,1)}, bf16[512,896]{1,0:T(8,128)(2,1)S(1)}, u32[]{:S(2)}, u32[]{:S(2)}) collective-permute-start(bf16[512,896]{1,0:T(8,128)(2,1)} %get-tuple-element.45), channel_id=1, source_target_pairs={{0,4},{4,0},{8,12},{12,8},{16,20},{20,16},{24,28},{28,24},{32,36},... | collective-permute-start | bytes 2752520 | tf_op jit(solution)/shard_map/ppermute | solution.py:93
  259.3 23.4 %collective-permute-start.9 = (bf16[512,896]{1,0:T(8,128)(2,1)}, bf16[512,896]{1,0:T(8,128)(2,1)S(1)}, u32[]{:S(2)}, u32[]{:S(2)}) collective-permute-start(bf16[512,896]{1,0:T(8,128)(2,1)} %get-tuple-element.46), channel_id=1, source_target_pairs={{0,4},{4,0},{8,12},{12,8},{16,20},{20,16},{24,28},{28,24},{32,36},... | collective-permute-start | bytes 2752520 | tf_op jit(solution)/shard_map/ppermute | solution.py:93
  291.3 14.8 %collective-permute-start.16 = (bf16[512,896]{1,0:T(8,128)(2,1)}, bf16[512,896]{1,0:T(8,128)(2,1)S(1)}, u32[]{:S(2)}, u32[]{:S(2)}) collective-permute-start(bf16[512,896]{1,0:T(8,128)(2,1)} %get-tuple-element.55), channel_id=1, source_target_pairs={{0,12},{4,8},{8,4},{12,0},{16,28},{20,24},{24,20},{28,16},{32,44},... | collective-permute-start | bytes 2752520 | tf_op jit(solution)/shard_map/ppermute | solution.py:93
  291.9 14.6 %collective-permute-start.17 = (bf16[512,896]{1,0:T(8,128)(2,1)S(1)}, bf16[512,896]{1,0:T(8,128)(2,1)S(1)}, u32[]{:S(2)}, u32[]{:S(2)}) collective-permute-start(bf16[512,896]{1,0:T(8,128)(2,1)S(1)} %copy-done.21), channel_id=1, source_target_pairs={{0,48},{4,52},{8,56},{12,60},{16,32},{20,36},{24,40},{28,44},{32,1... | collective-permute-start | bytes 2752520 | tf_op jit(solution)/shard_map/ppermute | solution.py:93
  317.1 9.5 %collective-permute-start.18 = (bf16[128,1664]{1,0:T(8,128)(2,1)}, bf16[128,1664]{1,0:T(8,128)(2,1)S(1)}, u32[]{:S(2)}, u32[]{:S(2)}) collective-permute-start(bf16[128,1664]{1,0:T(8,128)(2,1)} %get-tuple-element.59), channel_id=1, source_target_pairs={{0,3},{1,2},{2,1},{3,0},{64,65},{65,64},{66,67},{67,66},{4,7},{5,6... | collective-permute-start | bytes 1277960 | tf_op jit(solution)/shard_map/ppermute | solution.py:102
  320.3 8.9 %collective-permute-start.19 = (bf16[128,1664]{1,0:T(8,128)(2,1)}, bf16[128,1664]{1,0:T(8,128)(2,1)S(1)}, u32[]{:S(2)}, u32[]{:S(2)}) collective-permute-start(bf16[128,1664]{1,0:T(8,128)(2,1)} %get-tuple-element.60), channel_id=1, source_target_pairs={{0,1},{1,0},{2,3},{3,2},{64,67},{65,66},{66,65},{67,64},{4,5},{5,4... | collective-permute-start | bytes 1277960 | tf_op jit(solution)/shard_map/ppermute | solution.py:102
  320.3 15.6 %collective-permute-start.20 = (bf16[128,1664]{1,0:T(8,128)(2,1)}, bf16[128,1664]{1,0:T(8,128)(2,1)S(1)}, u32[]{:S(2)}, u32[]{:S(2)}) collective-permute-start(bf16[128,1664]{1,0:T(8,128)(2,1)} %get-tuple-element.61), channel_id=1, source_target_pairs={{0,2},{1,3},{2,0},{3,1},{4,6},{5,7},{6,4},{7,5},{8,10},{9,11},{10,... | collective-permute-start | bytes 1277960 | tf_op jit(solution)/shard_map/ppermute | solution.py:476
  339.3 15.4 %collective-permute-start.21 = (bf16[128,1664]{1,0:T(8,128)(2,1)}, bf16[128,1664]{1,0:T(8,128)(2,1)S(1)}, u32[]{:S(2)}, u32[]{:S(2)}) collective-permute-start(bf16[128,1664]{1,0:T(8,128)(2,1)} %compress.1), channel_id=1, source_target_pairs={{0,3},{1,2},{2,1},{3,0},{64,65},{65,64},{66,67},{67,66},{4,7},{5,6... | collective-permute-start | bytes 1277960 | tf_op jit(solution)/shard_map/ppermute | solution.py:102
  356.1 12.8 %collective-permute-start.22 = (bf16[256,1664]{1,0:T(8,128)(2,1)S(1)}, bf16[256,1664]{1,0:T(8,128)(2,1)S(1)}, u32[]{:S(2)}, u32[]{:S(2)}) collective-permute-start(bf16[256,1664]{1,0:T(8,128)(2,1)S(1)} %maximum_select_fusion.x_ref), channel_id=1, source_target_pairs={{0,1},{1,0},{2,3},{3,2},{64,67},{65,66},{66,65},{67,64},{4,5},{5,4... | collective-permute-start | bytes 2555912 | tf_op jit(solution)/shard_map/ppermute | solution.py:102
  (23 other events, 310.5 us)
Sparse Core Ops, SparseCore 0:
  10.3 54.3 all-gather.2
  163.3 71.8 all-gather.4
